TPU v7x, 32 devices: a whole 2x2x4 slice. The times are simulated.
32 devices in a mesh: chan: 8 (over z, y), rep: 4 (over x, core).
Axes of the slice: x: 2, y: 2, z: 4, core: 2. Of those that a mesh axis runs over, the one named last changes fastest.
Arguments:
- records: bfloat16 [2, 8, 256, 2048], P(None, None, 'rep', 'chan'), may hold values from -6 to 6
- sources: int32 [128], replicated, may hold values from 0 to 2047
- dead_list: int32 [2, 128], replicated, may hold values from 0 to 2047
Outputs:
- correlations: float32 [128, 64, 2048], P('rep', None, 'chan')
All inputs are finite; a program needn't handle non-finite values.
Results may differ from a plain program's by a relative error of at most 0.0072.
Values may be sent and summed in bfloat16 or wider, within the bound.
No kernel may reach another device: no remote copies, remote signals or barrier semaphores. Data moves between devices by JAX's collectives and lax.ppermute only.
A program may use at most 64 MiB of HBM per device.

v0:
```python
import math

import jax
import jax.numpy as jnp
from jax import lax
from jax.sharding import PartitionSpec as P

WINDOW_SAMPLES = 2048
K = 256
K0 = 16
HALF = 32
WH = 32
LAGS = 64


tile_span = 128
tiny_eps = 1e-06


def live_table(dead_list, total):
    window_count, listed = dead_list.shape
    window_rows = jnp.broadcast_to(
        jnp.arange(window_count, dtype=jnp.int32)[:, None], (window_count, listed)
    )
    return jnp.ones((window_count, total), jnp.float32).at[window_rows, dead_list].set(0.0)


def running_mean(records):
    length = records.shape[-1]
    blocks = length // tile_span
    leading = records.shape[:-1]
    magnitude = jnp.abs(records)
    padded = jnp.pad(magnitude, [(0, 0)] * (records.ndim - 1) + [(tile_span, tile_span)])
    before = padded[..., :length].reshape(leading + (blocks, tile_span))
    middle = magnitude.reshape(leading + (blocks, tile_span))
    after = padded[..., 2 * tile_span :].reshape(leading + (blocks, tile_span))
    views = jnp.concatenate([before, middle, after], axis=-1).reshape(-1, 3 * tile_span)
    offsets = jnp.arange(3 * tile_span, dtype=jnp.int32)[:, None] - tile_span
    targets = jnp.arange(tile_span, dtype=jnp.int32)[None, :]
    band_unit_mask = (jnp.abs(offsets - targets) <= HALF).astype(jnp.bfloat16)
    totals = jnp.dot(views, band_unit_mask, preferred_element_type=jnp.float32).reshape(
        leading + (length,)
    )
    sample = jnp.arange(length, dtype=jnp.int32)
    counts = (jnp.minimum(sample, HALF) + jnp.minimum(length - 1 - sample, HALF) + 1).astype(
        jnp.float32
    )
    return totals / counts


def dft_table(length):
    sample = jnp.arange(length, dtype=jnp.int32)[:, None]
    bin_index = K0 + jnp.arange(K, dtype=jnp.int32)[None, :]
    phase = sample * bin_index % length
    angle = phase.astype(jnp.float32) * (2.0 * math.pi / length)
    return jnp.concatenate([jnp.cos(angle), -jnp.sin(angle)], axis=1).astype(jnp.bfloat16)


def whiten(spectrum):
    real_part = spectrum[:, :K]
    imag_part = spectrum[:, K:]
    amplitude = jnp.sqrt(real_part * real_part + imag_part * imag_part)
    index_row = jnp.arange(K, dtype=jnp.int32)[:, None]
    index_col = jnp.arange(K, dtype=jnp.int32)[None, :]
    band = (jnp.abs(index_row - index_col) <= WH).astype(jnp.float32)
    smoothed_amplitude = jnp.dot(amplitude, band, precision=lax.Precision.HIGHEST) / jnp.sum(
        band, axis=0
    )
    return (
        spectrum / (jnp.concatenate([smoothed_amplitude, smoothed_amplitude], axis=1) + tiny_eps)
    ).astype(jnp.bfloat16)


def preprocess(records):
    mean_abs = running_mean(records)
    normed = (records.astype(jnp.float32) / (mean_abs + tiny_eps)).astype(jnp.bfloat16)
    spectrum = jnp.dot(normed, dft_table(records.shape[-1]), preferred_element_type=jnp.float32)
    return whiten(spectrum)


def lag_kernel(source_spectrum):
    bin_index = K0 + jnp.arange(K, dtype=jnp.int32)[None, :]
    lag_index = jnp.arange(LAGS, dtype=jnp.int32)[:, None] - LAGS // 2
    phase = jnp.mod(lag_index * bin_index, WINDOW_SAMPLES)
    angle = phase.astype(jnp.float32) * (2.0 * math.pi / WINDOW_SAMPLES)
    cosine_lookup = jnp.cos(angle)[None, :, None, :]
    sin_table = jnp.sin(angle)[None, :, None, :]
    real_part = source_spectrum[:, None, :, :K].astype(jnp.float32)
    imag_part = source_spectrum[:, None, :, K:].astype(jnp.float32)
    with_real = real_part * cosine_lookup + imag_part * sin_table
    with_imag = imag_part * cosine_lookup - real_part * sin_table
    return jnp.concatenate([with_real, with_imag], axis=3).astype(jnp.bfloat16)


def correlate(kernel, spectra, source_live, chan_live):
    summed = lax.dot_general(
        kernel, spectra, (((2, 3), (0, 2)), ((), ())), preferred_element_type=jnp.float32
    )
    pairs = jnp.dot(source_live.T, chan_live, precision=lax.Precision.HIGHEST)
    return summed / (math.sqrt(K) * jnp.maximum(pairs, 1.0))[:, None, :]


def shards(records, sources, dead_list):
    window_count, groups, ch_width, span_len = records.shape
    reps = lax.axis_size("rep")
    chan_place = lax.axis_index("chan")
    rep_place = lax.axis_index("rep")
    group_share = ch_width * reps
    total = groups * group_share
    live = live_table(dead_list, total)
    group_ids = (
        jnp.arange(groups, dtype=jnp.int32)[:, None] * group_share
        + rep_place * ch_width
        + jnp.arange(ch_width, dtype=jnp.int32)[None, :]
    )
    live_here = live[:, group_ids]
    masked = jnp.where(live_here[..., None] > 0.5, records, jnp.zeros_like(records))
    arrived = lax.all_to_all(masked, "chan", split_axis=1, concat_axis=3, tiled=True)
    flat_rows = arrived.reshape(-1, arrived.shape[-1])
    spectra = preprocess(flat_rows).reshape(arrived.shape[0], ch_width, 2 * K)
    own_ids = (
        chan_place * group_share + rep_place * ch_width + jnp.arange(ch_width, dtype=jnp.int32)
    )
    onehot = (sources[:, None] == own_ids[None, :]).astype(jnp.bfloat16)
    picked = jnp.einsum("sc,wcf->swf", onehot, spectra, preferred_element_type=jnp.float32)
    quarter = sources.shape[0] // reps
    summed = lax.psum(picked, ("chan", "rep"))
    mine = lax.dynamic_slice_in_dim(summed, rep_place * quarter, quarter, 0)
    source_spectrum = mine.astype(jnp.bfloat16)
    source_live = live[:, sources]
    kernel = lag_kernel(source_spectrum)
    quarter_live = lax.dynamic_slice_in_dim(source_live, rep_place * quarter, quarter, 1)
    piece = lax.all_gather(spectra, "rep", axis=1, tiled=True)
    piece_ids = chan_place * group_share + jnp.arange(piece.shape[1], dtype=jnp.int32)
    return correlate(kernel, piece, quarter_live, live[:, piece_ids])


def solution(mesh):
    placed = (P(None, None, "rep", "chan"), P(), P())
    return jax.shard_map(
        shards, mesh=mesh, in_specs=placed, out_specs=P("rep", None, "chan"), check_vma=False
    )
```

profile of v0, /device:TPU:0, one launch (start us, length us, event | category | flops | bytes accessed | tf_op | source)
XLA Modules:
  0.0 100.0 jit_solution(6747961052449455351)
XLA Ops:
  0.0 0.0 copy-start.2
  0.0 0.7 fusion.51
  0.8 0.1 compare_select_fusion
  0.8 0.1 reshape.213
  0.9 12.1 %scatter_fusion = f32[2,2048]{1,0:T(2,128)S(1)} fusion(f32[2,2048]{1,0:T(2,128)S(1)} %broadcast_in_dim.20, s32[256]{0:T(256)S(1)} %fusion.51, f32[256]{0:T(256)S(1)} %broadcast.268), kind=kCustom, calls=%fused_computation.3 | custom fusion | bytes 5120 | tf_op jit(solution)/shard_map/scatter | solution.py:25
  13.1 0.0 copy-start.3
  13.1 0.4 copy.29
  13.5 1.0 %gather_fusion = f32[512,2]{1,0:T(8,128)S(1)} fusion(f32[2,2048]{0,1:T(8,128)S(1)} %copy.29, s32[1024]{0:T(1024)S(1)} %pad_clamp_fusion.2), kind=kCustom, calls=%fused_computation | custom fusion | bytes 10240 | tf_op jit(solution)/shard_map/gather | solution.py:116
  14.5 0.2 copy.30
  14.7 0.0 copy-done.2
  14.7 1.0 %copy_select_fusion = bf16[2,8,64,256]{3,2,0,1:T(8,128)(2,1)} fusion(bf16[2,8,64,256]{3,2,1,0:T(8,128)(2,1)S(1)} %copy-done.2, pred[2,8,64]{2,0,1:T(4,128)(4,1)S(1)} %copy.30), kind=kLoop, calls=%fused_computation.40 | loop fusion | flops 262144 | bytes 1049600 | tf_op jit(solution)/shard_map/jit(_where)/select_n | solution.py:117
  15.7 7.3 %all-to-all-start = ((bf16[2,8,64,256]{3,2,0,1:T(8,128)(2,1)}), bf16[2,8,64,256]{3,2,0,1:T(8,128)(2,1)S(1)}, u32[]{:S(2)}, u32[]{:S(2)}) async-start(bf16[2,8,64,256]{3,2,0,1:T(8,128)(2,1)} %copy_select_fusion), calls=%async_computation | async-start | bytes 1048576 | tf_op jit(solution)/shard_map/all_to_all | solution.py:118
  23.0 0.1 convert_reduce_fusion
  23.1 0.0 copy-done.3
  23.2 0.6 gather_fusion.1
  23.8 0.7 gather_fusion.2
  24.6 0.3 fusion.38
  24.9 0.2 fusion.22
  25.2 9.4 %cosine_convert_fusion = (bf16[2048,256]{1,0:T(8,128)(2,1)}, bf16[2048,256]{1,0:T(8,128)(2,1)}) fusion(s32[256]{0:T(256)S(1)} %iota_add_fusion.1), kind=kLoop, calls=%fused_computation.22 | loop fusion | flops 8912896 | bytes 2098176 | tf_op jit(solution)/shard_map/convert.5
  34.5 3.0 %all-to-all-done = bf16[2,8,64,256]{3,2,0,1:T(8,128)(2,1)S(1)} async-done(((bf16[2,8,64,256]{3,2,0,1:T(8,128)(2,1)}), bf16[2,8,64,256]{3,2,0,1:T(8,128)(2,1)S(1)}, u32[]{:S(2)}, u32[]{:S(2)}) %all-to-all-start) | async-done | bytes 524320 | tf_op jit(solution)/shard_map/all_to_all | solution.py:118
  37.5 0.1 abs_bitcast_fusion
  37.6 0.3 copy.33
  37.9 1.0 abs.31
  38.9 0.1 copy.41
  39.0 0.1 pad_slice_fusion.1
  39.1 1.0 %concatenate.23 = bf16[2048,128]{1,0:T(8,128)(2,1)} reshape(bf16[128,2048]{1,0:T(8,128)(2,1)S(1)} %get-tuple-element.5) | data formatting | bytes 1048576 | tf_op jit(solution)/shard_map/concatenate | solution.py:37
  40.1 0.2 concatenate.24
  40.4 1.8 %fusion.16 = f32[2048,128]{1,0:T(8,128)S(1)} fusion(bf16[2048,128]{1,0:T(8,128)(2,1)S(1)} %concatenate.24, bf16[2048,128]{1,0:T(8,128)(2,1)} %abs.31, bf16[2048,128]{1,0:T(8,128)(2,1)} %concatenate.23, s32[384]{0:T(512)S(1)} %iota_add_fusion), kind=kOutput, calls=%fused_computation.26 | convolution fusion | flops 206192640 | bytes 2622976 | tf_op jit(solution)/shard_map/dot_general | solution.py:41
  42.2 0.2 reshape.207
  42.4 0.0 copy-start
  42.4 0.0 copy-start.1
  42.4 0.6 copy.32
  43.0 0.3 copy.40
  43.4 0.2 copy-done
  43.6 0.3 copy-done.1
  43.9 0.6 fusion.7
  44.5 0.3 convolution_divide_fusion
  44.9 7.2 %all_gather.3 = bf16[2,256,512]{2,1,0:T(8,128)(2,1)S(1)} all-gather(bf16[2,64,512]{2,1,0:T(8,128)(2,1)S(1)} %bitcast.49), channel_id=1, replica_groups=mesh['chan'=8,'rep'=4] {'rep'}, dimensions={1}, use_global_device_ids=true | all-gather | bytes 655360 | tf_op jit(solution)/shard_map/all_gather | solution.py:133
  52.0 0.3 fusion.39
  52.4 43.3 %all-reduce.2 = bf16[128,2,512]{2,0,1:T(8,128)(2,1)S(1)} all-reduce(f32[128,2,512]{2,0,1:T(8,128)S(1)} %fusion.39), channel_id=1, replica_groups=mesh['chan'=8,'rep'=4] {'chan','rep'}, use_global_device_ids=true, to_apply=%region_2.3 | all-reduce | flops 131072 | bytes 786432 | tf_op jit(solution)/shard_map/psum | solution.py:127
  95.7 0.1 copy.35
  95.8 0.1 copy.36
  95.8 1.5 %add_convert_fusion = (bf16[32,64,2,256]{3,1,2,0:T(8,128)(2,1)S(1)}, bf16[32,64,2,256]{3,1,2,0:T(8,128)(2,1)S(1)}) fusion(f32[64,256]{1,0:T(8,128)S(1)} %get-tuple-element.14, f32[32,2,256]{2,1,0:T(2,128)S(1)} %copy.36, f32[64,256]{1,0:T(8,128)S(1)} %get-tuple-element.13, f32[32,2,256]{2,1,0:T(2,128)S(1)} %copy.35), kind=kLoop, calls=%fused_computation.9 | loop fusion | flops 8388608 | bytes 4456448 | tf_op jit(solution)/shard_map/convert.3
  97.3 2.7 %bitcast_divide_fusion = f32[32,64,256]{2,1,0:T(8,128)} fusion(bf16[32,64,2,256]{3,1,2,0:T(8,128)(2,1)S(1)} %get-tuple-element.10, bf16[32,64,2,256]{3,1,2,0:T(8,128)(2,1)S(1)} %get-tuple-element.9, f32[32,256]{1,0:T(8,128)S(1)} %fusion.22, bf16[2,256,512]{2,1,0:T(8,128)(2,1)S(1)} %all_gather.3), kind=kOutput, calls=%fused_computation.20 | convolution fusion | flops 1082654720 | bytes 6848512 | tf_op jit(solution)/shard_map/dot_general | solution.py:96
  (17 shorter events, 0.2 us)
Async XLA Ops:
  0.0 14.7 %copy-start.2 = (bf16[2,8,64,256]{3,2,1,0:T(8,128)(2,1)S(1)}, bf16[2,8,64,256]{3,2,1,0:T(8,128)(2,1)}, u32[]{:S(2)}) copy-start(bf16[2,8,64,256]{3,2,1,0:T(8,128)(2,1)} %param.3) | copy-start | bytes 1572868
  13.1 10.1 %copy-start.3 = (s32[128]{0:T(128)S(1)}, s32[128]{0:T(128)}, u32[]{:S(2)}) copy-start(s32[128]{0:T(128)} %param.4) | copy-start | bytes 1540
  15.7 21.8 %all-to-all-start = ((bf16[2,8,64,256]{3,2,0,1:T(8,128)(2,1)}), bf16[2,8,64,256]{3,2,0,1:T(8,128)(2,1)S(1)}, u32[]{:S(2)}, u32[]{:S(2)}) async-start(bf16[2,8,64,256]{3,2,0,1:T(8,128)(2,1)} %copy_select_fusion), calls=%async_computation | async-start | bytes 1048576 | tf_op jit(solution)/shard_map/all_to_all | solution.py:118
  42.4 1.2 %copy-start = (bf16[2048,256]{1,0:T(8,128)(2,1)S(1)}, bf16[2048,256]{1,0:T(8,128)(2,1)}, u32[]{:S(2)}) copy-start(bf16[2048,256]{1,0:T(8,128)(2,1)} %get-tuple-element.15) | copy-start | bytes 3145732
  42.4 1.5 %copy-start.1 = (bf16[2048,256]{1,0:T(8,128)(2,1)S(1)}, bf16[2048,256]{1,0:T(8,128)(2,1)}, u32[]{:S(2)}) copy-start(bf16[2048,256]{1,0:T(8,128)(2,1)} %get-tuple-element.16) | copy-start | bytes 3145732
where the time goes:
time: 100 us
  blocking collectives  50.5 us (50%)
  local copies, waits for them, and re-layouts  19.7 us (20%)
  other arithmetic  13.4 us (13%)
  starting transfers between devices  7.28 us (7%)
  matrix products  5.95 us (6%)
  waiting for transfers between devices  2.98 us (3%)
    psum x1, blocking collectives, shards(): summed = lax.psum(picked, ('chan', 'rep'))  43.3 us
    scatter x2, local copies, waits for them, and re-layouts, live_table(): jnp.ones((window_count, total), jnp.float32).at[window_rows, dead_list]  12.5 us
    another operation x2, other arithmetic  10.9 us
    all_to_all x1, starting transfers between devices, shards(): lax.all_to_all(masked, 'chan', split_axis=1, concat_axis=3, tiled=True)  7.28 us
    all_gather x1, blocking collectives, shards(): piece = lax.all_gather(spectra, 'rep', axis=1, tiled=True)  7.17 us
    all_to_all x1, waiting for transfers between devices, shards(): lax.all_to_all(masked, 'chan', split_axis=1, concat_axis=3, tiled=True)  2.98 us
    dot_general x1, matrix products, correlate(): lax.dot_general(kernel, spectra, (((2, 3), (0, 2)), ((), ())), preferred_...  2.66 us
  transfers between devices with their start and end apart: 1, of which 1 were waited for; matrix products, arithmetic and copies ran while one was open for 11% of the time, Pallas kernels for 0%

commit v1 on v0

v1 whole, which is shorter than its diff:
```python
import functools
import math

import jax
import jax.numpy as jnp
import numpy as np
from jax import lax
from jax.experimental import pallas as pl
from jax.experimental.pallas import tpu as pltpu
from jax.sharding import PartitionSpec as P

WINDOW_SAMPLES = 2048
K = 256
K0 = 16
HALF = 32
WH = 32
LAGS = 64
EPS = 1e-06

CHUNK = 256
EDGE = 128
VMEM = pl.BlockSpec(memory_space=pltpu.VMEM)
LIMIT = 40 * 1024 * 1024


def dft_table(length):
    sample = np.arange(length, dtype=np.int64)[:, None]
    bin_index = K0 + np.arange(K, dtype=np.int64)[None, :]
    angle = (sample * bin_index % length) * (2.0 * math.pi / length)
    table = np.concatenate([np.cos(angle), -np.sin(angle)], axis=1)
    return table.astype(np.float32).astype(jnp.bfloat16)


def lag_tables():
    bin_index = K0 + np.arange(K, dtype=np.int64)[None, :]
    lag = np.arange(LAGS, dtype=np.int64)[:, None] - LAGS // 2
    angle = np.mod(lag * bin_index, WINDOW_SAMPLES) * (2.0 * math.pi / WINDOW_SAMPLES)
    return np.cos(angle).astype(np.float32), np.sin(angle).astype(np.float32)


def sample_band():
    source = np.arange(CHUNK + 2 * EDGE)[:, None] - EDGE
    target = np.arange(CHUNK)[None, :]
    return (np.abs(source - target) <= HALF).astype(np.float32).astype(jnp.bfloat16)


def bin_band():
    row = np.arange(K)[:, None]
    column = np.arange(K)[None, :]
    band = np.abs(row - column) <= WH
    inverse = 1.0 / band.sum(axis=0, keepdims=True)
    return band.astype(np.float32).astype(jnp.bfloat16), inverse.astype(np.float32)


def iota(shape, dim):
    return lax.broadcasted_iota(jnp.int32, shape, dim)


def pack_kernel(cw, rec_ref, src_ref, out_ref, keep_ref, give_ref, pick_ref):
    windows, groups, width, span = rec_ref.shape
    reps = cw // width
    rep = lax.axis_index("rep")
    per = groups // out_ref.shape[0]
    for w in range(windows):
        for g in range(groups):
            out_ref[g // per, w, g % per] = rec_ref[w, g]
    count = src_ref.shape[1]
    column = jnp.broadcast_to(src_ref[...], (count, count)).T
    local = groups * width
    place = iota((count, local), 1)
    ids = (place // width) * cw + rep * width + place % width
    wide = jnp.concatenate([column] * (local // count), axis=1)
    onehot = jnp.where(wide == ids, 1.0, 0.0).astype(jnp.bfloat16)
    quarter = count // reps
    for w in range(windows):
        rows = rec_ref[w].reshape(local, span)
        picked = jnp.dot(onehot, rows, preferred_element_type=jnp.float32)
        pick_ref[...] = picked
        for half in range(reps // 2):
            for ref, bit in ((keep_ref, rep % 2), (give_ref, 1 - rep % 2)):
                first = pl.multiple_of((2 * half + bit) * quarter, quarter)
                ref[half, w] = pick_ref[pl.ds(first, quarter), :].astype(jnp.bfloat16)


def pack(records, sources, chans, reps):
    windows, groups, width, span = records.shape
    count = sources.shape[0]
    part = (reps // 2, windows, count // reps, span)
    return pl.pallas_call(
        functools.partial(pack_kernel, width * reps),
        out_shape=(
            jax.ShapeDtypeStruct((chans, windows, groups // chans, width, span), jnp.bfloat16),
            jax.ShapeDtypeStruct(part, jnp.bfloat16),
            jax.ShapeDtypeStruct(part, jnp.bfloat16),
        ),
        in_specs=[VMEM, VMEM],
        out_specs=(VMEM, VMEM, VMEM),
        scratch_shapes=[pltpu.VMEM((count, span), jnp.float32)],
        compiler_params=pltpu.CompilerParams(vmem_limit_bytes=LIMIT),
        name="pack",
    )(records, sources.reshape(1, count))


def listed(ids, dead_row):
    hit = jnp.where(ids == dead_row, 1.0, 0.0)
    return jnp.max(hit, axis=1, keepdims=True)


def whiten_rows(x_ref, ext_ref, table_ref, band_ref, bins_ref, inverse_ref):
    pieces, rows, _ = x_ref.shape
    length = pieces * CHUNK
    for i in range(pieces):
        here = pl.ds(i * rows, rows)
        ext_ref[here, EDGE : EDGE + CHUNK] = jnp.abs(x_ref[i])
        blank = jnp.zeros((rows, EDGE), jnp.bfloat16)
        ext_ref[here, :EDGE] = jnp.abs(x_ref[i - 1, :, CHUNK - EDGE :]) if i else blank
        ext_ref[here, EDGE + CHUNK :] = (
            jnp.abs(x_ref[i + 1, :, :EDGE]) if i < pieces - 1 else blank
        )
    totals = jnp.dot(ext_ref[...], band_ref[...], preferred_element_type=jnp.float32)
    spectrum = jnp.zeros((rows, 2 * K), jnp.float32)
    for i in range(pieces):
        sample = iota((1, CHUNK), 1) + i * CHUNK
        counts = jnp.minimum(sample, HALF) + jnp.minimum(length - 1 - sample, HALF) + 1
        mean = totals[i * rows : (i + 1) * rows] * (1.0 / counts.astype(jnp.float32))
        normed = (x_ref[i].astype(jnp.float32) / (mean + EPS)).astype(jnp.bfloat16)
        spectrum += jnp.dot(
            normed, table_ref[i * CHUNK : (i + 1) * CHUNK, :], preferred_element_type=jnp.float32
        )
    real_part, imag_part = spectrum[:, :K], spectrum[:, K:]
    amplitude = jnp.sqrt(real_part * real_part + imag_part * imag_part)
    high = amplitude.astype(jnp.bfloat16)
    rest = amplitude - high.astype(jnp.float32)
    middle = rest.astype(jnp.bfloat16)
    low = (rest - middle.astype(jnp.float32)).astype(jnp.bfloat16)
    stacked = jnp.concatenate([high, middle, low], axis=0)
    sums = jnp.dot(stacked, bins_ref[...], preferred_element_type=jnp.float32)
    smooth = (sums[:rows] + sums[rows : 2 * rows] + sums[2 * rows :]) * inverse_ref[...]
    scale = 1.0 / (smooth + EPS)
    return real_part * scale, imag_part * scale


def channel_kernel(cw, width, x_ref, dead_ref, table_ref, band_ref, bins_ref, inverse_ref, out_ref, ext_ref):
    windows, per = out_ref.shape[0], out_ref.shape[1] // width
    real_part, imag_part = whiten_rows(x_ref, ext_ref, table_ref, band_ref, bins_ref, inverse_ref)
    block = lax.axis_index("chan") * per
    rep = lax.axis_index("rep")
    count = per * width
    row = iota((count, 1), 0)
    ids = (block + row // width) * cw + rep * width + row % width
    for w in range(windows):
        live = 1.0 - listed(ids, dead_ref[w : w + 1, :])
        here = slice(w * count, (w + 1) * count)
        out_ref[w, :, :K] = (real_part[here] * live).astype(jnp.bfloat16)
        out_ref[w, :, K:] = (imag_part[here] * live).astype(jnp.bfloat16)


def channel_spectra(x, dead_list, tables, windows, cw, width):
    pieces, rows, _ = x.shape
    return pl.pallas_call(
        functools.partial(channel_kernel, cw, width),
        out_shape=jax.ShapeDtypeStruct((windows, rows // windows, 2 * K), jnp.bfloat16),
        in_specs=[VMEM] * 6,
        out_specs=VMEM,
        scratch_shapes=[pltpu.VMEM((pieces * rows, CHUNK + 2 * EDGE), jnp.bfloat16)],
        compiler_params=pltpu.CompilerParams(vmem_limit_bytes=LIMIT),
        cost_estimate=pl.CostEstimate(
            flops=2 * rows * 2048 * 1024, bytes_accessed=4 << 20, transcendentals=0
        ),
        name="channel_spectra",
    )(x, dead_list, *tables)


def source_kernel(keys, *refs):
    parts = refs[: len(keys)]
    src_ref, dead_ref, table_ref, band_ref, bins_ref, inverse_ref, out_ref, x_ref, ext_ref = refs[len(keys) :]
    chan = lax.axis_index("chan")
    for part, slots in zip(parts, keys):
        for n, key in enumerate(slots):
            x_ref[chan ^ key if key is not None else n] = part[n]
    real_part, imag_part = whiten_rows(x_ref, ext_ref, table_ref, band_ref, bins_ref, inverse_ref)
    windows = dead_ref.shape[0]
    quarter = out_ref.shape[0] // windows
    first = pl.multiple_of(lax.axis_index("rep") * quarter, quarter)
    mine = src_ref[pl.ds(first, quarter), :]
    for w in range(windows):
        live = 1.0 - listed(mine, dead_ref[w : w + 1, :])
        here = slice(w * quarter, (w + 1) * quarter)
        out_ref[here, :K] = (real_part[here] * live).astype(jnp.bfloat16).astype(jnp.float32)
        out_ref[here, K:] = (imag_part[here] * live).astype(jnp.bfloat16).astype(jnp.float32)


def source_spectra(parts, keys, sources, dead_list, tables):
    rows = parts[0].shape[1]
    pieces = sum(len(slots) for slots in keys)
    return pl.pallas_call(
        functools.partial(source_kernel, keys),
        out_shape=jax.ShapeDtypeStruct((rows, 2 * K), jnp.float32),
        in_specs=[VMEM] * (len(parts) + 6),
        out_specs=VMEM,
        scratch_shapes=[
            pltpu.VMEM((pieces, rows, CHUNK), jnp.bfloat16),
            pltpu.VMEM((pieces * rows, CHUNK + 2 * EDGE), jnp.bfloat16),
        ],
        compiler_params=pltpu.CompilerParams(vmem_limit_bytes=LIMIT),
        cost_estimate=pl.CostEstimate(
            flops=2 * rows * 2048 * 1024, bytes_accessed=4 << 20, transcendentals=0
        ),
        name="source_spectra",
    )(*parts, sources.reshape(-1, 1), dead_list, *tables)


def correlate_kernel(flips, cw, width, *refs):
    parts = refs[: len(flips)]
    spec_ref, src_ref, dead_ref, dead_t_ref, cos_ref, sin_ref, out_ref = refs[len(flips) : -2]
    right_ref, scale_ref = refs[-2:]
    windows, _, features = parts[0].shape
    step = pl.program_id(0)
    batch, lags, columns = out_ref.shape
    per = columns // cw
    quarter = spec_ref.shape[0] // windows

    @pl.when(step == 0)
    def _():
        rep = lax.axis_index("rep")
        for part, flip in zip(parts, flips):
            for w in range(windows):
                for g in range(per):
                    first = pl.multiple_of(g * cw + (rep ^ flip) * width, width)
                    right_ref[pl.ds(first, width), pl.ds(w * features, features)] = part[
                        w, pl.ds(g * width, width), :
                    ]
        ids = lax.axis_index("chan") * columns + iota((1, columns), 1)
        pairs = jnp.zeros((quarter, columns), jnp.float32)
        mine = src_ref[pl.ds(pl.multiple_of(rep * quarter, quarter), quarter), :]
        for w in range(windows):
            dead = jnp.where(dead_t_ref[:, w : w + 1] == ids, 1.0, 0.0)
            channel_live = 1.0 - jnp.max(dead, axis=0, keepdims=True)
            source_live = 1.0 - listed(mine, dead_ref[w : w + 1, :])
            pairs += source_live * channel_live
        scale_ref[...] = 1.0 / (math.sqrt(K) * jnp.maximum(pairs, 1.0))

    left = []
    for n in range(batch):
        s = step * batch + n
        row = []
        for w in range(windows):
            bins = spec_ref[pl.ds(w * quarter + s, 1), :]
            u, v = bins[:, :K], bins[:, K:]
            row.append((u * cos_ref[...] + v * sin_ref[...]).astype(jnp.bfloat16))
            row.append((v * cos_ref[...] - u * sin_ref[...]).astype(jnp.bfloat16))
        left.append(jnp.concatenate(row, axis=1))
    summed = lax.dot_general(
        jnp.concatenate(left, axis=0),
        right_ref[...],
        (((1,), (1,)), ((), ())),
        preferred_element_type=jnp.float32,
    )
    for n in range(batch):
        out_ref[n] = summed[n * lags : (n + 1) * lags] * scale_ref[pl.ds(step * batch + n, 1), :]


def correlate(parts, flips, source_spec, sources, dead_list, cw, width, columns):
    windows = dead_list.shape[0]
    quarter = source_spec.shape[0] // windows
    batch = 4
    cosine, sine = lag_tables()

    def whole(array):
        rank = array.ndim
        return pl.BlockSpec(array.shape, lambda i: (0,) * rank)

    operands = list(parts) + [
        source_spec, sources.reshape(-1, 1), dead_list, dead_list.T, jnp.asarray(cosine), jnp.asarray(sine)
    ]
    return pl.pallas_call(
        functools.partial(correlate_kernel, flips, cw, width),
        grid=(quarter // batch,),
        out_shape=jax.ShapeDtypeStruct((quarter, LAGS, columns), jnp.float32),
        in_specs=[whole(a) for a in operands],
        out_specs=pl.BlockSpec((batch, LAGS, columns), lambda i: (i, 0, 0)),
        scratch_shapes=[
            pltpu.VMEM((columns, windows * 2 * K), jnp.bfloat16),
            pltpu.VMEM((quarter, columns), jnp.float32),
        ],
        compiler_params=pltpu.CompilerParams(vmem_limit_bytes=LIMIT),
        name="correlate",
    )(*operands)


def swap(x, axis, flip):
    size = lax.axis_size(axis)
    return lax.ppermute(x, axis, [(i, i ^ flip) for i in range(size)])


def regroup(x):
    shards_in, rows, span = x.shape
    if span == CHUNK:
        return x
    joined = jnp.transpose(x, (1, 0, 2)).reshape(rows, -1, CHUNK)
    return jnp.transpose(joined, (1, 0, 2))


def gather_sources(keep, give):
    reps, chans = lax.axis_size("rep"), lax.axis_size("chan")
    rep, chan = lax.axis_index("rep"), lax.axis_index("chan")
    _, windows, quarter, span = keep.shape
    mine = keep + swap(give, "rep", 1)
    flip = 2
    while flip < reps:
        pairs = mine.reshape((-1, 2) + mine.shape[1:])
        bit = (rep // flip) % 2
        kept = lax.dynamic_index_in_dim(pairs, bit, 1, keepdims=False)
        given = lax.dynamic_index_in_dim(pairs, 1 - bit, 1, keepdims=False)
        mine = kept + swap(given, "rep", flip)
        flip *= 2
    held = mine.reshape(1, windows * quarter, span)
    keys = [0]
    flip = chans // 2
    while flip > 1:
        held = jnp.concatenate([held, swap(held, "chan", flip)], axis=0)
        keys = keys + [key ^ flip for key in keys]
        flip //= 2
    other = swap(held, "chan", 1)
    if span == CHUNK:
        return (held, other), (tuple(keys), tuple(key ^ 1 for key in keys))
    every = jnp.concatenate([held, other], axis=0)
    keys = jnp.asarray(keys + [key ^ 1 for key in keys], jnp.int32)
    every = jnp.zeros_like(every).at[chan ^ keys].set(every)
    every = regroup(every)
    return (every,), ((None,) * every.shape[0],)


def shards(records, sources, dead_list):
    windows, groups, width, span = records.shape
    reps, chans = lax.axis_size("rep"), lax.axis_size("chan")
    cw = width * reps
    per = groups // chans
    blocks, keep, give = pack(records, sources, chans, reps)
    blocks = blocks.reshape(chans, windows * per * width, span)
    bins, inverse = bin_band()
    tables = [
        jnp.asarray(a) for a in (dft_table(chans * span), sample_band(), bins, inverse)
    ]
    arrived = regroup(lax.all_to_all(blocks, "chan", 0, 0, tiled=True))
    parts, keys = gather_sources(keep, give)
    spectra = channel_spectra(arrived, dead_list, tables, windows, cw, width)
    source_spec = source_spectra(parts, keys, sources, dead_list, tables)
    pieces, flips = [spectra], [0]
    flip = reps // 2
    while flip:
        pieces = pieces + [swap(piece, "rep", flip) for piece in pieces]
        flips = flips + [f ^ flip for f in flips]
        flip //= 2
    return correlate(pieces, flips, source_spec, sources, dead_list, cw, width, per * cw)


def solution(mesh):
    placed = (P(None, None, "rep", "chan"), P(), P())
    return jax.shard_map(
        shards, mesh=mesh, in_specs=placed, out_specs=P("rep", None, "chan"), check_vma=False
    )
```

time: 100 us -> 42.1 us (0.42)
  blocking collectives: 50.5 us -> 0 us
  local copies, waits for them, and re-layouts: 19.7 us -> 3.97 us
  other arithmetic: 13.4 us -> 0.05 us
  waiting for transfers between devices: 2.98 us -> 14.6 us
  Pallas kernels: 0 us -> 8.14 us
  starting transfers between devices: 7.28 us -> 14.9 us
  matrix products: 5.95 us -> 0 us
    psum x1 -> x0, blocking collectives: 43.3 us -> none  [shards(): summed = lax.psum(picked, ('chan', 'rep'))]
    ppermute x0 -> x8, waiting for transfers between devices: none -> 14.6 us  [swap(): return lax.ppermute(x, axis, [(i, i ^ flip) for i in range(size)])]
    scatter x2 -> x0, local copies, waits for them, and re-layouts: 12.5 us -> none  [live_table(): jnp.ones((window_count, total), jnp.float32).at[window_rows, dead_list]]
    another operation x2 -> x0, other arithmetic: 10.9 us -> none
    pallas_call x0 -> x4, Pallas kernels: none -> 8.14 us  [the longest x1 4.84 us: correlate(): pl.pallas_call(functools.partial(correlate_kernel, flips, cw, width), gri...]
    ppermute x0 -> x8, starting transfers between devices: none -> 7.64 us  [swap(): return lax.ppermute(x, axis, [(i, i ^ flip) for i in range(size)])]
    all_gather x1 -> x0, blocking collectives: 7.17 us -> none  [shards(): piece = lax.all_gather(spectra, 'rep', axis=1, tiled=True)]
    dot_general x6 -> x0, matrix products: 5.95 us -> none  [the longest x1 2.66 us: correlate(): lax.dot_general(kernel, spectra, (((2, 3), (0, 2)), ((), ())), preferred_...]
  transfers between devices with their start and end apart: 1 -> 9, of which waited for: 1 -> 5; matrix products, arithmetic and copies ran while one was open for 11% -> 1% of each run, Pallas kernels for 0% -> 6%
where the time goes in v1:
time: 42.1 us; the launch traced here: 41.9 us
  starting transfers between devices  14.9 us (35%)
  waiting for transfers between devices  14.6 us (35%)
  Pallas kernels  8.14 us (19%)
  local copies, waits for them, and re-layouts  3.97 us (9%)
    ppermute x8, waiting for transfers between devices, swap(): return lax.ppermute(x, axis, [(i, i ^ flip) for i in range(size)])  14.6 us
    ppermute x8, starting transfers between devices, swap(): return lax.ppermute(x, axis, [(i, i ^ flip) for i in range(size)])  7.64 us
    all_to_all x1, starting transfers between devices, shards(): arrived = regroup(lax.all_to_all(blocks, 'chan', 0, 0, tiled=True))  7.28 us
    pallas_call x1, Pallas kernels, correlate(): pl.pallas_call(functools.partial(correlate_kernel, flips, cw, width), gri...  4.84 us
    unnamed x25, local copies, waits for them, and re-layouts  3.84 us
    pallas_call x1, Pallas kernels, channel_spectra(): pl.pallas_call(functools.partial(channel_kernel, cw, width), out_shape=ja...  1.31 us
    pallas_call x1, Pallas kernels, source_spectra(): pl.pallas_call(functools.partial(source_kernel, keys), out_shape=jax.Shap...  1.05 us
    pallas_call x1, Pallas kernels, pack(): pl.pallas_call(functools.partial(pack_kernel, width * reps), out_shape=(j...  0.95 us
  transfers between devices with their start and end apart: 9, of which 5 were waited for; matrix products, arithmetic and copies ran while one was open for 1% of the time, Pallas kernels for 6%

profile of v1, /device:TPU:0, one launch (start us, length us, event | category | flops | bytes accessed | tf_op | source)
XLA Modules:
  0.0 41.9 jit_solution(10564470154118091883)
XLA Ops:
  0.0 0.0 copy-start.9
  0.0 0.0 copy-start
  0.0 0.0 copy-start.3
  0.0 1.2 %copy-done.3 = bf16[2,8,64,256]{3,2,1,0:T(8,128)(2,1)S(1)} copy-done((bf16[2,8,64,256]{3,2,1,0:T(8,128)(2,1)S(1)}, bf16[2,8,64,256]{3,2,1,0:T(8,128)(2,1)}, u32[]{:S(2)}) %copy-start.3) | copy-done | bytes 524312
  1.2 0.0 copy-start.10
  1.2 0.7 %copy-done.10 = s32[128]{0:T(128)S(1)} copy-done((s32[128]{0:T(128)S(1)}, s32[128]{0:T(128)}, u32[]{:S(2)}) %copy-start.10) | copy-done | bytes 536
  1.9 0.0 copy-start.8
  1.9 1.0 %pack.1 = (bf16[8,2,1,64,256]{4,3,2,1,0:T(8,128)(2,1)}, bf16[2,2,32,256]{3,2,1,0:T(8,128)(2,1)S(1)}, bf16[2,2,32,256]{3,2,1,0:T(8,128)(2,1)S(1)}) custom-call(bf16[2,8,64,256]{3,2,1,0:T(8,128)(2,1)S(1)} %copy-done.3, s32[1,128]{1,0:T(1,128)S(1)} %bitcast.6), custom_call_target="tpu_custom_call" | custom-call | tf_op jit(solution)/shard_map/pack/pallas_call | solution.py:89
  2.8 7.3 %all-to-all-start = ((bf16[8,128,256]{2,1,0:T(8,128)(2,1)}), bf16[8,128,256]{2,1,0:T(8,128)(2,1)S(1)}, u32[]{:S(2)}, u32[]{:S(2)}) async-start(bf16[8,128,256]{2,1,0:T(8,128)(2,1)} %bitcast.1), calls=%async_computation | async-start | bytes 1048576 | tf_op jit(solution)/shard_map/all_to_all | solution.py:345
  10.1 0.0 copy-start.11
  10.1 0.1 collective-permute-start.3
  10.2 1.2 %collective-permute-done.3 = bf16[2,2,32,256]{3,2,1,0:T(8,128)(2,1)S(1)} collective-permute-done((bf16[2,2,32,256]{3,2,1,0:T(8,128)(2,1)S(1)}, bf16[2,2,32,256]{3,2,1,0:T(8,128)(2,1)S(1)}, u32[]{:S(2)}, u32[]{:S(2)}) %collective-permute-start.3) | collective-permute-done | bytes 65568 | tf_op jit(solution)/shard_map/ppermute | solution.py:293
  11.5 1.6 %collective-permute-start.4 = (bf16[1,2,32,256]{3,2,1,0:T(8,128)(2,1)S(1)}, bf16[1,2,32,256]{3,2,1,0:T(8,128)(2,1)S(1)}, u32[]{:S(2)}, u32[]{:S(2)}) collective-permute-start(bf16[1,2,32,256]{3,2,1,0:T(8,128)(2,1)S(1)} %constant_dynamic-slice_fusion), channel_id=1, source_target_pairs={{0,2},{1,3},{2,0},{3,1},{4,6},{5,7},{6,4},{7,5},{8,10},{9,11},{10,... | collective-permute-start | bytes 98312 | tf_op jit(solution)/shard_map/ppermute | solution.py:293
  13.0 2.4 %collective-permute-done.4 = bf16[1,2,32,256]{3,2,1,0:T(8,128)(2,1)S(1)} collective-permute-done((bf16[1,2,32,256]{3,2,1,0:T(8,128)(2,1)S(1)}, bf16[1,2,32,256]{3,2,1,0:T(8,128)(2,1)S(1)}, u32[]{:S(2)}, u32[]{:S(2)}) %collective-permute-start.4) | collective-permute-done | bytes 32800 | tf_op jit(solution)/shard_map/ppermute | solution.py:293
  15.4 2.9 %collective-permute-start.5 = (bf16[1,64,256]{2,1,0:T(8,128)(2,1)S(1)}, bf16[1,64,256]{2,1,0:T(8,128)(2,1)S(1)}, u32[]{:S(2)}, u32[]{:S(2)}) collective-permute-start(bf16[1,64,256]{2,1,0:T(8,128)(2,1)S(1)} %bitcast.8), channel_id=1, source_target_pairs={{0,16},{4,20},{8,24},{12,28},{16,0},{20,4},{24,8},{28,12},{1,17},{... | collective-permute-start | bytes 98312 | tf_op jit(solution)/shard_map/ppermute | solution.py:293
  18.3 7.7 %collective-permute-done.5 = bf16[1,64,256]{2,1,0:T(8,128)(2,1)S(1)} collective-permute-done((bf16[1,64,256]{2,1,0:T(8,128)(2,1)S(1)}, bf16[1,64,256]{2,1,0:T(8,128)(2,1)S(1)}, u32[]{:S(2)}, u32[]{:S(2)}) %collective-permute-start.5) | collective-permute-done | bytes 32800 | tf_op jit(solution)/shard_map/ppermute | solution.py:293
  26.0 0.1 collective-permute-start.6
  26.1 0.0 all-to-all-done.x_ref
  26.1 0.0 copy-done.9
  26.1 0.0 copy-done
  26.1 0.0 copy-done.8
  26.1 0.0 copy-start.1
  26.1 0.9 %copy-done.1 = bf16[512,256]{1,0:T(8,128)(2,1)S(1)} copy-done((bf16[512,256]{1,0:T(8,128)(2,1)S(1)}, bf16[512,256]{1,0:T(8,128)(2,1)}, u32[]{:S(2)}) %copy-start.1) | copy-done | bytes 262168
  27.1 0.0 copy-start.4
  27.1 0.9 %copy-done.4 = bf16[256,256]{1,0:T(8,128)(2,1)S(1)} copy-done((bf16[256,256]{1,0:T(8,128)(2,1)S(1)}, bf16[256,256]{1,0:T(8,128)(2,1)}, u32[]{:S(2)}) %copy-start.4) | copy-done | bytes 131096
  28.0 0.0 copy-start.2
  28.0 0.0 copy-start.5
  28.0 1.3 %channel_spectra.1.refs_0_ = bf16[2,64,512]{2,1,0:T(8,128)(2,1)S(1)} custom-call(bf16[8,128,256]{2,1,0:T(8,128)(2,1)S(1)} %all-to-all-done.x_ref, s32[2,128]{1,0:T(2,128)S(1)} %copy-done.8, bf16[2048,512]{1,0:T(8,128)(2,1)S(1)} %copy-done, bf16[512,256]{1,0:T(8,128)(2,1)S(1)} %copy-done.1, bf16[256,256]{1,0:T(8,128)(2,1)S(1)} %copy-done.4, ...), custom_call_target="tpu_custom_call" | custom-call | flops 536870912 | bytes 4194304 | tf_op jit(solution)/shard_map/channel_spectra/pallas_call | solution.py:160
  29.3 0.0 copy-start.6
  29.3 0.0 copy-start.7
  29.3 1.6 %collective-permute-start = (bf16[2,64,512]{2,1,0:T(8,128)(2,1)S(1)}, bf16[2,64,512]{2,1,0:T(8,128)(2,1)S(1)}, u32[]{:S(2)}, u32[]{:S(2)}) collective-permute-start(bf16[2,64,512]{2,1,0:T(8,128)(2,1)S(1)} %channel_spectra.1.refs_0_), channel_id=1, source_target_pairs={{0,2},{1,3},{2,0},{3,1},{4,6},{5,7},{6,4},{7,5},{8,10},{9,11},{10,... | collective-permute-start | bytes 393224 | tf_op jit(solution)/shard_map/ppermute | solution.py:293
  30.9 0.0 collective-permute-done.6
  30.9 1.5 %collective-permute-start.7 = (bf16[4,64,256]{2,1,0:T(8,128)(2,1)S(1)}, bf16[4,64,256]{2,1,0:T(8,128)(2,1)S(1)}, u32[]{:S(2)}, u32[]{:S(2)}) collective-permute-start(bf16[4,64,256]{2,1,0:T(8,128)(2,1)S(1)} %pad_maximum_fusion.refs_0_), channel_id=1, source_target_pairs={{0,4},{4,0},{8,12},{12,8},{16,20},{20,16},{24,28},{28,24},{1,5},{5... | collective-permute-start | bytes 393224 | tf_op jit(solution)/shard_map/ppermute | solution.py:293
  32.4 0.0 collective-permute-start.1
  32.4 1.9 %collective-permute-done.refs_1_ = bf16[2,64,512]{2,1,0:T(8,128)(2,1)S(1)} collective-permute-done((bf16[2,64,512]{2,1,0:T(8,128)(2,1)S(1)}, bf16[2,64,512]{2,1,0:T(8,128)(2,1)S(1)}, u32[]{:S(2)}, u32[]{:S(2)}) %collective-permute-start) | collective-permute-done | bytes 131104 | tf_op jit(solution)/shard_map/ppermute | solution.py:293
  34.3 0.0 collective-permute-start.2
  34.4 0.1 copy.11
  34.5 0.0 copy-done.11
  34.5 0.1 copy.10.refs_2_.refs_5_
  34.6 1.3 %collective-permute-done.7.refs_1_ = bf16[4,64,256]{2,1,0:T(8,128)(2,1)S(1)} collective-permute-done((bf16[4,64,256]{2,1,0:T(8,128)(2,1)S(1)}, bf16[4,64,256]{2,1,0:T(8,128)(2,1)S(1)}, u32[]{:S(2)}, u32[]{:S(2)}) %collective-permute-start.7) | collective-permute-done | bytes 131104 | tf_op jit(solution)/shard_map/ppermute | solution.py:293
  35.9 0.0 copy-done.2
  35.9 0.0 copy-done.5
  35.9 1.0 %source_spectra.1.refs_4_ = f32[64,512]{1,0:T(8,128)S(1)} custom-call(bf16[4,64,256]{2,1,0:T(8,128)(2,1)S(1)} %pad_maximum_fusion.refs_0_, bf16[4,64,256]{2,1,0:T(8,128)(2,1)S(1)} %collective-permute-done.7.refs_1_, s32[128,1]{1,0:T(8,128)S(1)} %copy.10.refs_2_.refs_5_, s32[2,128]{1,0:T(2,128)S(1)} %copy-done.8, bf16[2048,512]{1,0:T(8,128)(2,1)S(1)} %copy-done, ...), custom_call_target="tpu_custom_call" | custom-call | flops 268435456 | bytes 4194304 | tf_op jit(solution)/shard_map/source_spectra/pallas_call | solution.py:196
  37.0 0.0 collective-permute-done.1.refs_2_
  37.0 0.0 collective-permute-done.2.refs_3_
  37.0 0.0 copy-done.6
  37.0 0.0 copy-done.7
  37.0 4.8 %correlate.1 = f32[32,64,256]{2,1,0:T(8,128)} custom-call(bf16[2,64,512]{2,1,0:T(8,128)(2,1)S(1)} %channel_spectra.1.refs_0_, bf16[2,64,512]{2,1,0:T(8,128)(2,1)S(1)} %collective-permute-done.refs_1_, bf16[2,64,512]{2,1,0:T(8,128)(2,1)S(1)} %collective-permute-done.1.refs_2_, bf16[2,64,512]{2,1,0:T(8,128)(2,1)S(1)} %collective-permute-done.2.refs_3_, ...), custom_call_target="tpu_custom_call" | custom-call | tf_op jit(solution)/shard_map/correlate/pallas_call | solution.py:276
  (5 shorter events, 0.1 us)
Async XLA Ops:
  0.0 26.1 %copy-start.9 = (f32[1,256]{1,0:T(1,128)S(1)}, f32[1,256]{1,0:T(1,128)}, u32[]{:S(2)}) copy-start(f32[1,256]{1,0:T(1,128)} %constant.52.clone.inverse_ref.refs_7_) | copy-start | bytes 3076
  0.0 26.1 %copy-start = (bf16[2048,512]{1,0:T(8,128)(2,1)S(1)}, bf16[2048,512]{1,0:T(8,128)(2,1)}, u32[]{:S(2)}) copy-start(bf16[2048,512]{1,0:T(8,128)(2,1)} %constant.49.clone.table_ref.refs_4_) | copy-start | bytes 6291460
  0.0 1.2 %copy-start.3 = (bf16[2,8,64,256]{3,2,1,0:T(8,128)(2,1)S(1)}, bf16[2,8,64,256]{3,2,1,0:T(8,128)(2,1)}, u32[]{:S(2)}) copy-start(bf16[2,8,64,256]{3,2,1,0:T(8,128)(2,1)} %rec_ref.1) | copy-start | bytes 1572868
  1.2 0.7 %copy-start.10 = (s32[128]{0:T(128)S(1)}, s32[128]{0:T(128)}, u32[]{:S(2)}) copy-start(s32[128]{0:T(128)} %param.10) | copy-start | bytes 1540
  1.9 24.3 %copy-start.8 = (s32[2,128]{1,0:T(2,128)S(1)}, s32[2,128]{1,0:T(2,128)}, u32[]{:S(2)}) copy-start(s32[2,128]{1,0:T(2,128)} %refs_6_.2) | copy-start | bytes 3076
  2.8 23.3 %all-to-all-start = ((bf16[8,128,256]{2,1,0:T(8,128)(2,1)}), bf16[8,128,256]{2,1,0:T(8,128)(2,1)S(1)}, u32[]{:S(2)}, u32[]{:S(2)}) async-start(bf16[8,128,256]{2,1,0:T(8,128)(2,1)} %bitcast.1), calls=%async_computation | async-start | bytes 1048576 | tf_op jit(solution)/shard_map/all_to_all | solution.py:345
  10.1 24.4 %copy-start.11 = (s32[128]{0:T(128)S(1)}, s32[128]{0:T(128)}, u32[]{:S(2)}) copy-start(s32[128]{0:T(128)} %param.10) | copy-start | bytes 1540
  10.1 1.3 %collective-permute-start.3 = (bf16[2,2,32,256]{3,2,1,0:T(8,128)(2,1)S(1)}, bf16[2,2,32,256]{3,2,1,0:T(8,128)(2,1)S(1)}, u32[]{:S(2)}, u32[]{:S(2)}) collective-permute-start(bf16[2,2,32,256]{3,2,1,0:T(8,128)(2,1)S(1)} %get-tuple-element.10), channel_id=1, source_target_pairs={{0,1},{1,0},{2,3},{3,2},{4,5},{5,4},{6,7},{7,6},{8,9},{9,8},{10,11... | collective-permute-start | bytes 196616 | tf_op jit(solution)/shard_map/ppermute | solution.py:293
  11.5 4.0 %collective-permute-start.4 = (bf16[1,2,32,256]{3,2,1,0:T(8,128)(2,1)S(1)}, bf16[1,2,32,256]{3,2,1,0:T(8,128)(2,1)S(1)}, u32[]{:S(2)}, u32[]{:S(2)}) collective-permute-start(bf16[1,2,32,256]{3,2,1,0:T(8,128)(2,1)S(1)} %constant_dynamic-slice_fusion), channel_id=1, source_target_pairs={{0,2},{1,3},{2,0},{3,1},{4,6},{5,7},{6,4},{7,5},{8,10},{9,11},{10,... | collective-permute-start | bytes 98312 | tf_op jit(solution)/shard_map/ppermute | solution.py:293
  15.4 10.5 %collective-permute-start.5 = (bf16[1,64,256]{2,1,0:T(8,128)(2,1)S(1)}, bf16[1,64,256]{2,1,0:T(8,128)(2,1)S(1)}, u32[]{:S(2)}, u32[]{:S(2)}) collective-permute-start(bf16[1,64,256]{2,1,0:T(8,128)(2,1)S(1)} %bitcast.8), channel_id=1, source_target_pairs={{0,16},{4,20},{8,24},{12,28},{16,0},{20,4},{24,8},{28,12},{1,17},{... | collective-permute-start | bytes 98312 | tf_op jit(solution)/shard_map/ppermute | solution.py:293
  26.0 4.9 %collective-permute-start.6 = (bf16[2,64,256]{2,1,0:T(8,128)(2,1)S(1)}, bf16[2,64,256]{2,1,0:T(8,128)(2,1)S(1)}, u32[]{:S(2)}, u32[]{:S(2)}) collective-permute-start(bf16[2,64,256]{2,1,0:T(8,128)(2,1)S(1)} %pad_maximum_fusion.1), channel_id=1, source_target_pairs={{0,8},{4,12},{8,0},{12,4},{16,24},{20,28},{24,16},{28,20},{1,9},{5... | collective-permute-start | bytes 196616 | tf_op jit(solution)/shard_map/ppermute | solution.py:293
  26.1 1.0 %copy-start.1 = (bf16[512,256]{1,0:T(8,128)(2,1)S(1)}, bf16[512,256]{1,0:T(8,128)(2,1)}, u32[]{:S(2)}) copy-start(bf16[512,256]{1,0:T(8,128)(2,1)} %constant.50.clone.band_ref.refs_5_) | copy-start | bytes 786436
  27.1 0.9 %copy-start.4 = (bf16[256,256]{1,0:T(8,128)(2,1)S(1)}, bf16[256,256]{1,0:T(8,128)(2,1)}, u32[]{:S(2)}) copy-start(bf16[256,256]{1,0:T(8,128)(2,1)} %constant.51.clone.bins_ref.refs_6_) | copy-start | bytes 393220
  28.0 8.0 %copy-start.2 = (bf16[512,256]{1,0:T(8,128)(2,1)S(1)}, bf16[512,256]{1,0:T(8,128)(2,1)}, u32[]{:S(2)}) copy-start(bf16[512,256]{1,0:T(8,128)(2,1)} %constant.50.clone.band_ref.refs_5_) | copy-start | bytes 786436
  28.0 8.0 %copy-start.5 = (bf16[256,256]{1,0:T(8,128)(2,1)S(1)}, bf16[256,256]{1,0:T(8,128)(2,1)}, u32[]{:S(2)}) copy-start(bf16[256,256]{1,0:T(8,128)(2,1)} %constant.51.clone.bins_ref.refs_6_) | copy-start | bytes 393220
  29.3 7.7 %copy-start.6 = (f32[64,256]{1,0:T(8,128)S(1)}, f32[64,256]{1,0:T(8,128)}, u32[]{:S(2)}) copy-start(f32[64,256]{1,0:T(8,128)} %constant.54.clone.refs_9_) | copy-start | bytes 196612
  29.3 7.7 %copy-start.7 = (f32[64,256]{1,0:T(8,128)S(1)}, f32[64,256]{1,0:T(8,128)}, u32[]{:S(2)}) copy-start(f32[64,256]{1,0:T(8,128)} %constant.53.clone.refs_8_) | copy-start | bytes 196612
  29.3 5.0 %collective-permute-start = (bf16[2,64,512]{2,1,0:T(8,128)(2,1)S(1)}, bf16[2,64,512]{2,1,0:T(8,128)(2,1)S(1)}, u32[]{:S(2)}, u32[]{:S(2)}) collective-permute-start(bf16[2,64,512]{2,1,0:T(8,128)(2,1)S(1)} %channel_spectra.1.refs_0_), channel_id=1, source_target_pairs={{0,2},{1,3},{2,0},{3,1},{4,6},{5,7},{6,4},{7,5},{8,10},{9,11},{10,... | collective-permute-start | bytes 393224 | tf_op jit(solution)/shard_map/ppermute | solution.py:293
  30.9 5.0 %collective-permute-start.7 = (bf16[4,64,256]{2,1,0:T(8,128)(2,1)S(1)}, bf16[4,64,256]{2,1,0:T(8,128)(2,1)S(1)}, u32[]{:S(2)}, u32[]{:S(2)}) collective-permute-start(bf16[4,64,256]{2,1,0:T(8,128)(2,1)S(1)} %pad_maximum_fusion.refs_0_), channel_id=1, source_target_pairs={{0,4},{4,0},{8,12},{12,8},{16,20},{20,16},{24,28},{28,24},{1,5},{5... | collective-permute-start | bytes 393224 | tf_op jit(solution)/shard_map/ppermute | solution.py:293
  32.4 4.6 %collective-permute-start.1 = (bf16[2,64,512]{2,1,0:T(8,128)(2,1)S(1)}, bf16[2,64,512]{2,1,0:T(8,128)(2,1)S(1)}, u32[]{:S(2)}, u32[]{:S(2)}) collective-permute-start(bf16[2,64,512]{2,1,0:T(8,128)(2,1)S(1)} %channel_spectra.1.refs_0_), channel_id=1, source_target_pairs={{0,1},{1,0},{2,3},{3,2},{4,5},{5,4},{6,7},{7,6},{8,9},{9,8},{10,11... | collective-permute-start | bytes 393224 | tf_op jit(solution)/shard_map/ppermute | solution.py:293
  34.3 2.7 %collective-permute-start.2 = (bf16[2,64,512]{2,1,0:T(8,128)(2,1)S(1)}, bf16[2,64,512]{2,1,0:T(8,128)(2,1)S(1)}, u32[]{:S(2)}, u32[]{:S(2)}) collective-permute-start(bf16[2,64,512]{2,1,0:T(8,128)(2,1)S(1)} %collective-permute-done.refs_1_), channel_id=1, source_target_pairs={{0,1},{1,0},{2,3},{3,2},{4,5},{5,4},{6,7},{7,6},{8,9},{9,8},{10,11... | collective-permute-start | bytes 393224 | tf_op jit(solution)/shard_map/ppermute | solution.py:293

commit v2 on v1

v2 whole, which is shorter than its diff:
```python
import functools
import math

import jax
import jax.numpy as jnp
import numpy as np
from jax import lax
from jax.experimental import pallas as pl
from jax.experimental.pallas import tpu as pltpu
from jax.sharding import PartitionSpec as P

WINDOW_SAMPLES = 2048
K = 256
K0 = 16
HALF = 32
WH = 32
LAGS = 64
EPS = 1e-06

CHUNK = 256
EDGE = 128
VMEM = pl.BlockSpec(memory_space=pltpu.VMEM)
LIMIT = 40 * 1024 * 1024


def dft_table(length):
    sample = np.arange(length, dtype=np.int64)[:, None]
    bin_index = K0 + np.arange(K, dtype=np.int64)[None, :]
    angle = (sample * bin_index % length) * (2.0 * math.pi / length)
    table = np.concatenate([np.cos(angle), -np.sin(angle)], axis=1)
    return table.astype(np.float32).astype(jnp.bfloat16)


def lag_tables():
    bin_index = K0 + np.arange(K, dtype=np.int64)[None, :]
    lag = np.arange(LAGS, dtype=np.int64)[:, None] - LAGS // 2
    angle = np.mod(lag * bin_index, WINDOW_SAMPLES) * (2.0 * math.pi / WINDOW_SAMPLES)
    return np.cos(angle).astype(np.float32), np.sin(angle).astype(np.float32)


def sample_band():
    source = np.arange(CHUNK + 2 * EDGE)[:, None] - EDGE
    target = np.arange(CHUNK)[None, :]
    return (np.abs(source - target) <= HALF).astype(np.float32).astype(jnp.bfloat16)


def bin_band():
    row = np.arange(K)[:, None]
    column = np.arange(K)[None, :]
    band = np.abs(row - column) <= WH
    inverse = 1.0 / band.sum(axis=0, keepdims=True)
    return band.astype(np.float32).astype(jnp.bfloat16), inverse.astype(np.float32)


def iota(shape, dim):
    return lax.broadcasted_iota(jnp.int32, shape, dim)


def columns_of(row):
    return jnp.concatenate(
        [
            jnp.broadcast_to(row[:, i : i + 128], (128, 128)).T
            for i in range(0, row.shape[1], 128)
        ],
        axis=0,
    )


def listed(ids, dead):
    hit = jnp.zeros((ids.shape[0], 128), jnp.float32)
    for i in range(0, dead.shape[1], 128):
        hit = jnp.maximum(hit, jnp.where(ids == dead[:, i : i + 128], 1.0, 0.0))
    return jnp.max(hit, axis=1, keepdims=True)


def pack_kernel(
    cw, rec_hbm, src_hbm, dead_hbm,
    out_ref, keep_ref, give_ref, live_ref, source_live_ref, scale_ref,
    rec_ref, src_ref, dead_ref, pick_ref, sem,
):
    copies = [
        pltpu.make_async_copy(src_hbm, src_ref, sem.at[0]),
        pltpu.make_async_copy(dead_hbm, dead_ref, sem.at[1]),
        pltpu.make_async_copy(rec_hbm, rec_ref, sem.at[2]),
    ]
    for copy in copies:
        copy.start()
    windows, groups, width, span = rec_ref.shape
    reps = cw // width
    rep, chan = lax.axis_index("rep"), lax.axis_index("chan")
    per = groups // out_ref.shape[0]
    count = src_ref.shape[1]
    quarter = count // reps
    here = pl.ds(pl.multiple_of(rep * quarter, quarter), quarter)
    copies[0].wait()
    column = columns_of(src_ref[...])
    local = groups * width
    place = iota((count, local), 1)
    ids = (place // width) * cw + rep * width + place % width
    wide = jnp.concatenate([column] * (local // 128), axis=1)
    onehot = jnp.where(wide == ids, 1.0, 0.0).astype(jnp.bfloat16)
    copies[1].wait()
    row = iota((per * width, 1), 0)
    row_ids = (chan * per + row // width) * cw + rep * width + row % width
    block_ids = chan * per * cw + iota((1, per * cw), 1)
    pairs = jnp.zeros((count, per * cw), jnp.float32)
    for w in range(windows):
        dead = dead_ref[w : w + 1, :]
        live_ref[w * per * width : (w + 1) * per * width, :] = 1.0 - listed(row_ids, dead)
        source_live = 1.0 - listed(column, dead)
        pick_ref[:, :1] = source_live
        source_live_ref[w * quarter : (w + 1) * quarter, :] = pick_ref[here, :1]
        dead_column = columns_of(dead)
        hits = [
            jnp.max(
                jnp.where(dead_column == block_ids[:, i : i + 128], 1.0, 0.0), axis=0, keepdims=True
            )
            for i in range(0, per * cw, 128)
        ]
        pairs += source_live * (1.0 - jnp.concatenate(hits, axis=1))
    for i in range(0, per * cw, span):
        pick_ref[:, : min(span, per * cw)] = pairs[:, i : i + span]
        scale_ref[:, i : i + span] = 1.0 / (
            math.sqrt(K) * jnp.maximum(pick_ref[here, : min(span, per * cw)], 1.0)
        )
    copies[2].wait()
    for w in range(windows):
        for g in range(groups):
            out_ref[g // per, w, g % per] = rec_ref[w, g]
    for w in range(windows):
        rows = rec_ref[w].reshape(local, span)
        pick_ref[...] = jnp.dot(onehot, rows, preferred_element_type=jnp.float32)
        for half in range(reps // 2):
            for ref, bit in ((keep_ref, rep % 2), (give_ref, 1 - rep % 2)):
                first = pl.multiple_of((2 * half + bit) * quarter, quarter)
                ref[half, w] = pick_ref[pl.ds(first, quarter), :].astype(jnp.bfloat16)


def pack(records, sources, dead_list, chans, reps):
    windows, groups, width, span = records.shape
    count = sources.shape[0]
    per = groups // chans
    part = (reps // 2, windows, count // reps, span)
    anywhere = pl.BlockSpec(memory_space=pl.ANY)
    return pl.pallas_call(
        functools.partial(pack_kernel, width * reps),
        out_shape=(
            jax.ShapeDtypeStruct((chans, windows, per, width, span), jnp.bfloat16),
            jax.ShapeDtypeStruct(part, jnp.bfloat16),
            jax.ShapeDtypeStruct(part, jnp.bfloat16),
            jax.ShapeDtypeStruct((windows * per * width, 1), jnp.float32),
            jax.ShapeDtypeStruct((windows * count // reps, 1), jnp.float32),
            jax.ShapeDtypeStruct((count // reps, per * width * reps), jnp.float32),
        ),
        in_specs=[anywhere] * 3,
        out_specs=(VMEM,) * 6,
        scratch_shapes=[
            pltpu.VMEM(records.shape, jnp.bfloat16),
            pltpu.VMEM((1, count), jnp.int32),
            pltpu.VMEM(dead_list.shape, jnp.int32),
            pltpu.VMEM((count, span), jnp.float32),
            pltpu.SemaphoreType.DMA((3,)),
        ],
        compiler_params=pltpu.CompilerParams(vmem_limit_bytes=LIMIT),
        name="pack",
    )(records, sources.reshape(1, count), dead_list)


def whiten_rows(x_ref, ext_ref, table_ref, band_ref, bins_ref, inverse_ref):
    pieces, rows, _ = x_ref.shape
    length = pieces * CHUNK
    for i in range(pieces):
        here = pl.ds(i * rows, rows)
        ext_ref[here, EDGE : EDGE + CHUNK] = jnp.abs(x_ref[i])
        blank = jnp.zeros((rows, EDGE), jnp.bfloat16)
        ext_ref[here, :EDGE] = jnp.abs(x_ref[i - 1, :, CHUNK - EDGE :]) if i else blank
        ext_ref[here, EDGE + CHUNK :] = (
            jnp.abs(x_ref[i + 1, :, :EDGE]) if i < pieces - 1 else blank
        )
    totals = jnp.dot(ext_ref[...], band_ref[...], preferred_element_type=jnp.float32)
    spectrum = jnp.zeros((rows, 2 * K), jnp.float32)
    for i in range(pieces):
        sample = iota((1, CHUNK), 1) + i * CHUNK
        counts = jnp.minimum(sample, HALF) + jnp.minimum(length - 1 - sample, HALF) + 1
        mean = totals[i * rows : (i + 1) * rows] * (1.0 / counts.astype(jnp.float32))
        normed = (x_ref[i].astype(jnp.float32) / (mean + EPS)).astype(jnp.bfloat16)
        spectrum += jnp.dot(
            normed, table_ref[i * CHUNK : (i + 1) * CHUNK, :], preferred_element_type=jnp.float32
        )
    real_part, imag_part = spectrum[:, :K], spectrum[:, K:]
    amplitude = jnp.sqrt(real_part * real_part + imag_part * imag_part)
    high = amplitude.astype(jnp.bfloat16)
    rest = amplitude - high.astype(jnp.float32)
    middle = rest.astype(jnp.bfloat16)
    low = (rest - middle.astype(jnp.float32)).astype(jnp.bfloat16)
    stacked = jnp.concatenate([high, middle, low], axis=0)
    sums = jnp.dot(stacked, bins_ref[...], preferred_element_type=jnp.float32)
    smooth = (sums[:rows] + sums[rows : 2 * rows] + sums[2 * rows :]) * inverse_ref[...]
    scale = 1.0 / (smooth + EPS)
    return real_part * scale, imag_part * scale


def channel_kernel(x_ref, live_ref, table_ref, band_ref, bins_ref, inverse_ref, out_ref, ext_ref):
    windows, count, _ = out_ref.shape
    real_part, imag_part = whiten_rows(x_ref, ext_ref, table_ref, band_ref, bins_ref, inverse_ref)
    for w in range(windows):
        here = slice(w * count, (w + 1) * count)
        out_ref[w, :, :K] = (real_part[here] * live_ref[here, :]).astype(jnp.bfloat16)
        out_ref[w, :, K:] = (imag_part[here] * live_ref[here, :]).astype(jnp.bfloat16)


def channel_spectra(x, live, tables, windows):
    pieces, rows, _ = x.shape
    return pl.pallas_call(
        channel_kernel,
        out_shape=jax.ShapeDtypeStruct((windows, rows // windows, 2 * K), jnp.bfloat16),
        in_specs=[VMEM] * 6,
        out_specs=VMEM,
        scratch_shapes=[pltpu.VMEM((pieces * rows, CHUNK + 2 * EDGE), jnp.bfloat16)],
        compiler_params=pltpu.CompilerParams(vmem_limit_bytes=LIMIT),
        cost_estimate=pl.CostEstimate(
            flops=2 * rows * 2048 * 1024, bytes_accessed=4 << 20, transcendentals=0
        ),
        name="channel_spectra",
    )(x, live, *tables)


def source_kernel(keys, windows, *refs):
    parts = refs[: len(keys)]
    live_ref, cos_ref, sin_ref, table_ref, band_ref, bins_ref, inverse_ref = refs[len(keys) : -3]
    out_ref, x_ref, ext_ref = refs[-3:]
    chan = lax.axis_index("chan")
    for part, slots in zip(parts, keys):
        for n, key in enumerate(slots):
            x_ref[chan ^ key if key is not None else n] = part[n]
    real_part, imag_part = whiten_rows(x_ref, ext_ref, table_ref, band_ref, bins_ref, inverse_ref)
    real_part = (real_part * live_ref[...]).astype(jnp.bfloat16).astype(jnp.float32)
    imag_part = (imag_part * live_ref[...]).astype(jnp.bfloat16).astype(jnp.float32)
    quarter = real_part.shape[0] // windows
    lags = cos_ref.shape[0]
    for s in range(quarter):
        for w in range(windows):
            u = real_part[w * quarter + s : w * quarter + s + 1, :]
            v = imag_part[w * quarter + s : w * quarter + s + 1, :]
            rows = slice(s * lags, (s + 1) * lags)
            first = w * 2 * K
            out_ref[rows, first : first + K] = (
                u * cos_ref[...] + v * sin_ref[...]
            ).astype(jnp.bfloat16)
            out_ref[rows, first + K : first + 2 * K] = (
                v * cos_ref[...] - u * sin_ref[...]
            ).astype(jnp.bfloat16)


def source_kernels(parts, keys, live, tables, windows):
    rows = parts[0].shape[1]
    pieces = sum(len(slots) for slots in keys)
    cosine, sine = lag_tables()
    return pl.pallas_call(
        functools.partial(source_kernel, keys, windows),
        out_shape=jax.ShapeDtypeStruct((rows // windows * LAGS, windows * 2 * K), jnp.bfloat16),
        in_specs=[VMEM] * (len(parts) + 7),
        out_specs=VMEM,
        scratch_shapes=[
            pltpu.VMEM((pieces, rows, CHUNK), jnp.bfloat16),
            pltpu.VMEM((pieces * rows, CHUNK + 2 * EDGE), jnp.bfloat16),
        ],
        compiler_params=pltpu.CompilerParams(vmem_limit_bytes=LIMIT),
        cost_estimate=pl.CostEstimate(
            flops=2 * rows * 2048 * 1024, bytes_accessed=8 << 20, transcendentals=0
        ),
        name="source_kernels",
    )(*parts, live, jnp.asarray(cosine), jnp.asarray(sine), *tables)


def correlate_kernel(flips, cw, *refs):
    parts = refs[: len(flips)]
    left_ref, scale_ref, out_ref, right_ref = refs[len(flips) :]
    windows, count, features = parts[0].shape
    batch, lags, columns = out_ref.shape
    per = columns // cw
    width = count // per

    @pl.when(pl.program_id(0) == 0)
    def _():
        rep = lax.axis_index("rep")
        for part, flip in zip(parts, flips):
            for w in range(windows):
                for g in range(per):
                    first = pl.multiple_of(g * cw + (rep ^ flip) * width, width)
                    right_ref[pl.ds(first, width), pl.ds(w * features, features)] = part[
                        w, pl.ds(g * width, width), :
                    ]

    summed = lax.dot_general(
        left_ref[...], right_ref[...], (((1,), (1,)), ((), ())), preferred_element_type=jnp.float32
    )
    for n in range(batch):
        scale = scale_ref[pl.ds(pl.program_id(0) * batch + n, 1), :]
        out_ref[n] = summed[n * lags : (n + 1) * lags] * scale


def correlate(parts, flips, left, scale, cw):
    quarter, columns = scale.shape
    batch = 8

    def whole(array):
        rank = array.ndim
        return pl.BlockSpec(array.shape, lambda i: (0,) * rank)

    return pl.pallas_call(
        functools.partial(correlate_kernel, flips, cw),
        grid=(quarter // batch,),
        out_shape=jax.ShapeDtypeStruct((quarter, LAGS, columns), jnp.float32),
        in_specs=[whole(part) for part in parts]
        + [pl.BlockSpec((batch * LAGS, left.shape[1]), lambda i: (i, 0)), whole(scale)],
        out_specs=pl.BlockSpec((batch, LAGS, columns), lambda i: (i, 0, 0)),
        scratch_shapes=[pltpu.VMEM((columns, left.shape[1]), jnp.bfloat16)],
        compiler_params=pltpu.CompilerParams(vmem_limit_bytes=LIMIT),
        name="correlate",
    )(*parts, left, scale)


def swap(x, axis, flip):
    size = lax.axis_size(axis)
    return lax.ppermute(x, axis, [(i, i ^ flip) for i in range(size)])


def regroup(x):
    shards_in, rows, span = x.shape
    if span == CHUNK:
        return x
    joined = jnp.transpose(x, (1, 0, 2)).reshape(rows, -1, CHUNK)
    return jnp.transpose(joined, (1, 0, 2))


def gather_sources(keep, give):
    reps, chans = lax.axis_size("rep"), lax.axis_size("chan")
    rep, chan = lax.axis_index("rep"), lax.axis_index("chan")
    _, windows, quarter, span = keep.shape
    mine = keep + swap(give, "rep", 1)
    flip = 2
    while flip < reps:
        pairs = mine.reshape((-1, 2) + mine.shape[1:])
        bit = (rep // flip) % 2
        kept = lax.dynamic_index_in_dim(pairs, bit, 1, keepdims=False)
        given = lax.dynamic_index_in_dim(pairs, 1 - bit, 1, keepdims=False)
        mine = kept + swap(given, "rep", flip)
        flip *= 2
    held = mine.reshape(1, windows * quarter, span)
    near = min(4, chans // 2)
    keys = list(range(near))
    held = jnp.concatenate([held] + [swap(held, "chan", key) for key in keys[1:]], axis=0)
    flip = near
    while flip < chans // 2:
        held = jnp.concatenate([held, swap(held, "chan", flip)], axis=0)
        keys = keys + [key ^ flip for key in keys]
        flip *= 2
    other = swap(held, "chan", flip)
    if span == CHUNK:
        return (held, other), (tuple(keys), tuple(key ^ flip for key in keys))
    every = jnp.concatenate([held, other], axis=0)
    keys = jnp.asarray(keys + [key ^ flip for key in keys], jnp.int32)
    every = jnp.zeros_like(every).at[chan ^ keys].set(every)
    every = regroup(every)
    return (every,), ((None,) * every.shape[0],)


def shards(records, sources, dead_list):
    windows, groups, width, span = records.shape
    reps, chans = lax.axis_size("rep"), lax.axis_size("chan")
    cw = width * reps
    per = groups // chans
    blocks, keep, give, live, source_live, scale = pack(records, sources, dead_list, chans, reps)
    blocks = blocks.reshape(chans, windows * per * width, span)
    bins, inverse = bin_band()
    tables = [
        jnp.asarray(a) for a in (dft_table(chans * span), sample_band(), bins, inverse)
    ]
    arrived = regroup(lax.all_to_all(blocks, "chan", 0, 0, tiled=True))
    parts, keys = gather_sources(keep, give)
    spectra = channel_spectra(arrived, live, tables, windows)
    left = source_kernels(parts, keys, source_live, tables, windows)
    pieces, flips = [spectra], [0]
    flip = reps // 2
    while flip:
        pieces = pieces + [swap(piece, "rep", flip) for piece in pieces]
        flips = flips + [f ^ flip for f in flips]
        flip //= 2
    return correlate(pieces, flips, left, scale, cw)


def solution(mesh):
    placed = (P(None, None, "rep", "chan"), P(), P())
    return jax.shard_map(
        shards, mesh=mesh, in_specs=placed, out_specs=P("rep", None, "chan"), check_vma=False
    )
```

time: 42.1 us -> 43.7 us (1.038)
  waiting for transfers between devices: 14.6 us -> 16.4 us
  local copies, waits for them, and re-layouts: 3.97 us -> 4.72 us
  starting transfers between devices: 14.9 us -> 14.2 us
    all_to_all x1, waiting for transfers between devices: 0.01 us -> 5.63 us  [shards(): arrived = regroup(lax.all_to_all(blocks, 'chan', 0, 0, tiled=True))]
    ppermute x8 -> x9, waiting for transfers between devices: 14.6 us -> 10.8 us  [swap(): return lax.ppermute(x, axis, [(i, i ^ flip) for i in range(size)])]
    unnamed x25 -> x20, local copies, waits for them, and re-layouts: 3.84 us -> 4.71 us
    ppermute x8 -> x9, starting transfers between devices: 7.64 us -> 6.89 us  [swap(): return lax.ppermute(x, axis, [(i, i ^ flip) for i in range(size)])]
    pallas_call x3, Pallas kernels: 7.19 us -> 6.62 us  [the longest x1 3.11 us: correlate(): pl.pallas_call(functools.partial(correlate_kernel, flips, cw), grid=(quar...]
  transfers between devices with their start and end apart: 9 -> 10, of which waited for: 5 -> 5; matrix products, arithmetic and copies ran while one was open for 1% -> 0% of each run, Pallas kernels for 6% -> 8%
where the time goes in v2:
time: 43.7 us; the launch traced here: 43.4 us
  waiting for transfers between devices  16.4 us (38%)
  starting transfers between devices  14.2 us (32%)
  Pallas kernels  7.92 us (18%)
  local copies, waits for them, and re-layouts  4.72 us (11%)
    ppermute x9, waiting for transfers between devices, swap(): return lax.ppermute(x, axis, [(i, i ^ flip) for i in range(size)])  10.8 us
    all_to_all x1, starting transfers between devices, shards(): arrived = regroup(lax.all_to_all(blocks, 'chan', 0, 0, tiled=True))  7.29 us
    ppermute x9, starting transfers between devices, swap(): return lax.ppermute(x, axis, [(i, i ^ flip) for i in range(size)])  6.89 us
    all_to_all x1, waiting for transfers between devices, shards(): arrived = regroup(lax.all_to_all(blocks, 'chan', 0, 0, tiled=True))  5.63 us
    unnamed x20, local copies, waits for them, and re-layouts  4.71 us
    pallas_call x1, Pallas kernels, correlate(): pl.pallas_call(functools.partial(correlate_kernel, flips, cw), grid=(quar...  3.11 us
    pallas_call x1, Pallas kernels, source_kernels(): pl.pallas_call(functools.partial(source_kernel, keys, windows), out_shape...  2.21 us
    pallas_call x1, Pallas kernels, channel_spectra(): pl.pallas_call(channel_kernel, out_shape=jax.ShapeDtypeStruct((windows, r...  1.31 us
  transfers between devices with their start and end apart: 10, of which 5 were waited for; matrix products, arithmetic and copies ran while one was open for 0% of the time, Pallas kernels for 8%

profile of v2, /device:TPU:0, one launch (start us, length us, event | category | flops | bytes accessed | tf_op | source)
XLA Modules:
  0.0 43.4 jit_solution(15067600009212538044)
XLA Ops:
  0.0 0.0 copy-start.2
  0.0 0.0 copy-start.3
  0.0 1.1 %copy-done.3 = bf16[2,8,64,256]{3,2,1,0:T(8,128)(2,1)S(1)} copy-done((bf16[2,8,64,256]{3,2,1,0:T(8,128)(2,1)S(1)}, bf16[2,8,64,256]{3,2,1,0:T(8,128)(2,1)}, u32[]{:S(2)}) %copy-start.3) | copy-done | bytes 524312
  1.1 0.0 copy-start.8
  1.1 0.7 %copy-done.8 = s32[2,128]{1,0:T(2,128)S(1)} copy-done((s32[2,128]{1,0:T(2,128)S(1)}, s32[2,128]{1,0:T(2,128)}, u32[]{:S(2)}) %copy-start.8) | copy-done | bytes 1048
  1.8 0.0 copy-start.9
  1.8 0.7 %copy-done.9 = s32[128]{0:T(128)S(1)} copy-done((s32[128]{0:T(128)S(1)}, s32[128]{0:T(128)}, u32[]{:S(2)}) %copy-start.9) | copy-done | bytes 536
  2.4 0.0 copy-start.4
  2.4 1.3 %pack.1 = (bf16[8,2,1,64,256]{4,3,2,1,0:T(8,128)(2,1)}, bf16[2,2,32,256]{3,2,1,0:T(8,128)(2,1)S(1)}, bf16[2,2,32,256]{3,2,1,0:T(8,128)(2,1)S(1)}, f32[128,1]{1,0...) custom-call(bf16[2,8,64,256]{3,2,1,0:T(8,128)(2,1)S(1)} %copy-done.3, s32[1,128]{1,0:T(1,128)S(1)} %bitcast.3, ...), custom_call_target="tpu_custom_call" | custom-call | tf_op jit(solution)/shard_map/pack/pallas_call | solution.py:145
  3.7 7.3 %all-to-all-start = ((bf16[8,128,256]{2,1,0:T(8,128)(2,1)}), bf16[8,128,256]{2,1,0:T(8,128)(2,1)S(1)}, u32[]{:S(2)}, u32[]{:S(2)}) async-start(bf16[8,128,256]{2,1,0:T(8,128)(2,1)} %bitcast.1), calls=%async_computation | async-start | bytes 1048576 | tf_op jit(solution)/shard_map/all_to_all | solution.py:380
  11.0 0.0 copy-start.5
  11.0 0.0 copy-start.6
  11.0 0.1 collective-permute-start.3
  11.2 1.2 %collective-permute-done.3 = bf16[2,2,32,256]{3,2,1,0:T(8,128)(2,1)S(1)} collective-permute-done((bf16[2,2,32,256]{3,2,1,0:T(8,128)(2,1)S(1)}, bf16[2,2,32,256]{3,2,1,0:T(8,128)(2,1)S(1)}, u32[]{:S(2)}, u32[]{:S(2)}) %collective-permute-start.3) | collective-permute-done | bytes 65568 | tf_op jit(solution)/shard_map/ppermute | solution.py:326
  12.4 1.6 %collective-permute-start.4 = (bf16[1,2,32,256]{3,2,1,0:T(8,128)(2,1)S(1)}, bf16[1,2,32,256]{3,2,1,0:T(8,128)(2,1)S(1)}, u32[]{:S(2)}, u32[]{:S(2)}) collective-permute-start(bf16[1,2,32,256]{3,2,1,0:T(8,128)(2,1)S(1)} %constant_dynamic-slice_fusion), channel_id=1, source_target_pairs={{0,2},{1,3},{2,0},{3,1},{4,6},{5,7},{6,4},{7,5},{8,10},{9,11},{10,... | collective-permute-start | bytes 98312 | tf_op jit(solution)/shard_map/ppermute | solution.py:326
  14.0 2.4 %collective-permute-done.4 = bf16[1,2,32,256]{3,2,1,0:T(8,128)(2,1)S(1)} collective-permute-done((bf16[1,2,32,256]{3,2,1,0:T(8,128)(2,1)S(1)}, bf16[1,2,32,256]{3,2,1,0:T(8,128)(2,1)S(1)}, u32[]{:S(2)}, u32[]{:S(2)}) %collective-permute-start.4) | collective-permute-done | bytes 32800 | tf_op jit(solution)/shard_map/ppermute | solution.py:326
  16.4 2.8 %collective-permute-start.7 = (bf16[1,64,256]{2,1,0:T(8,128)(2,1)S(1)}, bf16[1,64,256]{2,1,0:T(8,128)(2,1)S(1)}, u32[]{:S(2)}, u32[]{:S(2)}) collective-permute-start(bf16[1,64,256]{2,1,0:T(8,128)(2,1)S(1)} %bitcast.4), channel_id=1, source_target_pairs={{0,12},{4,8},{8,4},{12,0},{16,28},{20,24},{24,20},{28,16},{1,13},{... | collective-permute-start | bytes 98312 | tf_op jit(solution)/shard_map/ppermute | solution.py:326
  19.2 0.6 %collective-permute-start.6 = (bf16[1,64,256]{2,1,0:T(8,128)(2,1)S(1)}, bf16[1,64,256]{2,1,0:T(8,128)(2,1)S(1)}, u32[]{:S(2)}, u32[]{:S(2)}) collective-permute-start(bf16[1,64,256]{2,1,0:T(8,128)(2,1)S(1)} %bitcast.5), channel_id=1, source_target_pairs={{0,8},{4,12},{8,0},{12,4},{16,24},{20,28},{24,16},{28,20},{1,9},{5... | collective-permute-start | bytes 98312 | tf_op jit(solution)/shard_map/ppermute | solution.py:326
  19.8 0.1 collective-permute-start.5
  19.9 5.6 %all-to-all-done.x_ref = bf16[8,128,256]{2,1,0:T(8,128)(2,1)S(1)} async-done(((bf16[8,128,256]{2,1,0:T(8,128)(2,1)}), bf16[8,128,256]{2,1,0:T(8,128)(2,1)S(1)}, u32[]{:S(2)}, u32[]{:S(2)}) %all-to-all-start) | async-done | bytes 524320 | tf_op jit(solution)/shard_map/all_to_all | solution.py:380
  25.5 0.0 copy-done.2
  25.5 0.0 copy-done.4
  25.5 0.0 copy-start
  25.5 1.6 %copy-done = bf16[2048,512]{1,0:T(8,128)(2,1)S(1)} copy-done((bf16[2048,512]{1,0:T(8,128)(2,1)S(1)}, bf16[2048,512]{1,0:T(8,128)(2,1)}, u32[]{:S(2)}) %copy-start) | copy-done | bytes 2097176
  27.1 0.0 copy-start.7
  27.1 0.7 %copy-done.7 = f32[1,256]{1,0:T(1,128)S(1)} copy-done((f32[1,256]{1,0:T(1,128)S(1)}, f32[1,256]{1,0:T(1,128)}, u32[]{:S(2)}) %copy-start.7) | copy-done | bytes 1048
  27.8 0.0 copy-start.1
  27.8 1.3 %channel_spectra.1.refs_0_ = bf16[2,64,512]{2,1,0:T(8,128)(2,1)S(1)} custom-call(bf16[8,128,256]{2,1,0:T(8,128)(2,1)S(1)} %all-to-all-done.x_ref, f32[128,1]{1,0:T(8,128)S(1)} %get-tuple-element.12.live_ref, bf16[2048,512]{1,0:T(8,128)(2,1)S(1)} %copy-done, bf16[512,256]{1,0:T(8,128)(2,1)S(1)} %copy-done.2, bf16[256,256]{1,0:T(8,128)(2,1)S(1)} %copy-done.4, ...), custom_call_target="tpu_custom_call" | custom-call | flops 536870912 | bytes 4194304 | tf_op jit(solution)/shard_map/channel_spectra/pallas_call | solution.py:214
  29.1 1.6 %collective-permute-start = (bf16[2,64,512]{2,1,0:T(8,128)(2,1)S(1)}, bf16[2,64,512]{2,1,0:T(8,128)(2,1)S(1)}, u32[]{:S(2)}, u32[]{:S(2)}) collective-permute-start(bf16[2,64,512]{2,1,0:T(8,128)(2,1)S(1)} %channel_spectra.1.refs_0_), channel_id=1, source_target_pairs={{0,2},{1,3},{2,0},{3,1},{4,6},{5,7},{6,4},{7,5},{8,10},{9,11},{10,... | collective-permute-start | bytes 393224 | tf_op jit(solution)/shard_map/ppermute | solution.py:326
  30.7 0.0 collective-permute-done.7
  30.7 0.0 collective-permute-done.6
  30.7 0.0 collective-permute-done.5
  30.7 0.2 collective-permute-start.8
  30.9 0.0 collective-permute-start.1
  30.9 3.2 %collective-permute-done.refs_1_ = bf16[2,64,512]{2,1,0:T(8,128)(2,1)S(1)} collective-permute-done((bf16[2,64,512]{2,1,0:T(8,128)(2,1)S(1)}, bf16[2,64,512]{2,1,0:T(8,128)(2,1)S(1)}, u32[]{:S(2)}, u32[]{:S(2)}) %collective-permute-start) | collective-permute-done | bytes 131104 | tf_op jit(solution)/shard_map/ppermute | solution.py:326
  34.1 0.0 collective-permute-start.2
  34.2 3.9 %collective-permute-done.8.refs_1_ = bf16[4,64,256]{2,1,0:T(8,128)(2,1)S(1)} collective-permute-done((bf16[4,64,256]{2,1,0:T(8,128)(2,1)S(1)}, bf16[4,64,256]{2,1,0:T(8,128)(2,1)S(1)}, u32[]{:S(2)}, u32[]{:S(2)}) %collective-permute-start.8) | collective-permute-done | bytes 131104 | tf_op jit(solution)/shard_map/ppermute | solution.py:326
  38.0 0.0 copy-done.5
  38.1 0.0 copy-done.6
  38.1 0.0 copy-done.1
  38.1 2.2 %source_kernels.1.refs_4_ = bf16[2048,1024]{1,0:T(8,128)(2,1)S(1)} custom-call(bf16[4,64,256]{2,1,0:T(8,128)(2,1)S(1)} %pad_maximum_fusion.refs_0_, bf16[4,64,256]{2,1,0:T(8,128)(2,1)S(1)} %collective-permute-done.8.refs_1_, f32[64,1]{1,0:T(8,128)S(1)} %get-tuple-element.15.refs_2_, f32[64,256]{1,0:T(8,128)S(1)} %copy-done.6, f32[64,256]{1,0:T(8,128)S(1)} %copy-done.5, ...), custom_call_target="tpu_custom_call" | custom-call | flops 268435456 | bytes 8388608 | tf_op jit(solution)/shard_map/source_kernels/pallas_call | solution.py:259
  40.3 0.0 collective-permute-done.1.refs_2_
  40.3 0.0 collective-permute-done.2.refs_3_
  40.3 3.1 %correlate.1 = f32[32,64,256]{2,1,0:T(8,128)} custom-call(bf16[2,64,512]{2,1,0:T(8,128)(2,1)S(1)} %channel_spectra.1.refs_0_, bf16[2,64,512]{2,1,0:T(8,128)(2,1)S(1)} %collective-permute-done.refs_1_, bf16[2,64,512]{2,1,0:T(8,128)(2,1)S(1)} %collective-permute-done.1.refs_2_, bf16[2,64,512]{2,1,0:T(8,128)(2,1)S(1)} %collective-permute-done.2.refs_3_, ...), custom_call_target="tpu_custom_call" | custom-call | tf_op jit(solution)/shard_map/correlate/pallas_call | solution.py:311
  (4 shorter events, 0.1 us)
Async XLA Ops:
  0.0 25.5 %copy-start.2 = (bf16[512,256]{1,0:T(8,128)(2,1)S(1)}, bf16[512,256]{1,0:T(8,128)(2,1)}, u32[]{:S(2)}) copy-start(bf16[512,256]{1,0:T(8,128)(2,1)} %constant.50.clone.band_ref.refs_6_) | copy-start | bytes 786436
  0.0 1.1 %copy-start.3 = (bf16[2,8,64,256]{3,2,1,0:T(8,128)(2,1)S(1)}, bf16[2,8,64,256]{3,2,1,0:T(8,128)(2,1)}, u32[]{:S(2)}) copy-start(bf16[2,8,64,256]{3,2,1,0:T(8,128)(2,1)} %rec_hbm.1) | copy-start | bytes 1572868
  1.1 0.7 %copy-start.8 = (s32[2,128]{1,0:T(2,128)S(1)}, s32[2,128]{1,0:T(2,128)}, u32[]{:S(2)}) copy-start(s32[2,128]{1,0:T(2,128)} %dead_hbm.1) | copy-start | bytes 3076
  1.8 0.7 %copy-start.9 = (s32[128]{0:T(128)S(1)}, s32[128]{0:T(128)}, u32[]{:S(2)}) copy-start(s32[128]{0:T(128)} %param.10) | copy-start | bytes 1540
  2.4 23.1 %copy-start.4 = (bf16[256,256]{1,0:T(8,128)(2,1)S(1)}, bf16[256,256]{1,0:T(8,128)(2,1)}, u32[]{:S(2)}) copy-start(bf16[256,256]{1,0:T(8,128)(2,1)} %constant.51.clone.bins_ref.refs_7_) | copy-start | bytes 393220
  3.7 21.8 %all-to-all-start = ((bf16[8,128,256]{2,1,0:T(8,128)(2,1)}), bf16[8,128,256]{2,1,0:T(8,128)(2,1)S(1)}, u32[]{:S(2)}, u32[]{:S(2)}) async-start(bf16[8,128,256]{2,1,0:T(8,128)(2,1)} %bitcast.1), calls=%async_computation | async-start | bytes 1048576 | tf_op jit(solution)/shard_map/all_to_all | solution.py:380
  11.0 27.0 %copy-start.5 = (f32[64,256]{1,0:T(8,128)S(1)}, f32[64,256]{1,0:T(8,128)}, u32[]{:S(2)}) copy-start(f32[64,256]{1,0:T(8,128)} %constant.54.clone.refs_4_) | copy-start | bytes 196612
  11.0 27.0 %copy-start.6 = (f32[64,256]{1,0:T(8,128)S(1)}, f32[64,256]{1,0:T(8,128)}, u32[]{:S(2)}) copy-start(f32[64,256]{1,0:T(8,128)} %constant.53.clone.refs_3_) | copy-start | bytes 196612
  11.0 1.3 %collective-permute-start.3 = (bf16[2,2,32,256]{3,2,1,0:T(8,128)(2,1)S(1)}, bf16[2,2,32,256]{3,2,1,0:T(8,128)(2,1)S(1)}, u32[]{:S(2)}, u32[]{:S(2)}) collective-permute-start(bf16[2,2,32,256]{3,2,1,0:T(8,128)(2,1)S(1)} %get-tuple-element.14), channel_id=1, source_target_pairs={{0,1},{1,0},{2,3},{3,2},{4,5},{5,4},{6,7},{7,6},{8,9},{9,8},{10,11... | collective-permute-start | bytes 196616 | tf_op jit(solution)/shard_map/ppermute | solution.py:326
  12.4 4.0 %collective-permute-start.4 = (bf16[1,2,32,256]{3,2,1,0:T(8,128)(2,1)S(1)}, bf16[1,2,32,256]{3,2,1,0:T(8,128)(2,1)S(1)}, u32[]{:S(2)}, u32[]{:S(2)}) collective-permute-start(bf16[1,2,32,256]{3,2,1,0:T(8,128)(2,1)S(1)} %constant_dynamic-slice_fusion), channel_id=1, source_target_pairs={{0,2},{1,3},{2,0},{3,1},{4,6},{5,7},{6,4},{7,5},{8,10},{9,11},{10,... | collective-permute-start | bytes 98312 | tf_op jit(solution)/shard_map/ppermute | solution.py:326
  16.4 14.3 %collective-permute-start.7 = (bf16[1,64,256]{2,1,0:T(8,128)(2,1)S(1)}, bf16[1,64,256]{2,1,0:T(8,128)(2,1)S(1)}, u32[]{:S(2)}, u32[]{:S(2)}) collective-permute-start(bf16[1,64,256]{2,1,0:T(8,128)(2,1)S(1)} %bitcast.4), channel_id=1, source_target_pairs={{0,12},{4,8},{8,4},{12,0},{16,28},{20,24},{24,20},{28,16},{1,13},{... | collective-permute-start | bytes 98312 | tf_op jit(solution)/shard_map/ppermute | solution.py:326
  19.2 11.4 %collective-permute-start.6 = (bf16[1,64,256]{2,1,0:T(8,128)(2,1)S(1)}, bf16[1,64,256]{2,1,0:T(8,128)(2,1)S(1)}, u32[]{:S(2)}, u32[]{:S(2)}) collective-permute-start(bf16[1,64,256]{2,1,0:T(8,128)(2,1)S(1)} %bitcast.5), channel_id=1, source_target_pairs={{0,8},{4,12},{8,0},{12,4},{16,24},{20,28},{24,16},{28,20},{1,9},{5... | collective-permute-start | bytes 98312 | tf_op jit(solution)/shard_map/ppermute | solution.py:326
  19.8 10.9 %collective-permute-start.5 = (bf16[1,64,256]{2,1,0:T(8,128)(2,1)S(1)}, bf16[1,64,256]{2,1,0:T(8,128)(2,1)S(1)}, u32[]{:S(2)}, u32[]{:S(2)}) collective-permute-start(bf16[1,64,256]{2,1,0:T(8,128)(2,1)S(1)} %bitcast.6), channel_id=1, source_target_pairs={{0,4},{4,0},{8,12},{12,8},{16,20},{20,16},{24,28},{28,24},{1,5},{5... | collective-permute-start | bytes 98312 | tf_op jit(solution)/shard_map/ppermute | solution.py:326
  25.5 1.6 %copy-start = (bf16[2048,512]{1,0:T(8,128)(2,1)S(1)}, bf16[2048,512]{1,0:T(8,128)(2,1)}, u32[]{:S(2)}) copy-start(bf16[2048,512]{1,0:T(8,128)(2,1)} %constant.49.clone.table_ref.refs_5_) | copy-start | bytes 6291460
  27.1 0.7 %copy-start.7 = (f32[1,256]{1,0:T(1,128)S(1)}, f32[1,256]{1,0:T(1,128)}, u32[]{:S(2)}) copy-start(f32[1,256]{1,0:T(1,128)} %constant.52.clone.inverse_ref.refs_8_) | copy-start | bytes 3076
  27.8 10.3 %copy-start.1 = (bf16[2048,512]{1,0:T(8,128)(2,1)S(1)}, bf16[2048,512]{1,0:T(8,128)(2,1)}, u32[]{:S(2)}) copy-start(bf16[2048,512]{1,0:T(8,128)(2,1)} %constant.49.clone.table_ref.refs_5_) | copy-start | bytes 6291460
  29.1 5.0 %collective-permute-start = (bf16[2,64,512]{2,1,0:T(8,128)(2,1)S(1)}, bf16[2,64,512]{2,1,0:T(8,128)(2,1)S(1)}, u32[]{:S(2)}, u32[]{:S(2)}) collective-permute-start(bf16[2,64,512]{2,1,0:T(8,128)(2,1)S(1)} %channel_spectra.1.refs_0_), channel_id=1, source_target_pairs={{0,2},{1,3},{2,0},{3,1},{4,6},{5,7},{6,4},{7,5},{8,10},{9,11},{10,... | collective-permute-start | bytes 393224 | tf_op jit(solution)/shard_map/ppermute | solution.py:326
  30.7 7.3 %collective-permute-start.8 = (bf16[4,64,256]{2,1,0:T(8,128)(2,1)S(1)}, bf16[4,64,256]{2,1,0:T(8,128)(2,1)S(1)}, u32[]{:S(2)}, u32[]{:S(2)}) collective-permute-start(bf16[4,64,256]{2,1,0:T(8,128)(2,1)S(1)} %pad_maximum_fusion.refs_0_), channel_id=1, source_target_pairs={{0,16},{4,20},{8,24},{12,28},{16,0},{20,4},{24,8},{28,12},{1,17},{... | collective-permute-start | bytes 393224 | tf_op jit(solution)/shard_map/ppermute | solution.py:326
  30.9 9.3 %collective-permute-start.1 = (bf16[2,64,512]{2,1,0:T(8,128)(2,1)S(1)}, bf16[2,64,512]{2,1,0:T(8,128)(2,1)S(1)}, u32[]{:S(2)}, u32[]{:S(2)}) collective-permute-start(bf16[2,64,512]{2,1,0:T(8,128)(2,1)S(1)} %channel_spectra.1.refs_0_), channel_id=1, source_target_pairs={{0,1},{1,0},{2,3},{3,2},{4,5},{5,4},{6,7},{7,6},{8,9},{9,8},{10,11... | collective-permute-start | bytes 393224 | tf_op jit(solution)/shard_map/ppermute | solution.py:326
  34.1 6.1 %collective-permute-start.2 = (bf16[2,64,512]{2,1,0:T(8,128)(2,1)S(1)}, bf16[2,64,512]{2,1,0:T(8,128)(2,1)S(1)}, u32[]{:S(2)}, u32[]{:S(2)}) collective-permute-start(bf16[2,64,512]{2,1,0:T(8,128)(2,1)S(1)} %collective-permute-done.refs_1_), channel_id=1, source_target_pairs={{0,1},{1,0},{2,3},{3,2},{4,5},{5,4},{6,7},{7,6},{8,9},{9,8},{10,11... | collective-permute-start | bytes 393224 | tf_op jit(solution)/shard_map/ppermute | solution.py:326

commit v3 on v2

--- a/solution.py
+++ b/solution.py
@@ -20,7 +20,9 @@
 CHUNK = 256
 EDGE = 128
 VMEM = pl.BlockSpec(memory_space=pltpu.VMEM)
-LIMIT = 40 * 1024 * 1024
+LIMIT = 16 * 1024 * 1024
+WHOLE = 60 * 1024 * 1024
+HBM = pl.BlockSpec(memory_space=pltpu.HBM)
 
 
 def dft_table(length):
@@ -47,9 +49,7 @@
 def bin_band():
     row = np.arange(K)[:, None]
     column = np.arange(K)[None, :]
-    band = np.abs(row - column) <= WH
-    inverse = 1.0 / band.sum(axis=0, keepdims=True)
-    return band.astype(np.float32).astype(jnp.bfloat16), inverse.astype(np.float32)
+    return (np.abs(row - column) <= WH).astype(np.float32).astype(jnp.bfloat16)
 
 
 def iota(shape, dim):
@@ -75,9 +75,10 @@
 
 def pack_kernel(
     cw, rec_hbm, src_hbm, dead_hbm,
-    out_ref, keep_ref, give_ref, live_ref, source_live_ref, scale_ref,
-    rec_ref, src_ref, dead_ref, pick_ref, sem,
+    out_ref, *refs,
 ):
+    part_refs = refs[:-8]
+    live_ref, source_live_ref, scale_ref, rec_ref, src_ref, dead_ref, pick_ref, sem = refs[-8:]
     copies = [
         pltpu.make_async_copy(src_hbm, src_ref, sem.at[0]),
         pltpu.make_async_copy(dead_hbm, dead_ref, sem.at[1]),
@@ -86,9 +87,9 @@
     for copy in copies:
         copy.start()
     windows, groups, width, span = rec_ref.shape
+    per = groups // out_ref.shape[0]
     reps = cw // width
     rep, chan = lax.axis_index("rep"), lax.axis_index("chan")
-    per = groups // out_ref.shape[0]
     count = src_ref.shape[1]
     quarter = count // reps
     here = pl.ds(pl.multiple_of(rep * quarter, quarter), quarter)
@@ -130,30 +131,27 @@
     for w in range(windows):
         rows = rec_ref[w].reshape(local, span)
         pick_ref[...] = jnp.dot(onehot, rows, preferred_element_type=jnp.float32)
-        for half in range(reps // 2):
-            for ref, bit in ((keep_ref, rep % 2), (give_ref, 1 - rep % 2)):
-                first = pl.multiple_of((2 * half + bit) * quarter, quarter)
-                ref[half, w] = pick_ref[pl.ds(first, quarter), :].astype(jnp.bfloat16)
+        for flip, ref in enumerate(part_refs):
+            first = pl.multiple_of((rep ^ flip) * quarter, quarter)
+            ref[w] = pick_ref[pl.ds(first, quarter), :].astype(jnp.bfloat16)
 
 
 def pack(records, sources, dead_list, chans, reps):
     windows, groups, width, span = records.shape
     count = sources.shape[0]
     per = groups // chans
-    part = (reps // 2, windows, count // reps, span)
-    anywhere = pl.BlockSpec(memory_space=pl.ANY)
+    part = jax.ShapeDtypeStruct((windows, count // reps, span), jnp.bfloat16)
     return pl.pallas_call(
         functools.partial(pack_kernel, width * reps),
         out_shape=(
             jax.ShapeDtypeStruct((chans, windows, per, width, span), jnp.bfloat16),
-            jax.ShapeDtypeStruct(part, jnp.bfloat16),
-            jax.ShapeDtypeStruct(part, jnp.bfloat16),
+            *[part] * reps,
             jax.ShapeDtypeStruct((windows * per * width, 1), jnp.float32),
             jax.ShapeDtypeStruct((windows * count // reps, 1), jnp.float32),
             jax.ShapeDtypeStruct((count // reps, per * width * reps), jnp.float32),
         ),
-        in_specs=[anywhere] * 3,
-        out_specs=(VMEM,) * 6,
+        in_specs=[HBM] * 3,
+        out_specs=(VMEM,) * (reps + 4),
         scratch_shapes=[
             pltpu.VMEM(records.shape, jnp.bfloat16),
             pltpu.VMEM((1, count), jnp.int32),
@@ -161,12 +159,12 @@
             pltpu.VMEM((count, span), jnp.float32),
             pltpu.SemaphoreType.DMA((3,)),
         ],
-        compiler_params=pltpu.CompilerParams(vmem_limit_bytes=LIMIT),
+        compiler_params=pltpu.CompilerParams(vmem_limit_bytes=WHOLE),
         name="pack",
     )(records, sources.reshape(1, count), dead_list)
 
 
-def whiten_rows(x_ref, ext_ref, table_ref, band_ref, bins_ref, inverse_ref):
+def whiten_rows(x_ref, ext_ref, table_ref, band_ref, bins_ref):
     pieces, rows, _ = x_ref.shape
     length = pieces * CHUNK
     for i in range(pieces):
@@ -195,14 +193,18 @@
     low = (rest - middle.astype(jnp.float32)).astype(jnp.bfloat16)
     stacked = jnp.concatenate([high, middle, low], axis=0)
     sums = jnp.dot(stacked, bins_ref[...], preferred_element_type=jnp.float32)
-    smooth = (sums[:rows] + sums[rows : 2 * rows] + sums[2 * rows :]) * inverse_ref[...]
+    place = iota((1, K), 1)
+    width = jnp.minimum(place, WH) + jnp.minimum(K - 1 - place, WH) + 1
+    smooth = (sums[:rows] + sums[rows : 2 * rows] + sums[2 * rows :]) * (
+        1.0 / width.astype(jnp.float32)
+    )
     scale = 1.0 / (smooth + EPS)
     return real_part * scale, imag_part * scale
 
 
-def channel_kernel(x_ref, live_ref, table_ref, band_ref, bins_ref, inverse_ref, out_ref, ext_ref):
+def channel_kernel(x_ref, live_ref, table_ref, band_ref, bins_ref, out_ref, ext_ref):
     windows, count, _ = out_ref.shape
-    real_part, imag_part = whiten_rows(x_ref, ext_ref, table_ref, band_ref, bins_ref, inverse_ref)
+    real_part, imag_part = whiten_rows(x_ref, ext_ref, table_ref, band_ref, bins_ref)
     for w in range(windows):
         here = slice(w * count, (w + 1) * count)
         out_ref[w, :, :K] = (real_part[here] * live_ref[here, :]).astype(jnp.bfloat16)
@@ -214,12 +216,12 @@
     return pl.pallas_call(
         channel_kernel,
         out_shape=jax.ShapeDtypeStruct((windows, rows // windows, 2 * K), jnp.bfloat16),
-        in_specs=[VMEM] * 6,
+        in_specs=[VMEM] * 5,
         out_specs=VMEM,
         scratch_shapes=[pltpu.VMEM((pieces * rows, CHUNK + 2 * EDGE), jnp.bfloat16)],
         compiler_params=pltpu.CompilerParams(vmem_limit_bytes=LIMIT),
         cost_estimate=pl.CostEstimate(
-            flops=2 * rows * 2048 * 1024, bytes_accessed=4 << 20, transcendentals=0
+            flops=1, bytes_accessed=1, transcendentals=0
         ),
         name="channel_spectra",
     )(x, live, *tables)
@@ -227,13 +229,13 @@
 
 def source_kernel(keys, windows, *refs):
     parts = refs[: len(keys)]
-    live_ref, cos_ref, sin_ref, table_ref, band_ref, bins_ref, inverse_ref = refs[len(keys) : -3]
+    live_ref, cos_ref, sin_ref, table_ref, band_ref, bins_ref = refs[len(keys) : -3]
     out_ref, x_ref, ext_ref = refs[-3:]
     chan = lax.axis_index("chan")
     for part, slots in zip(parts, keys):
         for n, key in enumerate(slots):
             x_ref[chan ^ key if key is not None else n] = part[n]
-    real_part, imag_part = whiten_rows(x_ref, ext_ref, table_ref, band_ref, bins_ref, inverse_ref)
+    real_part, imag_part = whiten_rows(x_ref, ext_ref, table_ref, band_ref, bins_ref)
     real_part = (real_part * live_ref[...]).astype(jnp.bfloat16).astype(jnp.float32)
     imag_part = (imag_part * live_ref[...]).astype(jnp.bfloat16).astype(jnp.float32)
     quarter = real_part.shape[0] // windows
@@ -259,7 +261,7 @@
     return pl.pallas_call(
         functools.partial(source_kernel, keys, windows),
         out_shape=jax.ShapeDtypeStruct((rows // windows * LAGS, windows * 2 * K), jnp.bfloat16),
-        in_specs=[VMEM] * (len(parts) + 7),
+        in_specs=[VMEM] * (len(parts) + 6),
         out_specs=VMEM,
         scratch_shapes=[
             pltpu.VMEM((pieces, rows, CHUNK), jnp.bfloat16),
@@ -267,7 +269,7 @@
         ],
         compiler_params=pltpu.CompilerParams(vmem_limit_bytes=LIMIT),
         cost_estimate=pl.CostEstimate(
-            flops=2 * rows * 2048 * 1024, bytes_accessed=8 << 20, transcendentals=0
+            flops=1 << 34, bytes_accessed=8 << 20, transcendentals=0
         ),
         name="source_kernels",
     )(*parts, live, jnp.asarray(cosine), jnp.asarray(sine), *tables)
@@ -275,50 +277,75 @@
 
 def correlate_kernel(flips, cw, *refs):
     parts = refs[: len(flips)]
-    left_ref, scale_ref, out_ref, right_ref = refs[len(flips) :]
+    left_ref, scale_ref, out_hbm, right_ref, out_ref, sem = refs[len(flips) :]
     windows, count, features = parts[0].shape
-    batch, lags, columns = out_ref.shape
+    steps, batch, lags, columns = out_ref.shape
     per = columns // cw
     width = count // per
-
-    @pl.when(pl.program_id(0) == 0)
-    def _():
-        rep = lax.axis_index("rep")
-        for part, flip in zip(parts, flips):
-            for w in range(windows):
-                for g in range(per):
-                    first = pl.multiple_of(g * cw + (rep ^ flip) * width, width)
-                    right_ref[pl.ds(first, width), pl.ds(w * features, features)] = part[
-                        w, pl.ds(g * width, width), :
-                    ]
-
-    summed = lax.dot_general(
-        left_ref[...], right_ref[...], (((1,), (1,)), ((), ())), preferred_element_type=jnp.float32
-    )
-    for n in range(batch):
-        scale = scale_ref[pl.ds(pl.program_id(0) * batch + n, 1), :]
-        out_ref[n] = summed[n * lags : (n + 1) * lags] * scale
+    rep = lax.axis_index("rep")
+    for part, flip in zip(parts, flips):
+        for w in range(windows):
+            for g in range(per):
+                first = pl.multiple_of(g * cw + (rep ^ flip) * width, width)
+                right_ref[pl.ds(first, width), pl.ds(w * features, features)] = part[
+                    w, pl.ds(g * width, width), :
+                ]
+    copies = []
+    for i in range(steps):
+        summed = lax.dot_general(
+            left_ref[i * batch * lags : (i + 1) * batch * lags, :],
+            right_ref[...],
+            (((1,), (1,)), ((), ())),
+            preferred_element_type=jnp.float32,
+        )
+        for n in range(batch):
+            s = i * batch + n
+            out_ref[i, n] = summed[n * lags : (n + 1) * lags] * scale_ref[s : s + 1, :]
+        copies.append(
+            pltpu.make_async_copy(
+                out_ref.at[i], out_hbm.at[pl.ds(i * batch, batch)], sem.at[i]
+            )
+        )
+        copies[-1].start()
+    for copy in copies:
+        copy.wait()
 
 
 def correlate(parts, flips, left, scale, cw):
     quarter, columns = scale.shape
-    batch = 8
-
-    def whole(array):
-        rank = array.ndim
-        return pl.BlockSpec(array.shape, lambda i: (0,) * rank)
-
+    steps = 4
     return pl.pallas_call(
         functools.partial(correlate_kernel, flips, cw),
-        grid=(quarter // batch,),
         out_shape=jax.ShapeDtypeStruct((quarter, LAGS, columns), jnp.float32),
-        in_specs=[whole(part) for part in parts]
-        + [pl.BlockSpec((batch * LAGS, left.shape[1]), lambda i: (i, 0)), whole(scale)],
-        out_specs=pl.BlockSpec((batch, LAGS, columns), lambda i: (i, 0, 0)),
-        scratch_shapes=[pltpu.VMEM((columns, left.shape[1]), jnp.bfloat16)],
+        in_specs=[VMEM] * (len(parts) + 2),
+        out_specs=HBM,
+        scratch_shapes=[
+            pltpu.VMEM((columns, left.shape[1]), jnp.bfloat16),
+            pltpu.VMEM((steps, quarter // steps, LAGS, columns), jnp.float32),
+            pltpu.SemaphoreType.DMA((steps,)),
+        ],
         compiler_params=pltpu.CompilerParams(vmem_limit_bytes=LIMIT),
         name="correlate",
     )(*parts, left, scale)
+
+
+def stage_kernel(table_hbm, after_hbm, out_ref, sem):
+    copy = pltpu.make_async_copy(table_hbm, out_ref, sem)
+    copy.start()
+    copy.wait()
+
+
+def stage(table, after):
+    return pl.pallas_call(
+        stage_kernel,
+        out_shape=jax.ShapeDtypeStruct(table.shape, table.dtype),
+        in_specs=[HBM, pl.BlockSpec(memory_space=pl.ANY)],
+        out_specs=VMEM,
+        scratch_shapes=[pltpu.SemaphoreType.DMA(())],
+        compiler_params=pltpu.CompilerParams(vmem_limit_bytes=LIMIT),
+        cost_estimate=pl.CostEstimate(flops=1, bytes_accessed=4 << 20, transcendentals=0),
+        name="stage",
+    )(table, after)
 
 
 def swap(x, axis, flip):
@@ -334,19 +361,13 @@
     return jnp.transpose(joined, (1, 0, 2))
 
 
-def gather_sources(keep, give):
-    reps, chans = lax.axis_size("rep"), lax.axis_size("chan")
-    rep, chan = lax.axis_index("rep"), lax.axis_index("chan")
-    _, windows, quarter, span = keep.shape
-    mine = keep + swap(give, "rep", 1)
-    flip = 2
-    while flip < reps:
-        pairs = mine.reshape((-1, 2) + mine.shape[1:])
-        bit = (rep // flip) % 2
-        kept = lax.dynamic_index_in_dim(pairs, bit, 1, keepdims=False)
-        given = lax.dynamic_index_in_dim(pairs, 1 - bit, 1, keepdims=False)
-        mine = kept + swap(given, "rep", flip)
-        flip *= 2
+def gather_sources(given, table):
+    chans, chan = lax.axis_size("chan"), lax.axis_index("chan")
+    windows, quarter, span = given[0].shape
+    mine = given[0]
+    for other in [swap(part, "rep", flip) for flip, part in enumerate(given) if flip]:
+        mine = mine + other
+    table = stage(table, mine)
     held = mine.reshape(1, windows * quarter, span)
     near = min(4, chans // 2)
     keys = list(range(near))
@@ -356,14 +377,15 @@
         held = jnp.concatenate([held, swap(held, "chan", flip)], axis=0)
         keys = keys + [key ^ flip for key in keys]
         flip *= 2
+    held, table = lax.optimization_barrier((held, table))
     other = swap(held, "chan", flip)
     if span == CHUNK:
-        return (held, other), (tuple(keys), tuple(key ^ flip for key in keys))
+        return table, (held, other), (tuple(keys), tuple(key ^ flip for key in keys))
     every = jnp.concatenate([held, other], axis=0)
     keys = jnp.asarray(keys + [key ^ flip for key in keys], jnp.int32)
     every = jnp.zeros_like(every).at[chan ^ keys].set(every)
     every = regroup(every)
-    return (every,), ((None,) * every.shape[0],)
+    return table, (every,), ((None,) * every.shape[0],)
 
 
 def shards(records, sources, dead_list):
@@ -371,20 +393,20 @@
     reps, chans = lax.axis_size("rep"), lax.axis_size("chan")
     cw = width * reps
     per = groups // chans
-    blocks, keep, give, live, source_live, scale = pack(records, sources, dead_list, chans, reps)
+    blocks, *given, live, source_live, scale = pack(records, sources, dead_list, chans, reps)
     blocks = blocks.reshape(chans, windows * per * width, span)
-    bins, inverse = bin_band()
-    tables = [
-        jnp.asarray(a) for a in (dft_table(chans * span), sample_band(), bins, inverse)
-    ]
     arrived = regroup(lax.all_to_all(blocks, "chan", 0, 0, tiled=True))
-    parts, keys = gather_sources(keep, give)
+    table, parts, keys = gather_sources(given, jnp.asarray(dft_table(chans * span)))
+    tables = [table, jnp.asarray(sample_band()), jnp.asarray(bin_band())]
     spectra = channel_spectra(arrived, live, tables, windows)
     left = source_kernels(parts, keys, source_live, tables, windows)
     pieces, flips = [spectra], [0]
     flip = reps // 2
     while flip:
-        pieces = pieces + [swap(piece, "rep", flip) for piece in pieces]
+        others = [swap(piece, "rep", flip) for piece in pieces]
+        if flip > 1:
+            others, left = lax.optimization_barrier((others, left))
+        pieces = pieces + others
         flips = flips + [f ^ flip for f in flips]
         flip //= 2
     return correlate(pieces, flips, left, scale, cw)

time: 43.7 us -> 37.6 us (0.86)
  waiting for transfers between devices: 16.4 us -> 9.79 us
  local copies, waits for them, and re-layouts: 4.72 us -> 1.62 us
  starting transfers between devices: 14.2 us -> 16.9 us
  other arithmetic: 0.04 us -> 0.83 us
    all_to_all x1, waiting for transfers between devices: 5.63 us -> 0.01 us  [shards(): arrived = regroup(lax.all_to_all(blocks, 'chan', 0, 0, tiled=True))]
    unnamed x20 -> x16, local copies, waits for them, and re-layouts: 4.71 us -> 1.62 us
    ppermute x9 -> x10, starting transfers between devices: 6.89 us -> 9.62 us  [swap(): return lax.ppermute(x, axis, [(i, i ^ flip) for i in range(size)])]
    ppermute x9 -> x10, waiting for transfers between devices: 10.8 us -> 9.79 us  [swap(): return lax.ppermute(x, axis, [(i, i ^ flip) for i in range(size)])]
    add x2 -> x1, other arithmetic: 0.02 us -> 0.81 us  [gather_sources(): mine = mine + other]
    pallas_call x1, Pallas kernels: 1.3 us -> 2.03 us  [pack(): pl.pallas_call(functools.partial(pack_kernel, width * reps), out_shape=(j...]
    pallas_call x1 -> x2, Pallas kernels: 3.11 us -> 2.54 us  [the longest x1 2.39 us: correlate(): pl.pallas_call(functools.partial(correlate_kernel, flips, cw), out_shape=...]
  transfers between devices with their start and end apart: 10 -> 11, of which waited for: 5 -> 8; matrix products, arithmetic and copies ran while one was open for 0% -> 2% of each run, Pallas kernels for 8% -> 10%
where the time goes in v3:
time: 37.6 us; the launch traced here: 37.3 us
  starting transfers between devices  16.9 us (45%)
  waiting for transfers between devices  9.79 us (26%)
  Pallas kernels  8.08 us (21%)
  local copies, waits for them, and re-layouts  1.62 us (4%)
  other arithmetic  0.83 us (2%)
    ppermute x10, waiting for transfers between devices, swap(): return lax.ppermute(x, axis, [(i, i ^ flip) for i in range(size)])  9.79 us
    ppermute x10, starting transfers between devices, swap(): return lax.ppermute(x, axis, [(i, i ^ flip) for i in range(size)])  9.62 us
    all_to_all x1, starting transfers between devices, shards(): arrived = regroup(lax.all_to_all(blocks, 'chan', 0, 0, tiled=True))  7.29 us
    pallas_call x1, Pallas kernels, correlate(): pl.pallas_call(functools.partial(correlate_kernel, flips, cw), out_shape=...  2.39 us
    pallas_call x1, Pallas kernels, source_kernels(): pl.pallas_call(functools.partial(source_kernel, keys, windows), out_shape...  2.2 us
    pallas_call x1, Pallas kernels, pack(): pl.pallas_call(functools.partial(pack_kernel, width * reps), out_shape=(j...  2.03 us
    unnamed x16, local copies, waits for them, and re-layouts  1.62 us
    pallas_call x1, Pallas kernels, channel_spectra(): pl.pallas_call(channel_kernel, out_shape=jax.ShapeDtypeStruct((windows, r...  1.31 us
  transfers between devices with their start and end apart: 11, of which 8 were waited for; matrix products, arithmetic and copies ran while one was open for 2% of the time, Pallas kernels for 10%

profile of v3, /device:TPU:0, one launch (start us, length us, event | category | flops | bytes accessed | tf_op | source)
XLA Modules:
  0.0 37.3 jit_solution(5702889571920376013)
XLA Ops:
  0.0 2.0 %pack.1 = (bf16[8,2,1,64,256]{4,3,2,1,0:T(8,128)(2,1)}, bf16[2,32,256]{2,1,0:T(8,128)(2,1)}, bf16[2,32,256]{2,1,0:T(8,128)(2,1)}, bf16[2,32,256]{2,1,0:T(8,128)(...) custom-call(bf16[2,8,64,256]{3,2,1,0:T(8,128)(2,1)} %rec_hbm.1, ...), custom_call_target="tpu_custom_call" | custom-call | tf_op jit(solution)/shard_map/pack/pallas_call | solution.py:144
  2.0 7.3 %all-to-all-start = ((bf16[8,128,256]{2,1,0:T(8,128)(2,1)}), bf16[8,128,256]{2,1,0:T(8,128)(2,1)S(1)}, u32[]{:S(2)}, u32[]{:S(2)}) async-start(bf16[8,128,256]{2,1,0:T(8,128)(2,1)} %bitcast.7), calls=%async_computation | async-start | bytes 1048576 | tf_op jit(solution)/shard_map/all_to_all | solution.py:398
  9.3 0.7 %collective-permute-start.2 = (bf16[2,32,256]{2,1,0:T(8,128)(2,1)}, bf16[2,32,256]{2,1,0:T(8,128)(2,1)S(1)}, u32[]{:S(2)}, u32[]{:S(2)}) collective-permute-start(bf16[2,32,256]{2,1,0:T(8,128)(2,1)} %get-tuple-element.22), channel_id=1, source_target_pairs={{0,3},{1,2},{2,1},{3,0},{4,7},{5,6},{6,5},{7,4},{8,11},{9,10},{10,... | collective-permute-start | bytes 98312 | tf_op jit(solution)/shard_map/ppermute | solution.py:353
  10.0 0.9 %collective-permute-start.1 = (bf16[2,32,256]{2,1,0:T(8,128)(2,1)}, bf16[2,32,256]{2,1,0:T(8,128)(2,1)S(1)}, u32[]{:S(2)}, u32[]{:S(2)}) collective-permute-start(bf16[2,32,256]{2,1,0:T(8,128)(2,1)} %get-tuple-element.21), channel_id=1, source_target_pairs={{0,2},{1,3},{2,0},{3,1},{4,6},{5,7},{6,4},{7,5},{8,10},{9,11},{10,... | collective-permute-start | bytes 98312 | tf_op jit(solution)/shard_map/ppermute | solution.py:353
  10.9 0.3 collective-permute-start
  11.2 2.0 %collective-permute-done.2 = bf16[2,32,256]{2,1,0:T(8,128)(2,1)S(1)} collective-permute-done((bf16[2,32,256]{2,1,0:T(8,128)(2,1)}, bf16[2,32,256]{2,1,0:T(8,128)(2,1)S(1)}, u32[]{:S(2)}, u32[]{:S(2)}) %collective-permute-start.2) | collective-permute-done | bytes 32800 | tf_op jit(solution)/shard_map/ppermute | solution.py:353
  13.2 1.3 %collective-permute-done.1 = bf16[2,32,256]{2,1,0:T(8,128)(2,1)S(1)} collective-permute-done((bf16[2,32,256]{2,1,0:T(8,128)(2,1)}, bf16[2,32,256]{2,1,0:T(8,128)(2,1)S(1)}, u32[]{:S(2)}, u32[]{:S(2)}) %collective-permute-start.1) | collective-permute-done | bytes 32800 | tf_op jit(solution)/shard_map/ppermute | solution.py:353
  14.5 0.0 collective-permute-done
  14.5 0.0 copy-start.2
  14.5 0.8 %add_add_fusion.after_hbm = bf16[2,32,256]{2,1,0:T(8,128)(2,1)S(1)} fusion(bf16[2,32,256]{2,1,0:T(8,128)(2,1)S(1)} %collective-permute-done.2, bf16[2,32,256]{2,1,0:T(8,128)(2,1)S(1)} %collective-permute-done.1, bf16[2,32,256]{2,1,0:T(8,128)(2,1)} %get-tuple-element.19, bf16[2,32,256]{2,1,0:T(8,128)(2,1)S(1)} %collective-permute-done), kind=kLoop, calls=%fused_computation.1 | loop fusion | flops 49152 | bytes 163840 | tf_op jit(solution)/shard_map/add | solution.py:369
  15.3 2.5 %collective-permute-start.5 = (bf16[1,64,256]{2,1,0:T(8,128)(2,1)S(1)}, bf16[1,64,256]{2,1,0:T(8,128)(2,1)S(1)}, u32[]{:S(2)}, u32[]{:S(2)}) collective-permute-start(bf16[1,64,256]{2,1,0:T(8,128)(2,1)S(1)} %bitcast.3), channel_id=1, source_target_pairs={{0,12},{4,8},{8,4},{12,0},{16,28},{20,24},{24,20},{28,16},{1,13},{... | collective-permute-start | bytes 98312 | tf_op jit(solution)/shard_map/ppermute | solution.py:353
  17.7 0.6 %collective-permute-start.4 = (bf16[1,64,256]{2,1,0:T(8,128)(2,1)S(1)}, bf16[1,64,256]{2,1,0:T(8,128)(2,1)S(1)}, u32[]{:S(2)}, u32[]{:S(2)}) collective-permute-start(bf16[1,64,256]{2,1,0:T(8,128)(2,1)S(1)} %bitcast.4), channel_id=1, source_target_pairs={{0,8},{4,12},{8,0},{12,4},{16,24},{20,28},{24,16},{28,20},{1,9},{5... | collective-permute-start | bytes 98312 | tf_op jit(solution)/shard_map/ppermute | solution.py:353
  18.3 0.5 %collective-permute-start.3 = (bf16[1,64,256]{2,1,0:T(8,128)(2,1)S(1)}, bf16[1,64,256]{2,1,0:T(8,128)(2,1)S(1)}, u32[]{:S(2)}, u32[]{:S(2)}) collective-permute-start(bf16[1,64,256]{2,1,0:T(8,128)(2,1)S(1)} %bitcast.5), channel_id=1, source_target_pairs={{0,4},{4,0},{8,12},{12,8},{16,20},{20,16},{24,28},{28,24},{1,5},{5... | collective-permute-start | bytes 98312 | tf_op jit(solution)/shard_map/ppermute | solution.py:353
  18.8 0.0 copy-start
  18.8 1.6 %copy-done = bf16[2048,512]{1,0:T(8,128)(2,1)S(1)} copy-done((bf16[2048,512]{1,0:T(8,128)(2,1)S(1)}, bf16[2048,512]{1,0:T(8,128)(2,1)}, u32[]{:S(2)}) %copy-start) | copy-done | bytes 2097176
  20.4 0.0 copy-start.1
  20.4 0.0 copy-start.3
  20.4 0.1 stage.1.table_ref.refs_5_
  20.6 0.0 copy-start.5
  20.6 0.0 copy-start.6
  20.6 0.0 copy-start.7
  20.6 0.5 %collective-permute-done.5 = bf16[1,64,256]{2,1,0:T(8,128)(2,1)S(1)} collective-permute-done((bf16[1,64,256]{2,1,0:T(8,128)(2,1)S(1)}, bf16[1,64,256]{2,1,0:T(8,128)(2,1)S(1)}, u32[]{:S(2)}, u32[]{:S(2)}) %collective-permute-start.5) | collective-permute-done | bytes 32800 | tf_op jit(solution)/shard_map/ppermute | solution.py:353
  21.2 0.6 %collective-permute-done.4 = bf16[1,64,256]{2,1,0:T(8,128)(2,1)S(1)} collective-permute-done((bf16[1,64,256]{2,1,0:T(8,128)(2,1)S(1)}, bf16[1,64,256]{2,1,0:T(8,128)(2,1)S(1)}, u32[]{:S(2)}, u32[]{:S(2)}) %collective-permute-start.4) | collective-permute-done | bytes 32800 | tf_op jit(solution)/shard_map/ppermute | solution.py:353
  21.8 0.9 %collective-permute-done.3 = bf16[1,64,256]{2,1,0:T(8,128)(2,1)S(1)} collective-permute-done((bf16[1,64,256]{2,1,0:T(8,128)(2,1)S(1)}, bf16[1,64,256]{2,1,0:T(8,128)(2,1)S(1)}, u32[]{:S(2)}, u32[]{:S(2)}) %collective-permute-start.3) | collective-permute-done | bytes 32800 | tf_op jit(solution)/shard_map/ppermute | solution.py:353
  22.7 2.2 %collective-permute-start.7 = (bf16[4,64,256]{2,1,0:T(8,128)(2,1)S(1)}, bf16[4,64,256]{2,1,0:T(8,128)(2,1)S(1)}, u32[]{:S(2)}, u32[]{:S(2)}) collective-permute-start(bf16[4,64,256]{2,1,0:T(8,128)(2,1)S(1)} %pad_maximum_fusion.refs_0_), channel_id=1, source_target_pairs={{0,16},{4,20},{8,24},{12,28},{16,0},{20,4},{24,8},{28,12},{1,17},{... | collective-permute-start | bytes 393224 | tf_op jit(solution)/shard_map/ppermute | solution.py:353
  25.0 0.0 all-to-all-done.x_ref
  25.0 0.0 copy-done.2
  25.0 0.0 copy-done.1
  25.0 0.0 copy-done.3
  25.0 1.3 %channel_spectra.1.refs_0_ = bf16[2,64,512]{2,1,0:T(8,128)(2,1)S(1)} custom-call(bf16[8,128,256]{2,1,0:T(8,128)(2,1)S(1)} %all-to-all-done.x_ref, f32[128,1]{1,0:T(8,128)S(1)} %copy-done.3, bf16[2048,512]{1,0:T(8,128)(2,1)S(1)} %stage.1.table_ref.refs_5_, bf16[512,256]{1,0:T(8,128)(2,1)S(1)} %copy-done.1, bf16[256,256]{1,0:T(8,128)(2,1)S(1)} %copy-done.2), custom_call_target="tpu_custom_call" | custom-call | flops 1 | bytes 1 | tf_op jit(solution)/shard_map/channel_spectra/pallas_call | solution.py:216
  26.3 1.4 %collective-permute-start.6 = (bf16[2,64,512]{2,1,0:T(8,128)(2,1)S(1)}, bf16[2,64,512]{2,1,0:T(8,128)(2,1)S(1)}, u32[]{:S(2)}, u32[]{:S(2)}) collective-permute-start(bf16[2,64,512]{2,1,0:T(8,128)(2,1)S(1)} %channel_spectra.1.refs_0_), channel_id=1, source_target_pairs={{0,2},{1,3},{2,0},{3,1},{4,6},{5,7},{6,4},{7,5},{8,10},{9,11},{10,... | collective-permute-start | bytes 393224 | tf_op jit(solution)/shard_map/ppermute | solution.py:353
  27.7 3.4 %collective-permute-done.7.refs_1_ = bf16[4,64,256]{2,1,0:T(8,128)(2,1)S(1)} collective-permute-done((bf16[4,64,256]{2,1,0:T(8,128)(2,1)S(1)}, bf16[4,64,256]{2,1,0:T(8,128)(2,1)S(1)}, u32[]{:S(2)}, u32[]{:S(2)}) %collective-permute-start.7) | collective-permute-done | bytes 131104 | tf_op jit(solution)/shard_map/ppermute | solution.py:353
  31.1 0.0 copy-done.5
  31.1 0.0 copy-done.6
  31.1 0.0 copy-done.7
  31.1 0.0 copy-start.4
  31.1 2.2 %source_kernels.1.refs_4_ = bf16[2048,1024]{1,0:T(8,128)(2,1)S(1)} custom-call(bf16[4,64,256]{2,1,0:T(8,128)(2,1)S(1)} %pad_maximum_fusion.refs_0_, bf16[4,64,256]{2,1,0:T(8,128)(2,1)S(1)} %collective-permute-done.7.refs_1_, f32[64,1]{1,0:T(8,128)S(1)} %copy-done.5, f32[64,256]{1,0:T(8,128)S(1)} %copy-done.6, f32[64,256]{1,0:T(8,128)S(1)} %copy-done.7, ...), custom_call_target="tpu_custom_call" | custom-call | flops 17179869184 | bytes 8388608 | tf_op jit(solution)/shard_map/source_kernels/pallas_call | solution.py:261
  33.4 0.1 collective-permute-start.8
  33.4 0.0 collective-permute-done.6.refs_1_
  33.4 0.5 %collective-permute-start.9 = (bf16[2,64,512]{2,1,0:T(8,128)(2,1)S(1)}, bf16[2,64,512]{2,1,0:T(8,128)(2,1)S(1)}, u32[]{:S(2)}, u32[]{:S(2)}) collective-permute-start(bf16[2,64,512]{2,1,0:T(8,128)(2,1)S(1)} %collective-permute-done.6.refs_1_), channel_id=1, source_target_pairs={{0,1},{1,0},{2,3},{3,2},{4,5},{5,4},{6,7},{7,6},{8,9},{9,8},{10,11... | collective-permute-start | bytes 393224 | tf_op jit(solution)/shard_map/ppermute | solution.py:353
  33.9 0.8 %collective-permute-done.8.refs_2_ = bf16[2,64,512]{2,1,0:T(8,128)(2,1)S(1)} collective-permute-done((bf16[2,64,512]{2,1,0:T(8,128)(2,1)S(1)}, bf16[2,64,512]{2,1,0:T(8,128)(2,1)S(1)}, u32[]{:S(2)}, u32[]{:S(2)}) %collective-permute-start.8) | collective-permute-done | bytes 131104 | tf_op jit(solution)/shard_map/ppermute | solution.py:353
  34.8 0.2 collective-permute-done.9.refs_3_
  35.0 0.0 copy-done.4
  35.0 2.4 %correlate.1 = f32[32,64,256]{2,1,0:T(8,128)} custom-call(bf16[2,64,512]{2,1,0:T(8,128)(2,1)S(1)} %channel_spectra.1.refs_0_, bf16[2,64,512]{2,1,0:T(8,128)(2,1)S(1)} %collective-permute-done.6.refs_1_, bf16[2,64,512]{2,1,0:T(8,128)(2,1)S(1)} %collective-permute-done.8.refs_2_, bf16[2,64,512]{2,1,0:T(8,128)(2,1)S(1)} %collective-permute-done.9.refs_3_, ...), custom_call_target="tpu_custom_call" | custom-call | tf_op jit(solution)/shard_map/correlate/pallas_call | solution.py:317
  (1 shorter events, 0.0 us)
Async XLA Ops:
  2.0 22.9 %all-to-all-start = ((bf16[8,128,256]{2,1,0:T(8,128)(2,1)}), bf16[8,128,256]{2,1,0:T(8,128)(2,1)S(1)}, u32[]{:S(2)}, u32[]{:S(2)}) async-start(bf16[8,128,256]{2,1,0:T(8,128)(2,1)} %bitcast.7), calls=%async_computation | async-start | bytes 1048576 | tf_op jit(solution)/shard_map/all_to_all | solution.py:398
  9.3 3.9 %collective-permute-start.2 = (bf16[2,32,256]{2,1,0:T(8,128)(2,1)}, bf16[2,32,256]{2,1,0:T(8,128)(2,1)S(1)}, u32[]{:S(2)}, u32[]{:S(2)}) collective-permute-start(bf16[2,32,256]{2,1,0:T(8,128)(2,1)} %get-tuple-element.22), channel_id=1, source_target_pairs={{0,3},{1,2},{2,1},{3,0},{4,7},{5,6},{6,5},{7,4},{8,11},{9,10},{10,... | collective-permute-start | bytes 98312 | tf_op jit(solution)/shard_map/ppermute | solution.py:353
  10.0 4.5 %collective-permute-start.1 = (bf16[2,32,256]{2,1,0:T(8,128)(2,1)}, bf16[2,32,256]{2,1,0:T(8,128)(2,1)S(1)}, u32[]{:S(2)}, u32[]{:S(2)}) collective-permute-start(bf16[2,32,256]{2,1,0:T(8,128)(2,1)} %get-tuple-element.21), channel_id=1, source_target_pairs={{0,2},{1,3},{2,0},{3,1},{4,6},{5,7},{6,4},{7,5},{8,10},{9,11},{10,... | collective-permute-start | bytes 98312 | tf_op jit(solution)/shard_map/ppermute | solution.py:353
  10.9 3.6 %collective-permute-start = (bf16[2,32,256]{2,1,0:T(8,128)(2,1)}, bf16[2,32,256]{2,1,0:T(8,128)(2,1)S(1)}, u32[]{:S(2)}, u32[]{:S(2)}) collective-permute-start(bf16[2,32,256]{2,1,0:T(8,128)(2,1)} %get-tuple-element.20), channel_id=1, source_target_pairs={{0,1},{1,0},{2,3},{3,2},{4,5},{5,4},{6,7},{7,6},{8,9},{9,8},{10,11... | collective-permute-start | bytes 98312 | tf_op jit(solution)/shard_map/ppermute | solution.py:353
  14.5 10.5 %copy-start.2 = (bf16[256,256]{1,0:T(8,128)(2,1)S(1)}, bf16[256,256]{1,0:T(8,128)(2,1)}, u32[]{:S(2)}) copy-start(bf16[256,256]{1,0:T(8,128)(2,1)} %constant.12.clone.bins_ref.refs_7_) | copy-start | bytes 393220
  15.3 5.9 %collective-permute-start.5 = (bf16[1,64,256]{2,1,0:T(8,128)(2,1)S(1)}, bf16[1,64,256]{2,1,0:T(8,128)(2,1)S(1)}, u32[]{:S(2)}, u32[]{:S(2)}) collective-permute-start(bf16[1,64,256]{2,1,0:T(8,128)(2,1)S(1)} %bitcast.3), channel_id=1, source_target_pairs={{0,12},{4,8},{8,4},{12,0},{16,28},{20,24},{24,20},{28,16},{1,13},{... | collective-permute-start | bytes 98312 | tf_op jit(solution)/shard_map/ppermute | solution.py:353
  17.7 4.0 %collective-permute-start.4 = (bf16[1,64,256]{2,1,0:T(8,128)(2,1)S(1)}, bf16[1,64,256]{2,1,0:T(8,128)(2,1)S(1)}, u32[]{:S(2)}, u32[]{:S(2)}) collective-permute-start(bf16[1,64,256]{2,1,0:T(8,128)(2,1)S(1)} %bitcast.4), channel_id=1, source_target_pairs={{0,8},{4,12},{8,0},{12,4},{16,24},{20,28},{24,16},{28,20},{1,9},{5... | collective-permute-start | bytes 98312 | tf_op jit(solution)/shard_map/ppermute | solution.py:353
  18.3 4.4 %collective-permute-start.3 = (bf16[1,64,256]{2,1,0:T(8,128)(2,1)S(1)}, bf16[1,64,256]{2,1,0:T(8,128)(2,1)S(1)}, u32[]{:S(2)}, u32[]{:S(2)}) collective-permute-start(bf16[1,64,256]{2,1,0:T(8,128)(2,1)S(1)} %bitcast.5), channel_id=1, source_target_pairs={{0,4},{4,0},{8,12},{12,8},{16,20},{20,16},{24,28},{28,24},{1,5},{5... | collective-permute-start | bytes 98312 | tf_op jit(solution)/shard_map/ppermute | solution.py:353
  18.8 1.6 %copy-start = (bf16[2048,512]{1,0:T(8,128)(2,1)S(1)}, bf16[2048,512]{1,0:T(8,128)(2,1)}, u32[]{:S(2)}) copy-start(bf16[2048,512]{1,0:T(8,128)(2,1)} %constant.10.clone.table_hbm) | copy-start | bytes 6291460
  20.4 4.6 %copy-start.1 = (bf16[512,256]{1,0:T(8,128)(2,1)S(1)}, bf16[512,256]{1,0:T(8,128)(2,1)}, u32[]{:S(2)}) copy-start(bf16[512,256]{1,0:T(8,128)(2,1)} %constant.11.clone.band_ref.refs_6_) | copy-start | bytes 786436
  20.4 4.6 %copy-start.3 = (f32[128,1]{1,0:T(8,128)S(1)}, f32[128,1]{1,0:T(8,128)}, u32[]{:S(2)}) copy-start(f32[128,1]{1,0:T(8,128)} %get-tuple-element.18.live_ref) | copy-start | bytes 1540
  20.6 10.6 %copy-start.5 = (f32[64,1]{1,0:T(8,128)S(1)}, f32[64,1]{1,0:T(8,128)}, u32[]{:S(2)}) copy-start(f32[64,1]{1,0:T(8,128)} %get-tuple-element.25.refs_2_) | copy-start | bytes 772
  20.6 10.5 %copy-start.6 = (f32[64,256]{1,0:T(8,128)S(1)}, f32[64,256]{1,0:T(8,128)}, u32[]{:S(2)}) copy-start(f32[64,256]{1,0:T(8,128)} %constant.13.clone.refs_3_) | copy-start | bytes 196612
  20.6 10.5 %copy-start.7 = (f32[64,256]{1,0:T(8,128)S(1)}, f32[64,256]{1,0:T(8,128)}, u32[]{:S(2)}) copy-start(f32[64,256]{1,0:T(8,128)} %constant.14.clone.refs_4_) | copy-start | bytes 196612
  22.7 8.4 %collective-permute-start.7 = (bf16[4,64,256]{2,1,0:T(8,128)(2,1)S(1)}, bf16[4,64,256]{2,1,0:T(8,128)(2,1)S(1)}, u32[]{:S(2)}, u32[]{:S(2)}) collective-permute-start(bf16[4,64,256]{2,1,0:T(8,128)(2,1)S(1)} %pad_maximum_fusion.refs_0_), channel_id=1, source_target_pairs={{0,16},{4,20},{8,24},{12,28},{16,0},{20,4},{24,8},{28,12},{1,17},{... | collective-permute-start | bytes 393224 | tf_op jit(solution)/shard_map/ppermute | solution.py:353
  26.3 7.1 %collective-permute-start.6 = (bf16[2,64,512]{2,1,0:T(8,128)(2,1)S(1)}, bf16[2,64,512]{2,1,0:T(8,128)(2,1)S(1)}, u32[]{:S(2)}, u32[]{:S(2)}) collective-permute-start(bf16[2,64,512]{2,1,0:T(8,128)(2,1)S(1)} %channel_spectra.1.refs_0_), channel_id=1, source_target_pairs={{0,2},{1,3},{2,0},{3,1},{4,6},{5,7},{6,4},{7,5},{8,10},{9,11},{10,... | collective-permute-start | bytes 393224 | tf_op jit(solution)/shard_map/ppermute | solution.py:353
  31.1 3.8 %copy-start.4 = (f32[32,256]{1,0:T(8,128)S(1)}, f32[32,256]{1,0:T(8,128)}, u32[]{:S(2)}) copy-start(f32[32,256]{1,0:T(8,128)} %get-tuple-element.28.refs_5_) | copy-start | bytes 98308
  33.4 1.4 %collective-permute-start.8 = (bf16[2,64,512]{2,1,0:T(8,128)(2,1)S(1)}, bf16[2,64,512]{2,1,0:T(8,128)(2,1)S(1)}, u32[]{:S(2)}, u32[]{:S(2)}) collective-permute-start(bf16[2,64,512]{2,1,0:T(8,128)(2,1)S(1)} %channel_spectra.1.refs_0_), channel_id=1, source_target_pairs={{0,1},{1,0},{2,3},{3,2},{4,5},{5,4},{6,7},{7,6},{8,9},{9,8},{10,11... | collective-permute-start | bytes 393224 | tf_op jit(solution)/shard_map/ppermute | solution.py:353
  33.4 1.5 %collective-permute-start.9 = (bf16[2,64,512]{2,1,0:T(8,128)(2,1)S(1)}, bf16[2,64,512]{2,1,0:T(8,128)(2,1)S(1)}, u32[]{:S(2)}, u32[]{:S(2)}) collective-permute-start(bf16[2,64,512]{2,1,0:T(8,128)(2,1)S(1)} %collective-permute-done.6.refs_1_), channel_id=1, source_target_pairs={{0,1},{1,0},{2,3},{3,2},{4,5},{5,4},{6,7},{7,6},{8,9},{9,8},{10,11... | collective-permute-start | bytes 393224 | tf_op jit(solution)/shard_map/ppermute | solution.py:353

commit v4 on v3

--- a/solution.py
+++ b/solution.py
@@ -82,12 +82,14 @@
     copies = [
         pltpu.make_async_copy(src_hbm, src_ref, sem.at[0]),
         pltpu.make_async_copy(dead_hbm, dead_ref, sem.at[1]),
-        pltpu.make_async_copy(rec_hbm, rec_ref, sem.at[2]),
     ]
-    for copy in copies:
-        copy.start()
     windows, groups, width, span = rec_ref.shape
     per = groups // out_ref.shape[0]
+    brought = [
+        pltpu.make_async_copy(rec_hbm.at[w], rec_ref.at[w], sem.at[2 + w]) for w in range(windows)
+    ]
+    for copy in copies + brought:
+        copy.start()
     reps = cw // width
     rep, chan = lax.axis_index("rep"), lax.axis_index("chan")
     count = src_ref.shape[1]
@@ -124,8 +126,8 @@
         scale_ref[:, i : i + span] = 1.0 / (
             math.sqrt(K) * jnp.maximum(pick_ref[here, : min(span, per * cw)], 1.0)
         )
-    copies[2].wait()
     for w in range(windows):
+        brought[w].wait()
         for g in range(groups):
             out_ref[g // per, w, g % per] = rec_ref[w, g]
     for w in range(windows):
@@ -137,8 +139,9 @@
 
 
 def pack(records, sources, dead_list, chans, reps):
+    records, sources, dead_list = [pltpu.with_memory_space_constraint(a, pltpu.HBM) for a in (records, sources.reshape(1, -1), dead_list)]
     windows, groups, width, span = records.shape
-    count = sources.shape[0]
+    count = sources.shape[1]
     per = groups // chans
     part = jax.ShapeDtypeStruct((windows, count // reps, span), jnp.bfloat16)
     return pl.pallas_call(
@@ -157,11 +160,11 @@
             pltpu.VMEM((1, count), jnp.int32),
             pltpu.VMEM(dead_list.shape, jnp.int32),
             pltpu.VMEM((count, span), jnp.float32),
-            pltpu.SemaphoreType.DMA((3,)),
+            pltpu.SemaphoreType.DMA((2 + windows,)),
         ],
-        compiler_params=pltpu.CompilerParams(vmem_limit_bytes=WHOLE),
+        compiler_params=pltpu.CompilerParams(vmem_limit_bytes=LIMIT),
         name="pack",
-    )(records, sources.reshape(1, count), dead_list)
+    )(records, sources, dead_list)
 
 
 def whiten_rows(x_ref, ext_ref, table_ref, band_ref, bins_ref):
@@ -227,23 +230,45 @@
     )(x, live, *tables)
 
 
-def source_kernel(keys, windows, *refs):
+def source_kernel(keys, *refs):
     parts = refs[: len(keys)]
-    live_ref, cos_ref, sin_ref, table_ref, band_ref, bins_ref = refs[len(keys) : -3]
+    live_ref, table_ref, band_ref, bins_ref = refs[len(keys) : -3]
     out_ref, x_ref, ext_ref = refs[-3:]
     chan = lax.axis_index("chan")
     for part, slots in zip(parts, keys):
         for n, key in enumerate(slots):
             x_ref[chan ^ key if key is not None else n] = part[n]
     real_part, imag_part = whiten_rows(x_ref, ext_ref, table_ref, band_ref, bins_ref)
-    real_part = (real_part * live_ref[...]).astype(jnp.bfloat16).astype(jnp.float32)
-    imag_part = (imag_part * live_ref[...]).astype(jnp.bfloat16).astype(jnp.float32)
-    quarter = real_part.shape[0] // windows
+    out_ref[:, :K] = (real_part * live_ref[...]).astype(jnp.bfloat16)
+    out_ref[:, K:] = (imag_part * live_ref[...]).astype(jnp.bfloat16)
+
+
+def source_spectra(parts, keys, live, tables):
+    rows = parts[0].shape[1]
+    pieces = sum(len(slots) for slots in keys)
+    return pl.pallas_call(
+        functools.partial(source_kernel, keys),
+        out_shape=jax.ShapeDtypeStruct((rows, 2 * K), jnp.bfloat16),
+        in_specs=[VMEM] * (len(parts) + 4),
+        out_specs=VMEM,
+        scratch_shapes=[
+            pltpu.VMEM((pieces, rows, CHUNK), jnp.bfloat16),
+            pltpu.VMEM((pieces * rows, CHUNK + 2 * EDGE), jnp.bfloat16),
+        ],
+        compiler_params=pltpu.CompilerParams(vmem_limit_bytes=LIMIT),
+        cost_estimate=pl.CostEstimate(flops=1 << 34, bytes_accessed=8 << 20, transcendentals=0),
+        name="source_spectra",
+    )(*parts, live, *tables)
+
+
+def lag_kernel(windows, spec_ref, cos_ref, sin_ref, out_ref):
+    spec = spec_ref[...].astype(jnp.float32)
+    quarter = spec.shape[0] // windows
     lags = cos_ref.shape[0]
     for s in range(quarter):
         for w in range(windows):
-            u = real_part[w * quarter + s : w * quarter + s + 1, :]
-            v = imag_part[w * quarter + s : w * quarter + s + 1, :]
+            u = spec[w * quarter + s : w * quarter + s + 1, :K]
+            v = spec[w * quarter + s : w * quarter + s + 1, K:]
             rows = slice(s * lags, (s + 1) * lags)
             first = w * 2 * K
             out_ref[rows, first : first + K] = (
@@ -254,25 +279,37 @@
             ).astype(jnp.bfloat16)
 
 
-def source_kernels(parts, keys, live, tables, windows):
-    rows = parts[0].shape[1]
-    pieces = sum(len(slots) for slots in keys)
+def lag_kernels(spec, windows):
+    rows = spec.shape[0]
     cosine, sine = lag_tables()
     return pl.pallas_call(
-        functools.partial(source_kernel, keys, windows),
+        functools.partial(lag_kernel, windows),
         out_shape=jax.ShapeDtypeStruct((rows // windows * LAGS, windows * 2 * K), jnp.bfloat16),
-        in_specs=[VMEM] * (len(parts) + 6),
+        in_specs=[VMEM] * 3,
         out_specs=VMEM,
-        scratch_shapes=[
-            pltpu.VMEM((pieces, rows, CHUNK), jnp.bfloat16),
-            pltpu.VMEM((pieces * rows, CHUNK + 2 * EDGE), jnp.bfloat16),
-        ],
-        compiler_params=pltpu.CompilerParams(vmem_limit_bytes=LIMIT),
-        cost_estimate=pl.CostEstimate(
-            flops=1 << 34, bytes_accessed=8 << 20, transcendentals=0
-        ),
-        name="source_kernels",
-    )(*parts, live, jnp.asarray(cosine), jnp.asarray(sine), *tables)
+        compiler_params=pltpu.CompilerParams(vmem_limit_bytes=LIMIT),
+        cost_estimate=pl.CostEstimate(flops=1 << 34, bytes_accessed=8 << 20, transcendentals=0),
+        name="lag_kernels",
+    )(spec, jnp.asarray(cosine), jnp.asarray(sine))
+
+
+def merge_kernel(*refs):
+    total = refs[0][...]
+    for ref in refs[1:-1]:
+        total = total + ref[...]
+    refs[-1][...] = total
+
+
+def merge(parts):
+    return pl.pallas_call(
+        merge_kernel,
+        out_shape=jax.ShapeDtypeStruct(parts[0].shape, parts[0].dtype),
+        in_specs=[VMEM] * len(parts),
+        out_specs=VMEM,
+        compiler_params=pltpu.CompilerParams(vmem_limit_bytes=LIMIT),
+        cost_estimate=pl.CostEstimate(flops=1, bytes_accessed=1, transcendentals=0),
+        name="merge",
+    )(*parts)
 
 
 def correlate_kernel(flips, cw, *refs):
@@ -313,7 +350,7 @@
 
 def correlate(parts, flips, left, scale, cw):
     quarter, columns = scale.shape
-    steps = 4
+    steps = 8
     return pl.pallas_call(
         functools.partial(correlate_kernel, flips, cw),
         out_shape=jax.ShapeDtypeStruct((quarter, LAGS, columns), jnp.float32),
@@ -364,9 +401,7 @@
 def gather_sources(given, table):
     chans, chan = lax.axis_size("chan"), lax.axis_index("chan")
     windows, quarter, span = given[0].shape
-    mine = given[0]
-    for other in [swap(part, "rep", flip) for flip, part in enumerate(given) if flip]:
-        mine = mine + other
+    mine = merge([swap(part, "rep", flip) if flip else part for flip, part in enumerate(given)])
     table = stage(table, mine)
     held = mine.reshape(1, windows * quarter, span)
     near = min(4, chans // 2)
@@ -399,16 +434,17 @@
     table, parts, keys = gather_sources(given, jnp.asarray(dft_table(chans * span)))
     tables = [table, jnp.asarray(sample_band()), jnp.asarray(bin_band())]
     spectra = channel_spectra(arrived, live, tables, windows)
-    left = source_kernels(parts, keys, source_live, tables, windows)
+    source_spec = source_spectra(parts, keys, source_live, tables)
     pieces, flips = [spectra], [0]
     flip = reps // 2
     while flip:
         others = [swap(piece, "rep", flip) for piece in pieces]
         if flip > 1:
-            others, left = lax.optimization_barrier((others, left))
+            others, source_spec = lax.optimization_barrier((others, source_spec))
         pieces = pieces + others
         flips = flips + [f ^ flip for f in flips]
         flip //= 2
+    left = lag_kernels(source_spec, windows)
     return correlate(pieces, flips, left, scale, cw)
 
 

time: 37.6 us -> 35.9 us (0.955)
  waiting for transfers between devices: 9.79 us -> 8.32 us
  starting transfers between devices: 16.9 us -> 17.9 us
  other arithmetic: 0.83 us -> 0.02 us
    ppermute x10, waiting for transfers between devices: 9.79 us -> 8.32 us  [swap(): return lax.ppermute(x, axis, [(i, i ^ flip) for i in range(size)])]
    ppermute x10, starting transfers between devices: 9.62 us -> 10.6 us  [swap(): return lax.ppermute(x, axis, [(i, i ^ flip) for i in range(size)])]
    add x1 -> x0, other arithmetic: 0.81 us -> none  [gather_sources(): mine = mine + other]
    pallas_call x1 -> x3, Pallas kernels: 2.2 us -> 2.04 us  [the longest x1 1.04 us: source_spectra(): pl.pallas_call(functools.partial(source_kernel, keys), out_shape=jax.Shap...]
    unnamed x16 -> x10, local copies, waits for them, and re-layouts: 1.62 us -> 1.61 us
  transfers between devices with their start and end apart: 11 -> 11, of which waited for: 8 -> 6; matrix products, arithmetic and copies ran while one was open for 2% -> 0% of each run, Pallas kernels for 10% -> 10%
where the time goes in v4:
time: 35.9 us; the launch traced here: 35.7 us
  starting transfers between devices  17.9 us (50%)
  waiting for transfers between devices  8.32 us (23%)
  Pallas kernels  7.76 us (22%)
  local copies, waits for them, and re-layouts  1.61 us (4%)
    ppermute x10, starting transfers between devices, swap(): return lax.ppermute(x, axis, [(i, i ^ flip) for i in range(size)])  10.6 us
    ppermute x10, waiting for transfers between devices, swap(): return lax.ppermute(x, axis, [(i, i ^ flip) for i in range(size)])  8.32 us
    all_to_all x1, starting transfers between devices, shards(): arrived = regroup(lax.all_to_all(blocks, 'chan', 0, 0, tiled=True))  7.29 us
    pallas_call x1, Pallas kernels, correlate(): pl.pallas_call(functools.partial(correlate_kernel, flips, cw), out_shape=...  2.25 us
    pallas_call x1, Pallas kernels, pack(): pl.pallas_call(functools.partial(pack_kernel, width * reps), out_shape=(j...  2.01 us
    unnamed x10, local copies, waits for them, and re-layouts  1.61 us
    pallas_call x1, Pallas kernels, channel_spectra(): pl.pallas_call(channel_kernel, out_shape=jax.ShapeDtypeStruct((windows, r...  1.31 us
    pallas_call x1, Pallas kernels, source_spectra(): pl.pallas_call(functools.partial(source_kernel, keys), out_shape=jax.Shap...  1.04 us
  transfers between devices with their start and end apart: 11, of which 6 were waited for; matrix products, arithmetic and copies ran while one was open for 0% of the time, Pallas kernels for 10%

profile of v4, /device:TPU:0, one launch (start us, length us, event | category | flops | bytes accessed | tf_op | source)
XLA Modules:
  0.0 35.7 jit_solution(11398715671062552289)
XLA Ops:
  0.0 2.0 %pack.1 = (bf16[8,2,1,64,256]{4,3,2,1,0:T(8,128)(2,1)}, bf16[2,32,256]{2,1,0:T(8,128)(2,1)S(1)}, bf16[2,32,256]{2,1,0:T(8,128)(2,1)S(1)}, bf16[2,32,256]{2,1,0:T...) custom-call(bf16[2,8,64,256]{3,2,1,0:T(8,128)(2,1)} %rec_hbm.1, ...), custom_call_target="tpu_custom_call" | custom-call | tf_op jit(solution)/shard_map/pack/pallas_call | solution.py:147
  2.0 7.3 %all-to-all-start = ((bf16[8,128,256]{2,1,0:T(8,128)(2,1)}), bf16[8,128,256]{2,1,0:T(8,128)(2,1)S(1)}, u32[]{:S(2)}, u32[]{:S(2)}) async-start(bf16[8,128,256]{2,1,0:T(8,128)(2,1)} %bitcast.1), calls=%async_computation | async-start | bytes 1048576 | tf_op jit(solution)/shard_map/all_to_all | solution.py:433
  9.3 0.0 collective-permute-start
  9.3 1.6 %collective-permute-start.1 = (bf16[2,32,256]{2,1,0:T(8,128)(2,1)S(1)}, bf16[2,32,256]{2,1,0:T(8,128)(2,1)S(1)}, u32[]{:S(2)}, u32[]{:S(2)}) collective-permute-start(bf16[2,32,256]{2,1,0:T(8,128)(2,1)S(1)} %get-tuple-element.21), channel_id=1, source_target_pairs={{0,2},{1,3},{2,0},{3,1},{4,6},{5,7},{6,4},{7,5},{8,10},{9,11},{10,... | collective-permute-start | bytes 98312 | tf_op jit(solution)/shard_map/ppermute | solution.py:390
  10.9 0.3 collective-permute-start.2
  11.2 0.0 collective-permute-done.refs_1_
  11.2 2.1 %collective-permute-done.1.refs_2_ = bf16[2,32,256]{2,1,0:T(8,128)(2,1)S(1)} collective-permute-done((bf16[2,32,256]{2,1,0:T(8,128)(2,1)S(1)}, bf16[2,32,256]{2,1,0:T(8,128)(2,1)S(1)}, u32[]{:S(2)}, u32[]{:S(2)}) %collective-permute-start.1) | collective-permute-done | bytes 32800 | tf_op jit(solution)/shard_map/ppermute | solution.py:390
  13.3 0.9 %collective-permute-done.2.refs_3_ = bf16[2,32,256]{2,1,0:T(8,128)(2,1)S(1)} collective-permute-done((bf16[2,32,256]{2,1,0:T(8,128)(2,1)S(1)}, bf16[2,32,256]{2,1,0:T(8,128)(2,1)S(1)}, u32[]{:S(2)}, u32[]{:S(2)}) %collective-permute-start.2) | collective-permute-done | bytes 32800 | tf_op jit(solution)/shard_map/ppermute | solution.py:390
  14.2 0.0 copy-start.2
  14.2 2.9 %collective-permute-start.5 = (bf16[1,64,256]{2,1,0:T(8,128)(2,1)S(1)}, bf16[1,64,256]{2,1,0:T(8,128)(2,1)S(1)}, u32[]{:S(2)}, u32[]{:S(2)}) collective-permute-start(bf16[1,64,256]{2,1,0:T(8,128)(2,1)S(1)} %bitcast.3), channel_id=1, source_target_pairs={{0,12},{4,8},{8,4},{12,0},{16,28},{20,24},{24,20},{28,16},{1,13},{... | collective-permute-start | bytes 98312 | tf_op jit(solution)/shard_map/ppermute | solution.py:390
  17.1 0.6 %collective-permute-start.4 = (bf16[1,64,256]{2,1,0:T(8,128)(2,1)S(1)}, bf16[1,64,256]{2,1,0:T(8,128)(2,1)S(1)}, u32[]{:S(2)}, u32[]{:S(2)}) collective-permute-start(bf16[1,64,256]{2,1,0:T(8,128)(2,1)S(1)} %bitcast.4), channel_id=1, source_target_pairs={{0,8},{4,12},{8,0},{12,4},{16,24},{20,28},{24,16},{28,20},{1,9},{5... | collective-permute-start | bytes 98312 | tf_op jit(solution)/shard_map/ppermute | solution.py:390
  17.7 0.1 collective-permute-start.3
  17.8 0.0 copy-start
  17.8 1.6 %copy-done = bf16[2048,512]{1,0:T(8,128)(2,1)S(1)} copy-done((bf16[2048,512]{1,0:T(8,128)(2,1)S(1)}, bf16[2048,512]{1,0:T(8,128)(2,1)}, u32[]{:S(2)}) %copy-start) | copy-done | bytes 2097176
  19.4 0.0 copy-start.1
  19.4 0.1 stage.1.table_ref.refs_3_
  19.5 1.4 %collective-permute-done.5 = bf16[1,64,256]{2,1,0:T(8,128)(2,1)S(1)} collective-permute-done((bf16[1,64,256]{2,1,0:T(8,128)(2,1)S(1)}, bf16[1,64,256]{2,1,0:T(8,128)(2,1)S(1)}, u32[]{:S(2)}, u32[]{:S(2)}) %collective-permute-start.5) | collective-permute-done | bytes 32800 | tf_op jit(solution)/shard_map/ppermute | solution.py:390
  21.0 0.2 collective-permute-done.4
  21.2 0.5 %collective-permute-done.3 = bf16[1,64,256]{2,1,0:T(8,128)(2,1)S(1)} collective-permute-done((bf16[1,64,256]{2,1,0:T(8,128)(2,1)S(1)}, bf16[1,64,256]{2,1,0:T(8,128)(2,1)S(1)}, u32[]{:S(2)}, u32[]{:S(2)}) %collective-permute-start.3) | collective-permute-done | bytes 32800 | tf_op jit(solution)/shard_map/ppermute | solution.py:390
  21.7 3.1 %collective-permute-start.7 = (bf16[4,64,256]{2,1,0:T(8,128)(2,1)S(1)}, bf16[4,64,256]{2,1,0:T(8,128)(2,1)S(1)}, u32[]{:S(2)}, u32[]{:S(2)}) collective-permute-start(bf16[4,64,256]{2,1,0:T(8,128)(2,1)S(1)} %pad_maximum_fusion.refs_0_), channel_id=1, source_target_pairs={{0,16},{4,20},{8,24},{12,28},{16,0},{20,4},{24,8},{28,12},{1,17},{... | collective-permute-start | bytes 393224 | tf_op jit(solution)/shard_map/ppermute | solution.py:390
  24.8 0.0 all-to-all-done.x_ref
  24.8 0.0 copy-done.2
  24.8 0.0 copy-done.1
  24.8 1.3 %channel_spectra.1.refs_0_ = bf16[2,64,512]{2,1,0:T(8,128)(2,1)S(1)} custom-call(bf16[8,128,256]{2,1,0:T(8,128)(2,1)S(1)} %all-to-all-done.x_ref, f32[128,1]{1,0:T(8,128)S(1)} %get-tuple-element.18.live_ref, bf16[2048,512]{1,0:T(8,128)(2,1)S(1)} %stage.1.table_ref.refs_3_, bf16[512,256]{1,0:T(8,128)(2,1)S(1)} %copy-done.1, bf16[256,256]{1,0:T(8,128)(2,1)S(1)} %copy-done.2), custom_call_target="tpu_custom_call" | custom-call | flops 1 | bytes 1 | tf_op jit(solution)/shard_map/channel_spectra/pallas_call | solution.py:219
  26.1 1.6 %collective-permute-start.6 = (bf16[2,64,512]{2,1,0:T(8,128)(2,1)S(1)}, bf16[2,64,512]{2,1,0:T(8,128)(2,1)S(1)}, u32[]{:S(2)}, u32[]{:S(2)}) collective-permute-start(bf16[2,64,512]{2,1,0:T(8,128)(2,1)S(1)} %channel_spectra.1.refs_0_), channel_id=1, source_target_pairs={{0,2},{1,3},{2,0},{3,1},{4,6},{5,7},{6,4},{7,5},{8,10},{9,11},{10,... | collective-permute-start | bytes 393224 | tf_op jit(solution)/shard_map/ppermute | solution.py:390
  27.7 3.1 %collective-permute-done.7.refs_1_ = bf16[4,64,256]{2,1,0:T(8,128)(2,1)S(1)} collective-permute-done((bf16[4,64,256]{2,1,0:T(8,128)(2,1)S(1)}, bf16[4,64,256]{2,1,0:T(8,128)(2,1)S(1)}, u32[]{:S(2)}, u32[]{:S(2)}) %collective-permute-start.7) | collective-permute-done | bytes 131104 | tf_op jit(solution)/shard_map/ppermute | solution.py:390
  30.8 0.0 copy-start.3
  30.8 0.0 copy-start.4
  30.8 1.0 %source_spectra.1.spec_ref = bf16[64,512]{1,0:T(8,128)(2,1)S(1)} custom-call(bf16[4,64,256]{2,1,0:T(8,128)(2,1)S(1)} %pad_maximum_fusion.refs_0_, bf16[4,64,256]{2,1,0:T(8,128)(2,1)S(1)} %collective-permute-done.7.refs_1_, f32[64,1]{1,0:T(8,128)S(1)} %get-tuple-element.25.refs_2_, bf16[2048,512]{1,0:T(8,128)(2,1)S(1)} %stage.1.table_ref.refs_3_, ...), custom_call_target="tpu_custom_call" | custom-call | flops 17179869184 | bytes 8388608 | tf_op jit(solution)/shard_map/source_spectra/pallas_call | solution.py:249
  31.8 0.1 collective-permute-start.8
  31.9 0.0 collective-permute-done.6.refs_1_
  31.9 0.5 %collective-permute-start.9 = (bf16[2,64,512]{2,1,0:T(8,128)(2,1)S(1)}, bf16[2,64,512]{2,1,0:T(8,128)(2,1)S(1)}, u32[]{:S(2)}, u32[]{:S(2)}) collective-permute-start(bf16[2,64,512]{2,1,0:T(8,128)(2,1)S(1)} %collective-permute-done.6.refs_1_), channel_id=1, source_target_pairs={{0,1},{1,0},{2,3},{3,2},{4,5},{5,4},{6,7},{7,6},{8,9},{9,8},{10,11... | collective-permute-start | bytes 393224 | tf_op jit(solution)/shard_map/ppermute | solution.py:390
  32.4 0.0 copy-done.3
  32.4 0.0 copy-done.4
  32.4 1.0 %lag_kernels.1.refs_4_ = bf16[2048,1024]{1,0:T(8,128)(2,1)S(1)} custom-call(bf16[64,512]{1,0:T(8,128)(2,1)S(1)} %source_spectra.1.spec_ref, f32[64,256]{1,0:T(8,128)S(1)} %copy-done.4, f32[64,256]{1,0:T(8,128)S(1)} %copy-done.3), custom_call_target="tpu_custom_call" | custom-call | flops 17179869184 | bytes 8388608 | tf_op jit(solution)/shard_map/lag_kernels/pallas_call | solution.py:285
  33.4 0.0 collective-permute-done.8.refs_2_
  33.4 0.0 collective-permute-done.9.refs_3_
  33.4 2.2 %correlate.1 = f32[32,64,256]{2,1,0:T(8,128)} custom-call(bf16[2,64,512]{2,1,0:T(8,128)(2,1)S(1)} %channel_spectra.1.refs_0_, bf16[2,64,512]{2,1,0:T(8,128)(2,1)S(1)} %collective-permute-done.6.refs_1_, bf16[2,64,512]{2,1,0:T(8,128)(2,1)S(1)} %collective-permute-done.8.refs_2_, bf16[2,64,512]{2,1,0:T(8,128)(2,1)S(1)} %collective-permute-done.9.refs_3_, ...), custom_call_target="tpu_custom_call" | custom-call | tf_op jit(solution)/shard_map/correlate/pallas_call | solution.py:354
  (2 shorter events, 0.0 us)
Async XLA Ops:
  2.0 22.8 %all-to-all-start = ((bf16[8,128,256]{2,1,0:T(8,128)(2,1)}), bf16[8,128,256]{2,1,0:T(8,128)(2,1)S(1)}, u32[]{:S(2)}, u32[]{:S(2)}) async-start(bf16[8,128,256]{2,1,0:T(8,128)(2,1)} %bitcast.1), calls=%async_computation | async-start | bytes 1048576 | tf_op jit(solution)/shard_map/all_to_all | solution.py:433
  9.3 1.9 %collective-permute-start = (bf16[2,32,256]{2,1,0:T(8,128)(2,1)S(1)}, bf16[2,32,256]{2,1,0:T(8,128)(2,1)S(1)}, u32[]{:S(2)}, u32[]{:S(2)}) collective-permute-start(bf16[2,32,256]{2,1,0:T(8,128)(2,1)S(1)} %get-tuple-element.20), channel_id=1, source_target_pairs={{0,1},{1,0},{2,3},{3,2},{4,5},{5,4},{6,7},{7,6},{8,9},{9,8},{10,11... | collective-permute-start | bytes 98312 | tf_op jit(solution)/shard_map/ppermute | solution.py:390
  9.3 4.0 %collective-permute-start.1 = (bf16[2,32,256]{2,1,0:T(8,128)(2,1)S(1)}, bf16[2,32,256]{2,1,0:T(8,128)(2,1)S(1)}, u32[]{:S(2)}, u32[]{:S(2)}) collective-permute-start(bf16[2,32,256]{2,1,0:T(8,128)(2,1)S(1)} %get-tuple-element.21), channel_id=1, source_target_pairs={{0,2},{1,3},{2,0},{3,1},{4,6},{5,7},{6,4},{7,5},{8,10},{9,11},{10,... | collective-permute-start | bytes 98312 | tf_op jit(solution)/shard_map/ppermute | solution.py:390
  10.9 3.4 %collective-permute-start.2 = (bf16[2,32,256]{2,1,0:T(8,128)(2,1)S(1)}, bf16[2,32,256]{2,1,0:T(8,128)(2,1)S(1)}, u32[]{:S(2)}, u32[]{:S(2)}) collective-permute-start(bf16[2,32,256]{2,1,0:T(8,128)(2,1)S(1)} %get-tuple-element.22), channel_id=1, source_target_pairs={{0,3},{1,2},{2,1},{3,0},{4,7},{5,6},{6,5},{7,4},{8,11},{9,10},{10,... | collective-permute-start | bytes 98312 | tf_op jit(solution)/shard_map/ppermute | solution.py:390
  14.2 10.6 %copy-start.2 = (bf16[256,256]{1,0:T(8,128)(2,1)S(1)}, bf16[256,256]{1,0:T(8,128)(2,1)}, u32[]{:S(2)}) copy-start(bf16[256,256]{1,0:T(8,128)(2,1)} %constant.12.clone.bins_ref.refs_5_) | copy-start | bytes 393220
  14.2 6.7 %collective-permute-start.5 = (bf16[1,64,256]{2,1,0:T(8,128)(2,1)S(1)}, bf16[1,64,256]{2,1,0:T(8,128)(2,1)S(1)}, u32[]{:S(2)}, u32[]{:S(2)}) collective-permute-start(bf16[1,64,256]{2,1,0:T(8,128)(2,1)S(1)} %bitcast.3), channel_id=1, source_target_pairs={{0,12},{4,8},{8,4},{12,0},{16,28},{20,24},{24,20},{28,16},{1,13},{... | collective-permute-start | bytes 98312 | tf_op jit(solution)/shard_map/ppermute | solution.py:390
  17.1 4.0 %collective-permute-start.4 = (bf16[1,64,256]{2,1,0:T(8,128)(2,1)S(1)}, bf16[1,64,256]{2,1,0:T(8,128)(2,1)S(1)}, u32[]{:S(2)}, u32[]{:S(2)}) collective-permute-start(bf16[1,64,256]{2,1,0:T(8,128)(2,1)S(1)} %bitcast.4), channel_id=1, source_target_pairs={{0,8},{4,12},{8,0},{12,4},{16,24},{20,28},{24,16},{28,20},{1,9},{5... | collective-permute-start | bytes 98312 | tf_op jit(solution)/shard_map/ppermute | solution.py:390
  17.7 4.0 %collective-permute-start.3 = (bf16[1,64,256]{2,1,0:T(8,128)(2,1)S(1)}, bf16[1,64,256]{2,1,0:T(8,128)(2,1)S(1)}, u32[]{:S(2)}, u32[]{:S(2)}) collective-permute-start(bf16[1,64,256]{2,1,0:T(8,128)(2,1)S(1)} %bitcast.5), channel_id=1, source_target_pairs={{0,4},{4,0},{8,12},{12,8},{16,20},{20,16},{24,28},{28,24},{1,5},{5... | collective-permute-start | bytes 98312 | tf_op jit(solution)/shard_map/ppermute | solution.py:390
  17.8 1.6 %copy-start = (bf16[2048,512]{1,0:T(8,128)(2,1)S(1)}, bf16[2048,512]{1,0:T(8,128)(2,1)}, u32[]{:S(2)}) copy-start(bf16[2048,512]{1,0:T(8,128)(2,1)} %constant.10.clone.table_hbm) | copy-start | bytes 6291460
  19.4 5.4 %copy-start.1 = (bf16[512,256]{1,0:T(8,128)(2,1)S(1)}, bf16[512,256]{1,0:T(8,128)(2,1)}, u32[]{:S(2)}) copy-start(bf16[512,256]{1,0:T(8,128)(2,1)} %constant.11.clone.band_ref.refs_4_) | copy-start | bytes 786436
  21.7 9.0 %collective-permute-start.7 = (bf16[4,64,256]{2,1,0:T(8,128)(2,1)S(1)}, bf16[4,64,256]{2,1,0:T(8,128)(2,1)S(1)}, u32[]{:S(2)}, u32[]{:S(2)}) collective-permute-start(bf16[4,64,256]{2,1,0:T(8,128)(2,1)S(1)} %pad_maximum_fusion.refs_0_), channel_id=1, source_target_pairs={{0,16},{4,20},{8,24},{12,28},{16,0},{20,4},{24,8},{28,12},{1,17},{... | collective-permute-start | bytes 393224 | tf_op jit(solution)/shard_map/ppermute | solution.py:390
  26.1 5.8 %collective-permute-start.6 = (bf16[2,64,512]{2,1,0:T(8,128)(2,1)S(1)}, bf16[2,64,512]{2,1,0:T(8,128)(2,1)S(1)}, u32[]{:S(2)}, u32[]{:S(2)}) collective-permute-start(bf16[2,64,512]{2,1,0:T(8,128)(2,1)S(1)} %channel_spectra.1.refs_0_), channel_id=1, source_target_pairs={{0,2},{1,3},{2,0},{3,1},{4,6},{5,7},{6,4},{7,5},{8,10},{9,11},{10,... | collective-permute-start | bytes 393224 | tf_op jit(solution)/shard_map/ppermute | solution.py:390
  30.8 1.6 %copy-start.3 = (f32[64,256]{1,0:T(8,128)S(1)}, f32[64,256]{1,0:T(8,128)}, u32[]{:S(2)}) copy-start(f32[64,256]{1,0:T(8,128)} %constant.14.clone.sin_ref) | copy-start | bytes 196612
  30.8 1.6 %copy-start.4 = (f32[64,256]{1,0:T(8,128)S(1)}, f32[64,256]{1,0:T(8,128)}, u32[]{:S(2)}) copy-start(f32[64,256]{1,0:T(8,128)} %constant.13.clone.cos_ref) | copy-start | bytes 196612
  31.8 1.6 %collective-permute-start.8 = (bf16[2,64,512]{2,1,0:T(8,128)(2,1)S(1)}, bf16[2,64,512]{2,1,0:T(8,128)(2,1)S(1)}, u32[]{:S(2)}, u32[]{:S(2)}) collective-permute-start(bf16[2,64,512]{2,1,0:T(8,128)(2,1)S(1)} %channel_spectra.1.refs_0_), channel_id=1, source_target_pairs={{0,1},{1,0},{2,3},{3,2},{4,5},{5,4},{6,7},{7,6},{8,9},{9,8},{10,11... | collective-permute-start | bytes 393224 | tf_op jit(solution)/shard_map/ppermute | solution.py:390
  31.9 1.5 %collective-permute-start.9 = (bf16[2,64,512]{2,1,0:T(8,128)(2,1)S(1)}, bf16[2,64,512]{2,1,0:T(8,128)(2,1)S(1)}, u32[]{:S(2)}, u32[]{:S(2)}) collective-permute-start(bf16[2,64,512]{2,1,0:T(8,128)(2,1)S(1)} %collective-permute-done.6.refs_1_), channel_id=1, source_target_pairs={{0,1},{1,0},{2,3},{3,2},{4,5},{5,4},{6,7},{7,6},{8,9},{9,8},{10,11... | collective-permute-start | bytes 393224 | tf_op jit(solution)/shard_map/ppermute | solution.py:390

commit v5 on v4

--- a/solution.py
+++ b/solution.py
@@ -19,9 +19,10 @@
 
 CHUNK = 256
 EDGE = 128
+ORDER = (3, 7, 6, 5, 1, 0, 4, 2)
 VMEM = pl.BlockSpec(memory_space=pltpu.VMEM)
 LIMIT = 16 * 1024 * 1024
-WHOLE = 60 * 1024 * 1024
+STAGE_FLOPS = 1
 HBM = pl.BlockSpec(memory_space=pltpu.HBM)
 
 
@@ -50,6 +51,10 @@
     row = np.arange(K)[:, None]
     column = np.arange(K)[None, :]
     return (np.abs(row - column) <= WH).astype(np.float32).astype(jnp.bfloat16)
+
+
+def order_of(chans):
+    return ORDER if chans == len(ORDER) else tuple(range(chans))
 
 
 def iota(shape, dim):
@@ -73,110 +78,162 @@
     return jnp.max(hit, axis=1, keepdims=True)
 
 
-def pack_kernel(
-    cw, rec_hbm, src_hbm, dead_hbm,
-    out_ref, *refs,
+def pack_kernel(cw, rec_hbm, src_hbm, out_ref, *refs):
+    *low_refs, high_ref, src_ref, pick_ref, sem = refs
+    windows, groups, width, span = rec_hbm.shape
+    per = groups // out_ref.shape[0]
+    order = order_of(out_ref.shape[0])
+    brought = pltpu.make_async_copy(src_hbm, src_ref, sem.at[windows, 0])
+    brought.start()
+    copies = []
+    for w in range(windows):
+        copies.append(
+            [
+                pltpu.make_async_copy(
+                    rec_hbm.at[w, pl.ds(member * per, per)], out_ref.at[n, w], sem.at[w, n]
+                )
+                for n, member in enumerate(order)
+            ]
+        )
+        for copy in copies[-1]:
+            copy.start()
+    reps = cw // width
+    rep = lax.axis_index("rep")
+    count = src_ref.shape[1]
+    quarter = count // reps
+    local = groups * width
+    place = iota((count, local), 1)
+    ids = (place // width) * cw + rep * width + place % width
+    brought.wait()
+    wide = jnp.concatenate([columns_of(src_ref[...])] * (local // 128), axis=1)
+    onehot = jnp.where(wide == ids, 1.0, 0.0).astype(jnp.bfloat16)
+    for w in range(windows):
+        for copy in copies[w]:
+            copy.wait()
+        rows = jnp.concatenate(
+            [out_ref[order.index(g // per), w, g % per] for g in range(groups)], axis=0
+        )
+        pick_ref[...] = jnp.dot(onehot, rows, preferred_element_type=jnp.float32)
+        for flip in range(reps):
+            first = pl.multiple_of((rep ^ flip) * quarter, quarter)
+            picked = pick_ref[pl.ds(first, quarter), :].astype(jnp.bfloat16)
+            if flip < reps // 2:
+                low_refs[flip][w] = picked
+            else:
+                high_ref[flip - reps // 2, w] = picked
+
+
+def in_hbm(*arrays):
+    return [pltpu.with_memory_space_constraint(array, pltpu.HBM) for array in arrays]
+
+
+def pack(records, sources, chans, reps):
+    windows, groups, width, span = records.shape
+    count = sources.shape[0]
+    per = groups // chans
+    part = (windows, count // reps, span)
+    return pl.pallas_call(
+        functools.partial(pack_kernel, width * reps),
+        out_shape=(
+            jax.ShapeDtypeStruct((chans, windows, per, width, span), jnp.bfloat16),
+            *[jax.ShapeDtypeStruct(part, jnp.bfloat16)] * (reps // 2),
+            jax.ShapeDtypeStruct((reps // 2,) + part, jnp.bfloat16),
+        ),
+        in_specs=[HBM] * 2,
+        out_specs=(VMEM,) * (reps // 2 + 2),
+        scratch_shapes=[
+            pltpu.VMEM((1, count), jnp.int32),
+            pltpu.VMEM((count, span), jnp.float32),
+            pltpu.SemaphoreType.DMA((1 + windows, chans)),
+        ],
+        compiler_params=pltpu.CompilerParams(vmem_limit_bytes=LIMIT),
+        name="pack",
+    )(*in_hbm(records, sources.reshape(1, count)))
+
+
+def stage_kernel(
+    cw, width, table_hbm, src_hbm, dead_hbm, after_hbm,
+    table_ref, live_ref, source_live_ref, scale_ref,
+    src_ref, dead_ref, pick_ref, sem,
 ):
-    part_refs = refs[:-8]
-    live_ref, source_live_ref, scale_ref, rec_ref, src_ref, dead_ref, pick_ref, sem = refs[-8:]
     copies = [
         pltpu.make_async_copy(src_hbm, src_ref, sem.at[0]),
         pltpu.make_async_copy(dead_hbm, dead_ref, sem.at[1]),
+        pltpu.make_async_copy(table_hbm, table_ref, sem.at[2]),
     ]
-    windows, groups, width, span = rec_ref.shape
-    per = groups // out_ref.shape[0]
-    brought = [
-        pltpu.make_async_copy(rec_hbm.at[w], rec_ref.at[w], sem.at[2 + w]) for w in range(windows)
-    ]
-    for copy in copies + brought:
+    for copy in copies:
         copy.start()
-    reps = cw // width
+    windows = dead_ref.shape[0]
     rep, chan = lax.axis_index("rep"), lax.axis_index("chan")
     count = src_ref.shape[1]
-    quarter = count // reps
+    quarter, columns = scale_ref.shape
+    per = columns // cw
     here = pl.ds(pl.multiple_of(rep * quarter, quarter), quarter)
-    copies[0].wait()
-    column = columns_of(src_ref[...])
-    local = groups * width
-    place = iota((count, local), 1)
-    ids = (place // width) * cw + rep * width + place % width
-    wide = jnp.concatenate([column] * (local // 128), axis=1)
-    onehot = jnp.where(wide == ids, 1.0, 0.0).astype(jnp.bfloat16)
-    copies[1].wait()
     row = iota((per * width, 1), 0)
     row_ids = (chan * per + row // width) * cw + rep * width + row % width
-    block_ids = chan * per * cw + iota((1, per * cw), 1)
-    pairs = jnp.zeros((count, per * cw), jnp.float32)
+    block_ids = chan * columns + iota((1, columns), 1)
+    copies[0].wait()
+    copies[1].wait()
+    column = columns_of(src_ref[...])
+    pick_ref[...] = column
+    mine = pick_ref[here, :]
+    pairs = jnp.zeros((quarter, columns), jnp.float32)
     for w in range(windows):
         dead = dead_ref[w : w + 1, :]
         live_ref[w * per * width : (w + 1) * per * width, :] = 1.0 - listed(row_ids, dead)
-        source_live = 1.0 - listed(column, dead)
-        pick_ref[:, :1] = source_live
-        source_live_ref[w * quarter : (w + 1) * quarter, :] = pick_ref[here, :1]
+        source_live = 1.0 - listed(mine, dead)
+        source_live_ref[w * quarter : (w + 1) * quarter, :] = source_live
         dead_column = columns_of(dead)
         hits = [
             jnp.max(
                 jnp.where(dead_column == block_ids[:, i : i + 128], 1.0, 0.0), axis=0, keepdims=True
             )
-            for i in range(0, per * cw, 128)
+            for i in range(0, columns, 128)
         ]
         pairs += source_live * (1.0 - jnp.concatenate(hits, axis=1))
-    for i in range(0, per * cw, span):
-        pick_ref[:, : min(span, per * cw)] = pairs[:, i : i + span]
-        scale_ref[:, i : i + span] = 1.0 / (
-            math.sqrt(K) * jnp.maximum(pick_ref[here, : min(span, per * cw)], 1.0)
-        )
-    for w in range(windows):
-        brought[w].wait()
-        for g in range(groups):
-            out_ref[g // per, w, g % per] = rec_ref[w, g]
-    for w in range(windows):
-        rows = rec_ref[w].reshape(local, span)
-        pick_ref[...] = jnp.dot(onehot, rows, preferred_element_type=jnp.float32)
-        for flip, ref in enumerate(part_refs):
-            first = pl.multiple_of((rep ^ flip) * quarter, quarter)
-            ref[w] = pick_ref[pl.ds(first, quarter), :].astype(jnp.bfloat16)
-
-
-def pack(records, sources, dead_list, chans, reps):
-    records, sources, dead_list = [pltpu.with_memory_space_constraint(a, pltpu.HBM) for a in (records, sources.reshape(1, -1), dead_list)]
-    windows, groups, width, span = records.shape
-    count = sources.shape[1]
-    per = groups // chans
-    part = jax.ShapeDtypeStruct((windows, count // reps, span), jnp.bfloat16)
-    return pl.pallas_call(
-        functools.partial(pack_kernel, width * reps),
+    scale_ref[...] = 1.0 / (math.sqrt(K) * jnp.maximum(pairs, 1.0))
+    copies[2].wait()
+
+
+def stage(table, sources, dead_list, after, per, cw, width):
+    windows = dead_list.shape[0]
+    count = sources.shape[0]
+    quarter = count // (cw // width)
+    return pl.pallas_call(
+        functools.partial(stage_kernel, cw, width),
         out_shape=(
-            jax.ShapeDtypeStruct((chans, windows, per, width, span), jnp.bfloat16),
-            *[part] * reps,
+            jax.ShapeDtypeStruct(table.shape, table.dtype),
             jax.ShapeDtypeStruct((windows * per * width, 1), jnp.float32),
-            jax.ShapeDtypeStruct((windows * count // reps, 1), jnp.float32),
-            jax.ShapeDtypeStruct((count // reps, per * width * reps), jnp.float32),
+            jax.ShapeDtypeStruct((windows * quarter, 1), jnp.float32),
+            jax.ShapeDtypeStruct((quarter, per * cw), jnp.float32),
         ),
-        in_specs=[HBM] * 3,
-        out_specs=(VMEM,) * (reps + 4),
+        in_specs=[HBM] * 3 + [pl.BlockSpec(memory_space=pl.ANY)],
+        out_specs=(VMEM,) * 4,
         scratch_shapes=[
-            pltpu.VMEM(records.shape, jnp.bfloat16),
             pltpu.VMEM((1, count), jnp.int32),
             pltpu.VMEM(dead_list.shape, jnp.int32),
-            pltpu.VMEM((count, span), jnp.float32),
-            pltpu.SemaphoreType.DMA((2 + windows,)),
+            pltpu.VMEM((count, 128), jnp.int32),
+            pltpu.SemaphoreType.DMA((3,)),
         ],
         compiler_params=pltpu.CompilerParams(vmem_limit_bytes=LIMIT),
-        name="pack",
-    )(records, sources, dead_list)
-
-
-def whiten_rows(x_ref, ext_ref, table_ref, band_ref, bins_ref):
+        cost_estimate=pl.CostEstimate(
+            flops=STAGE_FLOPS, bytes_accessed=4 << 20, transcendentals=0
+        ),
+        name="stage",
+    )(*in_hbm(table, sources.reshape(1, count), dead_list), after)
+
+
+def whiten_rows(x_ref, order, ext_ref, table_ref, band_ref, bins_ref):
     pieces, rows, _ = x_ref.shape
+    x = [x_ref.at[order.index(i)] for i in range(pieces)]
     length = pieces * CHUNK
     for i in range(pieces):
         here = pl.ds(i * rows, rows)
-        ext_ref[here, EDGE : EDGE + CHUNK] = jnp.abs(x_ref[i])
+        ext_ref[here, EDGE : EDGE + CHUNK] = jnp.abs(x[i][...])
         blank = jnp.zeros((rows, EDGE), jnp.bfloat16)
-        ext_ref[here, :EDGE] = jnp.abs(x_ref[i - 1, :, CHUNK - EDGE :]) if i else blank
+        ext_ref[here, :EDGE] = jnp.abs(x[i - 1][:, CHUNK - EDGE :]) if i else blank
         ext_ref[here, EDGE + CHUNK :] = (
-            jnp.abs(x_ref[i + 1, :, :EDGE]) if i < pieces - 1 else blank
+            jnp.abs(x[i + 1][:, :EDGE]) if i < pieces - 1 else blank
         )
     totals = jnp.dot(ext_ref[...], band_ref[...], preferred_element_type=jnp.float32)
     spectrum = jnp.zeros((rows, 2 * K), jnp.float32)
@@ -184,7 +241,7 @@
         sample = iota((1, CHUNK), 1) + i * CHUNK
         counts = jnp.minimum(sample, HALF) + jnp.minimum(length - 1 - sample, HALF) + 1
         mean = totals[i * rows : (i + 1) * rows] * (1.0 / counts.astype(jnp.float32))
-        normed = (x_ref[i].astype(jnp.float32) / (mean + EPS)).astype(jnp.bfloat16)
+        normed = (x[i][...].astype(jnp.float32) / (mean + EPS)).astype(jnp.bfloat16)
         spectrum += jnp.dot(
             normed, table_ref[i * CHUNK : (i + 1) * CHUNK, :], preferred_element_type=jnp.float32
         )
@@ -205,19 +262,19 @@
     return real_part * scale, imag_part * scale
 
 
-def channel_kernel(x_ref, live_ref, table_ref, band_ref, bins_ref, out_ref, ext_ref):
+def channel_kernel(order, x_ref, live_ref, table_ref, band_ref, bins_ref, out_ref, ext_ref):
     windows, count, _ = out_ref.shape
-    real_part, imag_part = whiten_rows(x_ref, ext_ref, table_ref, band_ref, bins_ref)
+    real_part, imag_part = whiten_rows(x_ref, order, ext_ref, table_ref, band_ref, bins_ref)
     for w in range(windows):
         here = slice(w * count, (w + 1) * count)
         out_ref[w, :, :K] = (real_part[here] * live_ref[here, :]).astype(jnp.bfloat16)
         out_ref[w, :, K:] = (imag_part[here] * live_ref[here, :]).astype(jnp.bfloat16)
 
 
-def channel_spectra(x, live, tables, windows):
+def channel_spectra(x, order, live, tables, windows):
     pieces, rows, _ = x.shape
     return pl.pallas_call(
-        channel_kernel,
+        functools.partial(channel_kernel, order),
         out_shape=jax.ShapeDtypeStruct((windows, rows // windows, 2 * K), jnp.bfloat16),
         in_specs=[VMEM] * 5,
         out_specs=VMEM,
@@ -238,7 +295,8 @@
     for part, slots in zip(parts, keys):
         for n, key in enumerate(slots):
             x_ref[chan ^ key if key is not None else n] = part[n]
-    real_part, imag_part = whiten_rows(x_ref, ext_ref, table_ref, band_ref, bins_ref)
+    order = tuple(range(x_ref.shape[0]))
+    real_part, imag_part = whiten_rows(x_ref, order, ext_ref, table_ref, band_ref, bins_ref)
     out_ref[:, :K] = (real_part * live_ref[...]).astype(jnp.bfloat16)
     out_ref[:, K:] = (imag_part * live_ref[...]).astype(jnp.bfloat16)
 
@@ -291,25 +349,6 @@
         cost_estimate=pl.CostEstimate(flops=1 << 34, bytes_accessed=8 << 20, transcendentals=0),
         name="lag_kernels",
     )(spec, jnp.asarray(cosine), jnp.asarray(sine))
-
-
-def merge_kernel(*refs):
-    total = refs[0][...]
-    for ref in refs[1:-1]:
-        total = total + ref[...]
-    refs[-1][...] = total
-
-
-def merge(parts):
-    return pl.pallas_call(
-        merge_kernel,
-        out_shape=jax.ShapeDtypeStruct(parts[0].shape, parts[0].dtype),
-        in_specs=[VMEM] * len(parts),
-        out_specs=VMEM,
-        compiler_params=pltpu.CompilerParams(vmem_limit_bytes=LIMIT),
-        cost_estimate=pl.CostEstimate(flops=1, bytes_accessed=1, transcendentals=0),
-        name="merge",
-    )(*parts)
 
 
 def correlate_kernel(flips, cw, *refs):
@@ -366,25 +405,6 @@
     )(*parts, left, scale)
 
 
-def stage_kernel(table_hbm, after_hbm, out_ref, sem):
-    copy = pltpu.make_async_copy(table_hbm, out_ref, sem)
-    copy.start()
-    copy.wait()
-
-
-def stage(table, after):
-    return pl.pallas_call(
-        stage_kernel,
-        out_shape=jax.ShapeDtypeStruct(table.shape, table.dtype),
-        in_specs=[HBM, pl.BlockSpec(memory_space=pl.ANY)],
-        out_specs=VMEM,
-        scratch_shapes=[pltpu.SemaphoreType.DMA(())],
-        compiler_params=pltpu.CompilerParams(vmem_limit_bytes=LIMIT),
-        cost_estimate=pl.CostEstimate(flops=1, bytes_accessed=4 << 20, transcendentals=0),
-        name="stage",
-    )(table, after)
-
-
 def swap(x, axis, flip):
     size = lax.axis_size(axis)
     return lax.ppermute(x, axis, [(i, i ^ flip) for i in range(size)])
@@ -398,11 +418,19 @@
     return jnp.transpose(joined, (1, 0, 2))
 
 
-def gather_sources(given, table):
+def gather_sources(low, high, prepare):
     chans, chan = lax.axis_size("chan"), lax.axis_index("chan")
-    windows, quarter, span = given[0].shape
-    mine = merge([swap(part, "rep", flip) if flip else part for flip, part in enumerate(given)])
-    table = stage(table, mine)
+    windows, quarter, span = low[0].shape
+    flip = len(low)
+    while flip:
+        came = swap(high, "rep", flip)
+        low = [part + came[n] for n, part in enumerate(low)]
+        flip //= 2
+        if flip:
+            high = jnp.stack(low[flip:])
+            low = low[:flip]
+    mine = low[0]
+    prepared = prepare(mine)
     held = mine.reshape(1, windows * quarter, span)
     near = min(4, chans // 2)
     keys = list(range(near))
@@ -412,15 +440,15 @@
         held = jnp.concatenate([held, swap(held, "chan", flip)], axis=0)
         keys = keys + [key ^ flip for key in keys]
         flip *= 2
-    held, table = lax.optimization_barrier((held, table))
+    held, prepared = lax.optimization_barrier((held, prepared))
     other = swap(held, "chan", flip)
     if span == CHUNK:
-        return table, (held, other), (tuple(keys), tuple(key ^ flip for key in keys))
+        return prepared, (held, other), (tuple(keys), tuple(key ^ flip for key in keys))
     every = jnp.concatenate([held, other], axis=0)
     keys = jnp.asarray(keys + [key ^ flip for key in keys], jnp.int32)
     every = jnp.zeros_like(every).at[chan ^ keys].set(every)
     every = regroup(every)
-    return table, (every,), ((None,) * every.shape[0],)
+    return prepared, (every,), ((None,) * every.shape[0],)
 
 
 def shards(records, sources, dead_list):
@@ -428,19 +456,26 @@
     reps, chans = lax.axis_size("rep"), lax.axis_size("chan")
     cw = width * reps
     per = groups // chans
-    blocks, *given, live, source_live, scale = pack(records, sources, dead_list, chans, reps)
+    blocks, *low, high = pack(records, sources, chans, reps)
     blocks = blocks.reshape(chans, windows * per * width, span)
-    arrived = regroup(lax.all_to_all(blocks, "chan", 0, 0, tiled=True))
-    table, parts, keys = gather_sources(given, jnp.asarray(dft_table(chans * span)))
+    order = order_of(chans)
+    arrived = lax.all_to_all(blocks, "chan", 0, 0, axis_index_groups=[list(order)], tiled=True)
+    if span != CHUNK:
+        arrived = regroup(jnp.stack([arrived[order.index(i)] for i in range(chans)]))
+        order = tuple(range(arrived.shape[0]))
+    table = jnp.asarray(dft_table(chans * span))
+
+    def prepare(after):
+        return stage(table, sources, dead_list, after, per, cw, width)
+
+    (table, live, source_live, scale), parts, keys = gather_sources(low, high, prepare)
     tables = [table, jnp.asarray(sample_band()), jnp.asarray(bin_band())]
-    spectra = channel_spectra(arrived, live, tables, windows)
+    spectra = channel_spectra(arrived, order, live, tables, windows)
     source_spec = source_spectra(parts, keys, source_live, tables)
     pieces, flips = [spectra], [0]
     flip = reps // 2
     while flip:
         others = [swap(piece, "rep", flip) for piece in pieces]
-        if flip > 1:
-            others, source_spec = lax.optimization_barrier((others, source_spec))
         pieces = pieces + others
         flips = flips + [f ^ flip for f in flips]
         flip //= 2

time: 35.9 us -> 35.1 us (0.978)
  Pallas kernels: 7.76 us -> 9.43 us
  starting transfers between devices: 17.9 us -> 16.3 us
  local copies, waits for them, and re-layouts: 1.61 us -> 0.02 us
  waiting for transfers between devices: 8.32 us -> 8.97 us
    ppermute x10 -> x9, starting transfers between devices: 10.6 us -> 8.43 us  [swap(): return lax.ppermute(x, axis, [(i, i ^ flip) for i in range(size)])]
    unnamed x10 -> x8, local copies, waits for them, and re-layouts: 1.61 us -> 0.02 us
    pallas_call x3 -> x2, Pallas kernels: 1.47 us -> 2.96 us  [the longest x1 1.65 us: stage(): pl.pallas_call(functools.partial(stage_kernel, cw, width), out_shape=(jax...]
    ppermute x10 -> x9, waiting for transfers between devices: 8.32 us -> 8.97 us  [swap(): return lax.ppermute(x, axis, [(i, i ^ flip) for i in range(size)])]
    all_to_all x1, starting transfers between devices: 7.29 us -> 7.85 us  [shards(): lax.all_to_all(blocks, 'chan', 0, 0, axis_index_groups=[list(order)], til...]
  transfers between devices with their start and end apart: 11 -> 10, of which waited for: 6 -> 5; matrix products, arithmetic and copies ran while one was open for 0% -> 0% of each run, Pallas kernels for 10% -> 14%
where the time goes in v5:
time: 35.1 us; the launch traced here: 34.8 us
  starting transfers between devices  16.3 us (46%)
  Pallas kernels  9.43 us (27%)
  waiting for transfers between devices  8.97 us (26%)
    ppermute x9, waiting for transfers between devices, swap(): return lax.ppermute(x, axis, [(i, i ^ flip) for i in range(size)])  8.97 us
    ppermute x9, starting transfers between devices, swap(): return lax.ppermute(x, axis, [(i, i ^ flip) for i in range(size)])  8.43 us
    all_to_all x1, starting transfers between devices, shards(): lax.all_to_all(blocks, 'chan', 0, 0, axis_index_groups=[list(order)], til...  7.85 us
    pallas_call x1, Pallas kernels, correlate(): pl.pallas_call(functools.partial(correlate_kernel, flips, cw), out_shape=...  2.25 us
    pallas_call x1, Pallas kernels, pack(): pl.pallas_call(functools.partial(pack_kernel, width * reps), out_shape=(j...  2.19 us
    pallas_call x1, Pallas kernels, stage(): pl.pallas_call(functools.partial(stage_kernel, cw, width), out_shape=(jax...  1.65 us
    pallas_call x1, Pallas kernels, channel_spectra(): pl.pallas_call(functools.partial(channel_kernel, order), out_shape=jax.Sh...  1.31 us
    pallas_call x1, Pallas kernels, source_spectra(): pl.pallas_call(functools.partial(source_kernel, keys), out_shape=jax.Shap...  1.04 us
  transfers between devices with their start and end apart: 10, of which 5 were waited for; matrix products, arithmetic and copies ran while one was open for 0% of the time, Pallas kernels for 14%

profile of v5, /device:TPU:0, one launch (start us, length us, event | category | flops | bytes accessed | tf_op | source)
XLA Modules:
  0.0 34.8 jit_solution(17025681581810494677)
XLA Ops:
  0.0 0.0 copy-start
  0.0 0.0 copy-start.1
  0.0 2.2 %pack.1 = (bf16[8,2,1,64,256]{4,3,2,1,0:T(8,128)(2,1)}, bf16[2,32,256]{2,1,0:T(8,128)(2,1)S(1)}, bf16[2,32,256]{2,1,0:T(8,128)(2,1)S(1)}, bf16[2,2,32,256]{3,2,1,0:T(8,128)(2,1)S(1)}) custom-call(bf16[2,8,64,256]{3,2,1,0:T(8,128)(2,1)} %rec_hbm.1, s32[1,128]{1,0:T(1,128)} %bitcast.23), custom_call_target="tpu_custom_call" | custom-call | tf_op jit(solution)/shard_map/pack/pallas_call | solution.py:135
  2.2 7.9 %all-to-all-start = ((bf16[8,128,256]{2,1,0:T(8,128)(2,1)}), bf16[8,128,256]{2,1,0:T(8,128)(2,1)S(1)}, u32[]{:S(2)}, u32[]{:S(2)}) async-start(bf16[8,128,256]{2,1,0:T(8,128)(2,1)} %bitcast.1), calls=%async_computation | async-start | bytes 1048576 | tf_op jit(solution)/shard_map/all_to_all | solution.py:462
  10.1 1.5 %collective-permute-start = (bf16[2,2,32,256]{3,2,1,0:T(8,128)(2,1)S(1)}, bf16[2,2,32,256]{3,2,1,0:T(8,128)(2,1)S(1)}, u32[]{:S(2)}, u32[]{:S(2)}) collective-permute-start(bf16[2,2,32,256]{3,2,1,0:T(8,128)(2,1)S(1)} %get-tuple-element.20), channel_id=1, source_target_pairs={{0,2},{1,3},{2,0},{3,1},{4,6},{5,7},{6,4},{7,5},{8,10},{9,11},{10,... | collective-permute-start | bytes 196616 | tf_op jit(solution)/shard_map/ppermute | solution.py:410
  11.5 2.8 %collective-permute-done = bf16[2,2,32,256]{3,2,1,0:T(8,128)(2,1)S(1)} collective-permute-done((bf16[2,2,32,256]{3,2,1,0:T(8,128)(2,1)S(1)}, bf16[2,2,32,256]{3,2,1,0:T(8,128)(2,1)S(1)}, u32[]{:S(2)}, u32[]{:S(2)}) %collective-permute-start) | collective-permute-done | bytes 65568 | tf_op jit(solution)/shard_map/ppermute | solution.py:410
  14.3 0.0 collective-permute-start.1
  14.3 1.2 %collective-permute-done.1 = bf16[1,2,32,256]{3,2,1,0:T(8,128)(2,1)S(1)} collective-permute-done((bf16[1,2,32,256]{3,2,1,0:T(8,128)(2,1)S(1)}, bf16[1,2,32,256]{3,2,1,0:T(8,128)(2,1)S(1)}, u32[]{:S(2)}, u32[]{:S(2)}) %collective-permute-start.1) | collective-permute-done | bytes 32800 | tf_op jit(solution)/shard_map/ppermute | solution.py:410
  15.5 0.1 collective-permute-start.4
  15.6 2.0 %collective-permute-start.3 = (bf16[1,64,256]{2,1,0:T(8,128)(2,1)S(1)}, bf16[1,64,256]{2,1,0:T(8,128)(2,1)S(1)}, u32[]{:S(2)}, u32[]{:S(2)}) collective-permute-start(bf16[1,64,256]{2,1,0:T(8,128)(2,1)S(1)} %bitcast.20), channel_id=1, source_target_pairs={{0,8},{4,12},{8,0},{12,4},{16,24},{20,28},{24,16},{28,20},{1,9},{5... | collective-permute-start | bytes 98312 | tf_op jit(solution)/shard_map/ppermute | solution.py:410
  17.6 1.5 %collective-permute-start.2 = (bf16[1,64,256]{2,1,0:T(8,128)(2,1)S(1)}, bf16[1,64,256]{2,1,0:T(8,128)(2,1)S(1)}, u32[]{:S(2)}, u32[]{:S(2)}) collective-permute-start(bf16[1,64,256]{2,1,0:T(8,128)(2,1)S(1)} %bitcast.21), channel_id=1, source_target_pairs={{0,4},{4,0},{8,12},{12,8},{16,20},{20,16},{24,28},{28,24},{1,5},{5... | collective-permute-start | bytes 98312 | tf_op jit(solution)/shard_map/ppermute | solution.py:410
  19.1 1.6 %stage.1 = (bf16[2048,512]{1,0:T(8,128)(2,1)S(1)}, f32[128,1]{1,0:T(8,128)S(1)}, f32[64,1]{1,0:T(8,128)S(1)}, f32[32,256]{1,0:T(8,128)S(1)}) custom-call(bf16[2048,512]{1,0:T(8,128)(2,1)} %constant.10.clone.table_hbm, s32[1,128]{1,0:T(1,128)} %bitcast.24, s32[2,128]{1,0:T(2,128)} %dead_hbm.1, bf16[2,32,256]{2,1,0:T(8,128)(2,1)S(1)} %fusion.3.after_hbm), custom_call_target="tpu_custom_call" | custom-call | flops 1 | bytes 4194304 | tf_op jit(solution)/shard_map/stage/pallas_call | solution.py:202
  20.8 0.1 collective-permute-done.4
  20.9 0.0 collective-permute-done.3
  20.9 1.2 %collective-permute-done.2 = bf16[1,64,256]{2,1,0:T(8,128)(2,1)S(1)} collective-permute-done((bf16[1,64,256]{2,1,0:T(8,128)(2,1)S(1)}, bf16[1,64,256]{2,1,0:T(8,128)(2,1)S(1)}, u32[]{:S(2)}, u32[]{:S(2)}) %collective-permute-start.2) | collective-permute-done | bytes 32800 | tf_op jit(solution)/shard_map/ppermute | solution.py:410
  22.1 1.3 %collective-permute-start.8 = (bf16[4,64,256]{2,1,0:T(8,128)(2,1)S(1)}, bf16[4,64,256]{2,1,0:T(8,128)(2,1)S(1)}, u32[]{:S(2)}, u32[]{:S(2)}) collective-permute-start(bf16[4,64,256]{2,1,0:T(8,128)(2,1)S(1)} %pad_maximum_fusion.refs_0_), channel_id=1, source_target_pairs={{0,16},{4,20},{8,24},{12,28},{16,0},{20,4},{24,8},{28,12},{1,17},{... | collective-permute-start | bytes 393224 | tf_op jit(solution)/shard_map/ppermute | solution.py:410
  23.4 0.0 all-to-all-done.x_ref
  23.4 0.0 copy-done
  23.4 0.0 copy-done.1
  23.4 1.3 %channel_spectra.1.refs_0_ = bf16[2,64,512]{2,1,0:T(8,128)(2,1)S(1)} custom-call(bf16[8,128,256]{2,1,0:T(8,128)(2,1)S(1)} %all-to-all-done.x_ref, f32[128,1]{1,0:T(8,128)S(1)} %get-tuple-element.26.live_ref, bf16[2048,512]{1,0:T(8,128)(2,1)S(1)} %get-tuple-element.27.table_ref.refs_3_, bf16[512,256]{1,0:T(8,128)(2,1)S(1)} %copy-done, ...), custom_call_target="tpu_custom_call" | custom-call | flops 1 | bytes 1 | tf_op jit(solution)/shard_map/channel_spectra/pallas_call | solution.py:276
  24.7 0.0 copy-start.2
  24.7 0.0 copy-start.3
  24.7 1.6 %collective-permute-start.5 = (bf16[2,64,512]{2,1,0:T(8,128)(2,1)S(1)}, bf16[2,64,512]{2,1,0:T(8,128)(2,1)S(1)}, u32[]{:S(2)}, u32[]{:S(2)}) collective-permute-start(bf16[2,64,512]{2,1,0:T(8,128)(2,1)S(1)} %channel_spectra.1.refs_0_), channel_id=1, source_target_pairs={{0,2},{1,3},{2,0},{3,1},{4,6},{5,7},{6,4},{7,5},{8,10},{9,11},{10,... | collective-permute-start | bytes 393224 | tf_op jit(solution)/shard_map/ppermute | solution.py:410
  26.3 3.7 %collective-permute-done.8.refs_1_ = bf16[4,64,256]{2,1,0:T(8,128)(2,1)S(1)} collective-permute-done((bf16[4,64,256]{2,1,0:T(8,128)(2,1)S(1)}, bf16[4,64,256]{2,1,0:T(8,128)(2,1)S(1)}, u32[]{:S(2)}, u32[]{:S(2)}) %collective-permute-start.8) | collective-permute-done | bytes 131104 | tf_op jit(solution)/shard_map/ppermute | solution.py:410
  29.9 1.0 %source_spectra.1.spec_ref = bf16[64,512]{1,0:T(8,128)(2,1)S(1)} custom-call(bf16[4,64,256]{2,1,0:T(8,128)(2,1)S(1)} %pad_maximum_fusion.refs_0_, bf16[4,64,256]{2,1,0:T(8,128)(2,1)S(1)} %collective-permute-done.8.refs_1_, f32[64,1]{1,0:T(8,128)S(1)} %get-tuple-element.29.refs_2_, bf16[2048,512]{1,0:T(8,128)(2,1)S(1)} %get-tuple-element.27.table_ref.refs_3_, ...), custom_call_target="tpu_custom_call" | custom-call | flops 17179869184 | bytes 8388608 | tf_op jit(solution)/shard_map/source_spectra/pallas_call | solution.py:307
  31.0 0.1 collective-permute-start.6
  31.1 0.0 collective-permute-done.5.refs_1_
  31.1 0.5 %collective-permute-start.7 = (bf16[2,64,512]{2,1,0:T(8,128)(2,1)S(1)}, bf16[2,64,512]{2,1,0:T(8,128)(2,1)S(1)}, u32[]{:S(2)}, u32[]{:S(2)}) collective-permute-start(bf16[2,64,512]{2,1,0:T(8,128)(2,1)S(1)} %collective-permute-done.5.refs_1_), channel_id=1, source_target_pairs={{0,1},{1,0},{2,3},{3,2},{4,5},{5,4},{6,7},{7,6},{8,9},{9,8},{10,11... | collective-permute-start | bytes 393224 | tf_op jit(solution)/shard_map/ppermute | solution.py:410
  31.6 0.0 copy-done.2
  31.6 0.0 copy-done.3
  31.6 1.0 %lag_kernels.1.refs_4_ = bf16[2048,1024]{1,0:T(8,128)(2,1)S(1)} custom-call(bf16[64,512]{1,0:T(8,128)(2,1)S(1)} %source_spectra.1.spec_ref, f32[64,256]{1,0:T(8,128)S(1)} %copy-done.3, f32[64,256]{1,0:T(8,128)S(1)} %copy-done.2), custom_call_target="tpu_custom_call" | custom-call | flops 17179869184 | bytes 8388608 | tf_op jit(solution)/shard_map/lag_kernels/pallas_call | solution.py:343
  32.6 0.0 collective-permute-done.6.refs_2_
  32.6 0.0 collective-permute-done.7.refs_3_
  32.6 2.2 %correlate.1 = f32[32,64,256]{2,1,0:T(8,128)} custom-call(bf16[2,64,512]{2,1,0:T(8,128)(2,1)S(1)} %channel_spectra.1.refs_0_, bf16[2,64,512]{2,1,0:T(8,128)(2,1)S(1)} %collective-permute-done.5.refs_1_, bf16[2,64,512]{2,1,0:T(8,128)(2,1)S(1)} %collective-permute-done.6.refs_2_, bf16[2,64,512]{2,1,0:T(8,128)(2,1)S(1)} %collective-permute-done.7.refs_3_, ...), custom_call_target="tpu_custom_call" | custom-call | tf_op jit(solution)/shard_map/correlate/pallas_call | solution.py:393
  (3 shorter events, 0.0 us)
Async XLA Ops:
  0.0 23.4 %copy-start = (bf16[512,256]{1,0:T(8,128)(2,1)S(1)}, bf16[512,256]{1,0:T(8,128)(2,1)}, u32[]{:S(2)}) copy-start(bf16[512,256]{1,0:T(8,128)(2,1)} %constant.11.clone.band_ref.refs_4_) | copy-start | bytes 786436
  0.0 23.4 %copy-start.1 = (bf16[256,256]{1,0:T(8,128)(2,1)S(1)}, bf16[256,256]{1,0:T(8,128)(2,1)}, u32[]{:S(2)}) copy-start(bf16[256,256]{1,0:T(8,128)(2,1)} %constant.12.clone.bins_ref.refs_5_) | copy-start | bytes 393220
  2.2 21.2 %all-to-all-start = ((bf16[8,128,256]{2,1,0:T(8,128)(2,1)}), bf16[8,128,256]{2,1,0:T(8,128)(2,1)S(1)}, u32[]{:S(2)}, u32[]{:S(2)}) async-start(bf16[8,128,256]{2,1,0:T(8,128)(2,1)} %bitcast.1), calls=%async_computation | async-start | bytes 1048576 | tf_op jit(solution)/shard_map/all_to_all | solution.py:462
  10.1 4.3 %collective-permute-start = (bf16[2,2,32,256]{3,2,1,0:T(8,128)(2,1)S(1)}, bf16[2,2,32,256]{3,2,1,0:T(8,128)(2,1)S(1)}, u32[]{:S(2)}, u32[]{:S(2)}) collective-permute-start(bf16[2,2,32,256]{3,2,1,0:T(8,128)(2,1)S(1)} %get-tuple-element.20), channel_id=1, source_target_pairs={{0,2},{1,3},{2,0},{3,1},{4,6},{5,7},{6,4},{7,5},{8,10},{9,11},{10,... | collective-permute-start | bytes 196616 | tf_op jit(solution)/shard_map/ppermute | solution.py:410
  14.3 1.2 %collective-permute-start.1 = (bf16[1,2,32,256]{3,2,1,0:T(8,128)(2,1)S(1)}, bf16[1,2,32,256]{3,2,1,0:T(8,128)(2,1)S(1)}, u32[]{:S(2)}, u32[]{:S(2)}) collective-permute-start(bf16[1,2,32,256]{3,2,1,0:T(8,128)(2,1)S(1)} %fusion.1), channel_id=1, source_target_pairs={{0,1},{1,0},{2,3},{3,2},{4,5},{5,4},{6,7},{7,6},{8,9},{9,8},{10,11... | collective-permute-start | bytes 98312 | tf_op jit(solution)/shard_map/ppermute | solution.py:410
  15.5 5.3 %collective-permute-start.4 = (bf16[1,64,256]{2,1,0:T(8,128)(2,1)S(1)}, bf16[1,64,256]{2,1,0:T(8,128)(2,1)S(1)}, u32[]{:S(2)}, u32[]{:S(2)}) collective-permute-start(bf16[1,64,256]{2,1,0:T(8,128)(2,1)S(1)} %bitcast.19), channel_id=1, source_target_pairs={{0,12},{4,8},{8,4},{12,0},{16,28},{20,24},{24,20},{28,16},{1,13},{... | collective-permute-start | bytes 98312 | tf_op jit(solution)/shard_map/ppermute | solution.py:410
  15.6 5.3 %collective-permute-start.3 = (bf16[1,64,256]{2,1,0:T(8,128)(2,1)S(1)}, bf16[1,64,256]{2,1,0:T(8,128)(2,1)S(1)}, u32[]{:S(2)}, u32[]{:S(2)}) collective-permute-start(bf16[1,64,256]{2,1,0:T(8,128)(2,1)S(1)} %bitcast.20), channel_id=1, source_target_pairs={{0,8},{4,12},{8,0},{12,4},{16,24},{20,28},{24,16},{28,20},{1,9},{5... | collective-permute-start | bytes 98312 | tf_op jit(solution)/shard_map/ppermute | solution.py:410
  17.6 4.4 %collective-permute-start.2 = (bf16[1,64,256]{2,1,0:T(8,128)(2,1)S(1)}, bf16[1,64,256]{2,1,0:T(8,128)(2,1)S(1)}, u32[]{:S(2)}, u32[]{:S(2)}) collective-permute-start(bf16[1,64,256]{2,1,0:T(8,128)(2,1)S(1)} %bitcast.21), channel_id=1, source_target_pairs={{0,4},{4,0},{8,12},{12,8},{16,20},{20,16},{24,28},{28,24},{1,5},{5... | collective-permute-start | bytes 98312 | tf_op jit(solution)/shard_map/ppermute | solution.py:410
  22.1 7.9 %collective-permute-start.8 = (bf16[4,64,256]{2,1,0:T(8,128)(2,1)S(1)}, bf16[4,64,256]{2,1,0:T(8,128)(2,1)S(1)}, u32[]{:S(2)}, u32[]{:S(2)}) collective-permute-start(bf16[4,64,256]{2,1,0:T(8,128)(2,1)S(1)} %pad_maximum_fusion.refs_0_), channel_id=1, source_target_pairs={{0,16},{4,20},{8,24},{12,28},{16,0},{20,4},{24,8},{28,12},{1,17},{... | collective-permute-start | bytes 393224 | tf_op jit(solution)/shard_map/ppermute | solution.py:410
  24.7 6.9 %copy-start.2 = (f32[64,256]{1,0:T(8,128)S(1)}, f32[64,256]{1,0:T(8,128)}, u32[]{:S(2)}) copy-start(f32[64,256]{1,0:T(8,128)} %constant.14.clone.sin_ref) | copy-start | bytes 196612
  24.7 6.9 %copy-start.3 = (f32[64,256]{1,0:T(8,128)S(1)}, f32[64,256]{1,0:T(8,128)}, u32[]{:S(2)}) copy-start(f32[64,256]{1,0:T(8,128)} %constant.13.clone.cos_ref) | copy-start | bytes 196612
  24.7 6.4 %collective-permute-start.5 = (bf16[2,64,512]{2,1,0:T(8,128)(2,1)S(1)}, bf16[2,64,512]{2,1,0:T(8,128)(2,1)S(1)}, u32[]{:S(2)}, u32[]{:S(2)}) collective-permute-start(bf16[2,64,512]{2,1,0:T(8,128)(2,1)S(1)} %channel_spectra.1.refs_0_), channel_id=1, source_target_pairs={{0,2},{1,3},{2,0},{3,1},{4,6},{5,7},{6,4},{7,5},{8,10},{9,11},{10,... | collective-permute-start | bytes 393224 | tf_op jit(solution)/shard_map/ppermute | solution.py:410
  31.0 1.6 %collective-permute-start.6 = (bf16[2,64,512]{2,1,0:T(8,128)(2,1)S(1)}, bf16[2,64,512]{2,1,0:T(8,128)(2,1)S(1)}, u32[]{:S(2)}, u32[]{:S(2)}) collective-permute-start(bf16[2,64,512]{2,1,0:T(8,128)(2,1)S(1)} %channel_spectra.1.refs_0_), channel_id=1, source_target_pairs={{0,1},{1,0},{2,3},{3,2},{4,5},{5,4},{6,7},{7,6},{8,9},{9,8},{10,11... | collective-permute-start | bytes 393224 | tf_op jit(solution)/shard_map/ppermute | solution.py:410
  31.1 1.5 %collective-permute-start.7 = (bf16[2,64,512]{2,1,0:T(8,128)(2,1)S(1)}, bf16[2,64,512]{2,1,0:T(8,128)(2,1)S(1)}, u32[]{:S(2)}, u32[]{:S(2)}) collective-permute-start(bf16[2,64,512]{2,1,0:T(8,128)(2,1)S(1)} %collective-permute-done.5.refs_1_), channel_id=1, source_target_pairs={{0,1},{1,0},{2,3},{3,2},{4,5},{5,4},{6,7},{7,6},{8,9},{9,8},{10,11... | collective-permute-start | bytes 393224 | tf_op jit(solution)/shard_map/ppermute | solution.py:410

commit v6 on v5

--- a/solution.py
+++ b/solution.py
@@ -19,7 +19,7 @@
 
 CHUNK = 256
 EDGE = 128
-ORDER = (3, 7, 6, 5, 1, 0, 4, 2)
+ORDER = (3, 6, 1, 2, 7, 0, 5, 4)
 VMEM = pl.BlockSpec(memory_space=pltpu.VMEM)
 LIMIT = 16 * 1024 * 1024
 STAGE_FLOPS = 1
@@ -432,21 +432,18 @@
     mine = low[0]
     prepared = prepare(mine)
     held = mine.reshape(1, windows * quarter, span)
-    near = min(4, chans // 2)
-    keys = list(range(near))
-    held = jnp.concatenate([held] + [swap(held, "chan", key) for key in keys[1:]], axis=0)
-    flip = near
-    while flip < chans // 2:
+    if chans == 8 and span == CHUNK:
+        pair = jnp.concatenate([held, swap(held, "chan", 1)], axis=0)
+        pair, prepared = lax.optimization_barrier((pair, prepared))
+        flips = (6, 4, 2)
+        parts = [pair] + [swap(pair, "chan", flip) for flip in flips]
+        return prepared, parts, tuple((flip, flip ^ 1) for flip in (0,) + flips)
+    keys, flip = [0], 1
+    while flip < chans:
         held = jnp.concatenate([held, swap(held, "chan", flip)], axis=0)
         keys = keys + [key ^ flip for key in keys]
         flip *= 2
-    held, prepared = lax.optimization_barrier((held, prepared))
-    other = swap(held, "chan", flip)
-    if span == CHUNK:
-        return prepared, (held, other), (tuple(keys), tuple(key ^ flip for key in keys))
-    every = jnp.concatenate([held, other], axis=0)
-    keys = jnp.asarray(keys + [key ^ flip for key in keys], jnp.int32)
-    every = jnp.zeros_like(every).at[chan ^ keys].set(every)
+    every = jnp.zeros_like(held).at[chan ^ jnp.asarray(keys, jnp.int32)].set(held)
     every = regroup(every)
     return prepared, (every,), ((None,) * every.shape[0],)
 

time: 35.1 us -> 34.2 us (0.974)
  waiting for transfers between devices: 8.97 us -> 8.35 us
    ppermute x9, waiting for transfers between devices: 8.97 us -> 8.35 us  [swap(): return lax.ppermute(x, axis, [(i, i ^ flip) for i in range(size)])]
  transfers between devices with their start and end apart: 10 -> 10, of which waited for: 5 -> 7; matrix products, arithmetic and copies ran while one was open for 0% -> 0% of each run, Pallas kernels for 14% -> 15%
where the time goes in v6:
time: 34.2 us; the launch traced here: 34 us
  starting transfers between devices  16.1 us (47%)
  Pallas kernels  9.43 us (28%)
  waiting for transfers between devices  8.35 us (24%)
    ppermute x9, waiting for transfers between devices, swap(): return lax.ppermute(x, axis, [(i, i ^ flip) for i in range(size)])  8.35 us
    ppermute x9, starting transfers between devices, swap(): return lax.ppermute(x, axis, [(i, i ^ flip) for i in range(size)])  8.2 us
    all_to_all x1, starting transfers between devices, shards(): lax.all_to_all(blocks, 'chan', 0, 0, axis_index_groups=[list(order)], til...  7.85 us
    pallas_call x1, Pallas kernels, correlate(): pl.pallas_call(functools.partial(correlate_kernel, flips, cw), out_shape=...  2.25 us
    pallas_call x1, Pallas kernels, pack(): pl.pallas_call(functools.partial(pack_kernel, width * reps), out_shape=(j...  2.19 us
    pallas_call x1, Pallas kernels, stage(): pl.pallas_call(functools.partial(stage_kernel, cw, width), out_shape=(jax...  1.65 us
    pallas_call x1, Pallas kernels, channel_spectra(): pl.pallas_call(functools.partial(channel_kernel, order), out_shape=jax.Sh...  1.31 us
    pallas_call x1, Pallas kernels, source_spectra(): pl.pallas_call(functools.partial(source_kernel, keys), out_shape=jax.Shap...  1.04 us
  transfers between devices with their start and end apart: 10, of which 7 were waited for; matrix products, arithmetic and copies ran while one was open for 0% of the time, Pallas kernels for 15%

profile of v6, /device:TPU:0, one launch (start us, length us, event | category | flops | bytes accessed | tf_op | source)
XLA Modules:
  0.0 34.0 jit_solution(7137678020587047185)
XLA Ops:
  0.0 0.0 copy-start.1
  0.0 0.0 copy-start
  0.0 2.2 %pack.1 = (bf16[8,2,1,64,256]{4,3,2,1,0:T(8,128)(2,1)}, bf16[2,32,256]{2,1,0:T(8,128)(2,1)S(1)}, bf16[2,32,256]{2,1,0:T(8,128)(2,1)S(1)}, bf16[2,2,32,256]{3,2,1,0:T(8,128)(2,1)S(1)}) custom-call(bf16[2,8,64,256]{3,2,1,0:T(8,128)(2,1)} %rec_hbm.1, s32[1,128]{1,0:T(1,128)} %bitcast.21), custom_call_target="tpu_custom_call" | custom-call | tf_op jit(solution)/shard_map/pack/pallas_call | solution.py:135
  2.2 7.9 %all-to-all-start = ((bf16[8,128,256]{2,1,0:T(8,128)(2,1)}), bf16[8,128,256]{2,1,0:T(8,128)(2,1)S(1)}, u32[]{:S(2)}, u32[]{:S(2)}) async-start(bf16[8,128,256]{2,1,0:T(8,128)(2,1)} %bitcast.1), calls=%async_computation | async-start | bytes 1048576 | tf_op jit(solution)/shard_map/all_to_all | solution.py:459
  10.1 1.5 %collective-permute-start = (bf16[2,2,32,256]{3,2,1,0:T(8,128)(2,1)S(1)}, bf16[2,2,32,256]{3,2,1,0:T(8,128)(2,1)S(1)}, u32[]{:S(2)}, u32[]{:S(2)}) collective-permute-start(bf16[2,2,32,256]{3,2,1,0:T(8,128)(2,1)S(1)} %get-tuple-element.20), channel_id=1, source_target_pairs={{0,2},{1,3},{2,0},{3,1},{4,6},{5,7},{6,4},{7,5},{8,10},{9,11},{10,... | collective-permute-start | bytes 196616 | tf_op jit(solution)/shard_map/ppermute | solution.py:410
  11.6 2.8 %collective-permute-done = bf16[2,2,32,256]{3,2,1,0:T(8,128)(2,1)S(1)} collective-permute-done((bf16[2,2,32,256]{3,2,1,0:T(8,128)(2,1)S(1)}, bf16[2,2,32,256]{3,2,1,0:T(8,128)(2,1)S(1)}, u32[]{:S(2)}, u32[]{:S(2)}) %collective-permute-start) | collective-permute-done | bytes 65568 | tf_op jit(solution)/shard_map/ppermute | solution.py:410
  14.3 0.0 collective-permute-start.1
  14.3 1.2 %collective-permute-done.1 = bf16[1,2,32,256]{3,2,1,0:T(8,128)(2,1)S(1)} collective-permute-done((bf16[1,2,32,256]{3,2,1,0:T(8,128)(2,1)S(1)}, bf16[1,2,32,256]{3,2,1,0:T(8,128)(2,1)S(1)}, u32[]{:S(2)}, u32[]{:S(2)}) %collective-permute-start.1) | collective-permute-done | bytes 32800 | tf_op jit(solution)/shard_map/ppermute | solution.py:410
  15.5 0.6 %collective-permute-start.2 = (bf16[1,64,256]{2,1,0:T(8,128)(2,1)S(1)}, bf16[1,64,256]{2,1,0:T(8,128)(2,1)S(1)}, u32[]{:S(2)}, u32[]{:S(2)}) collective-permute-start(bf16[1,64,256]{2,1,0:T(8,128)(2,1)S(1)} %bitcast.19), channel_id=1, source_target_pairs={{0,4},{4,0},{8,12},{12,8},{16,20},{20,16},{24,28},{28,24},{1,5},{5... | collective-permute-start | bytes 98312 | tf_op jit(solution)/shard_map/ppermute | solution.py:410
  16.2 1.6 %stage.1 = (bf16[2048,512]{1,0:T(8,128)(2,1)S(1)}, f32[128,1]{1,0:T(8,128)S(1)}, f32[64,1]{1,0:T(8,128)S(1)}, f32[32,256]{1,0:T(8,128)S(1)}) custom-call(bf16[2048,512]{1,0:T(8,128)(2,1)} %constant.10.clone.table_hbm, s32[1,128]{1,0:T(1,128)} %bitcast.22, s32[2,128]{1,0:T(2,128)} %dead_hbm.1, bf16[2,32,256]{2,1,0:T(8,128)(2,1)S(1)} %fusion.3.after_hbm), custom_call_target="tpu_custom_call" | custom-call | flops 1 | bytes 4194304 | tf_op jit(solution)/shard_map/stage/pallas_call | solution.py:202
  17.8 1.7 %collective-permute-done.2 = bf16[1,64,256]{2,1,0:T(8,128)(2,1)S(1)} collective-permute-done((bf16[1,64,256]{2,1,0:T(8,128)(2,1)S(1)}, bf16[1,64,256]{2,1,0:T(8,128)(2,1)S(1)}, u32[]{:S(2)}, u32[]{:S(2)}) %collective-permute-start.2) | collective-permute-done | bytes 32800 | tf_op jit(solution)/shard_map/ppermute | solution.py:410
  19.5 1.1 %collective-permute-start.8 = (bf16[2,64,256]{2,1,0:T(8,128)(2,1)S(1)}, bf16[2,64,256]{2,1,0:T(8,128)(2,1)S(1)}, u32[]{:S(2)}, u32[]{:S(2)}) collective-permute-start(bf16[2,64,256]{2,1,0:T(8,128)(2,1)S(1)} %pad_maximum_fusion.refs_0_), channel_id=1, source_target_pairs={{0,8},{4,12},{8,0},{12,4},{16,24},{20,28},{24,16},{28,20},{1,9},{5... | collective-permute-start | bytes 196616 | tf_op jit(solution)/shard_map/ppermute | solution.py:410
  20.6 1.9 %collective-permute-start.7 = (bf16[2,64,256]{2,1,0:T(8,128)(2,1)S(1)}, bf16[2,64,256]{2,1,0:T(8,128)(2,1)S(1)}, u32[]{:S(2)}, u32[]{:S(2)}) collective-permute-start(bf16[2,64,256]{2,1,0:T(8,128)(2,1)S(1)} %pad_maximum_fusion.refs_0_), channel_id=1, source_target_pairs={{0,16},{4,20},{8,24},{12,28},{16,0},{20,4},{24,8},{28,12},{1,17},{... | collective-permute-start | bytes 196616 | tf_op jit(solution)/shard_map/ppermute | solution.py:410
  22.5 1.5 %collective-permute-start.6 = (bf16[2,64,256]{2,1,0:T(8,128)(2,1)S(1)}, bf16[2,64,256]{2,1,0:T(8,128)(2,1)S(1)}, u32[]{:S(2)}, u32[]{:S(2)}) collective-permute-start(bf16[2,64,256]{2,1,0:T(8,128)(2,1)S(1)} %pad_maximum_fusion.refs_0_), channel_id=1, source_target_pairs={{0,24},{4,28},{8,16},{12,20},{16,8},{20,12},{24,0},{28,4},{1,25},{... | collective-permute-start | bytes 196616 | tf_op jit(solution)/shard_map/ppermute | solution.py:410
  24.0 0.0 all-to-all-done.x_ref
  24.0 0.0 copy-done.1
  24.0 0.0 copy-done
  24.0 1.3 %channel_spectra.1.refs_0_ = bf16[2,64,512]{2,1,0:T(8,128)(2,1)S(1)} custom-call(bf16[8,128,256]{2,1,0:T(8,128)(2,1)S(1)} %all-to-all-done.x_ref, f32[128,1]{1,0:T(8,128)S(1)} %get-tuple-element.26.live_ref, bf16[2048,512]{1,0:T(8,128)(2,1)S(1)} %get-tuple-element.27.table_ref.refs_5_, bf16[512,256]{1,0:T(8,128)(2,1)S(1)} %copy-done, ...), custom_call_target="tpu_custom_call" | custom-call | flops 1 | bytes 1 | tf_op jit(solution)/shard_map/channel_spectra/pallas_call | solution.py:276
  25.3 0.0 copy-start.2
  25.3 0.0 copy-start.3
  25.3 1.6 %collective-permute-start.3 = (bf16[2,64,512]{2,1,0:T(8,128)(2,1)S(1)}, bf16[2,64,512]{2,1,0:T(8,128)(2,1)S(1)}, u32[]{:S(2)}, u32[]{:S(2)}) collective-permute-start(bf16[2,64,512]{2,1,0:T(8,128)(2,1)S(1)} %channel_spectra.1.refs_0_), channel_id=1, source_target_pairs={{0,2},{1,3},{2,0},{3,1},{4,6},{5,7},{6,4},{7,5},{8,10},{9,11},{10,... | collective-permute-start | bytes 393224 | tf_op jit(solution)/shard_map/ppermute | solution.py:410
  26.9 0.0 collective-permute-done.8.refs_3_
  26.9 0.4 %collective-permute-done.7.refs_2_ = bf16[2,64,256]{2,1,0:T(8,128)(2,1)S(1)} collective-permute-done((bf16[2,64,256]{2,1,0:T(8,128)(2,1)S(1)}, bf16[2,64,256]{2,1,0:T(8,128)(2,1)S(1)}, u32[]{:S(2)}, u32[]{:S(2)}) %collective-permute-start.7) | collective-permute-done | bytes 65568 | tf_op jit(solution)/shard_map/ppermute | solution.py:410
  27.3 1.4 %collective-permute-done.6.refs_1_ = bf16[2,64,256]{2,1,0:T(8,128)(2,1)S(1)} collective-permute-done((bf16[2,64,256]{2,1,0:T(8,128)(2,1)S(1)}, bf16[2,64,256]{2,1,0:T(8,128)(2,1)S(1)}, u32[]{:S(2)}, u32[]{:S(2)}) %collective-permute-start.6) | collective-permute-done | bytes 65568 | tf_op jit(solution)/shard_map/ppermute | solution.py:410
  28.7 1.0 %source_spectra.1.spec_ref = bf16[64,512]{1,0:T(8,128)(2,1)S(1)} custom-call(bf16[2,64,256]{2,1,0:T(8,128)(2,1)S(1)} %pad_maximum_fusion.refs_0_, bf16[2,64,256]{2,1,0:T(8,128)(2,1)S(1)} %collective-permute-done.6.refs_1_, bf16[2,64,256]{2,1,0:T(8,128)(2,1)S(1)} %collective-permute-done.7.refs_2_, bf16[2,64,256]{2,1,0:T(8,128)(2,1)S(1)} %collective-permute-done.8.refs_3_, ...), custom_call_target="tpu_custom_call" | custom-call | flops 17179869184 | bytes 8388608 | tf_op jit(solution)/shard_map/source_spectra/pallas_call | solution.py:307
  29.7 0.1 collective-permute-start.4
  29.8 0.6 %collective-permute-done.3.refs_1_ = bf16[2,64,512]{2,1,0:T(8,128)(2,1)S(1)} collective-permute-done((bf16[2,64,512]{2,1,0:T(8,128)(2,1)S(1)}, bf16[2,64,512]{2,1,0:T(8,128)(2,1)S(1)}, u32[]{:S(2)}, u32[]{:S(2)}) %collective-permute-start.3) | collective-permute-done | bytes 131104 | tf_op jit(solution)/shard_map/ppermute | solution.py:410
  30.4 0.0 collective-permute-start.5
  30.4 0.0 copy-done.2
  30.4 0.0 copy-done.3
  30.4 1.0 %lag_kernels.1.refs_4_ = bf16[2048,1024]{1,0:T(8,128)(2,1)S(1)} custom-call(bf16[64,512]{1,0:T(8,128)(2,1)S(1)} %source_spectra.1.spec_ref, f32[64,256]{1,0:T(8,128)S(1)} %copy-done.3, f32[64,256]{1,0:T(8,128)S(1)} %copy-done.2), custom_call_target="tpu_custom_call" | custom-call | flops 17179869184 | bytes 8388608 | tf_op jit(solution)/shard_map/lag_kernels/pallas_call | solution.py:343
  31.4 0.0 collective-permute-done.4.refs_2_
  31.4 0.3 collective-permute-done.5.refs_3_
  31.7 2.2 %correlate.1 = f32[32,64,256]{2,1,0:T(8,128)} custom-call(bf16[2,64,512]{2,1,0:T(8,128)(2,1)S(1)} %channel_spectra.1.refs_0_, bf16[2,64,512]{2,1,0:T(8,128)(2,1)S(1)} %collective-permute-done.3.refs_1_, bf16[2,64,512]{2,1,0:T(8,128)(2,1)S(1)} %collective-permute-done.4.refs_2_, bf16[2,64,512]{2,1,0:T(8,128)(2,1)S(1)} %collective-permute-done.5.refs_3_, ...), custom_call_target="tpu_custom_call" | custom-call | tf_op jit(solution)/shard_map/correlate/pallas_call | solution.py:393
  (3 shorter events, 0.0 us)
Async XLA Ops:
  0.0 24.0 %copy-start.1 = (bf16[256,256]{1,0:T(8,128)(2,1)S(1)}, bf16[256,256]{1,0:T(8,128)(2,1)}, u32[]{:S(2)}) copy-start(bf16[256,256]{1,0:T(8,128)(2,1)} %constant.12.clone.bins_ref.refs_7_) | copy-start | bytes 393220
  0.0 24.0 %copy-start = (bf16[512,256]{1,0:T(8,128)(2,1)S(1)}, bf16[512,256]{1,0:T(8,128)(2,1)}, u32[]{:S(2)}) copy-start(bf16[512,256]{1,0:T(8,128)(2,1)} %constant.11.clone.band_ref.refs_6_) | copy-start | bytes 786436
  2.2 21.8 %all-to-all-start = ((bf16[8,128,256]{2,1,0:T(8,128)(2,1)}), bf16[8,128,256]{2,1,0:T(8,128)(2,1)S(1)}, u32[]{:S(2)}, u32[]{:S(2)}) async-start(bf16[8,128,256]{2,1,0:T(8,128)(2,1)} %bitcast.1), calls=%async_computation | async-start | bytes 1048576 | tf_op jit(solution)/shard_map/all_to_all | solution.py:459
  10.1 4.3 %collective-permute-start = (bf16[2,2,32,256]{3,2,1,0:T(8,128)(2,1)S(1)}, bf16[2,2,32,256]{3,2,1,0:T(8,128)(2,1)S(1)}, u32[]{:S(2)}, u32[]{:S(2)}) collective-permute-start(bf16[2,2,32,256]{3,2,1,0:T(8,128)(2,1)S(1)} %get-tuple-element.20), channel_id=1, source_target_pairs={{0,2},{1,3},{2,0},{3,1},{4,6},{5,7},{6,4},{7,5},{8,10},{9,11},{10,... | collective-permute-start | bytes 196616 | tf_op jit(solution)/shard_map/ppermute | solution.py:410
  14.3 1.2 %collective-permute-start.1 = (bf16[1,2,32,256]{3,2,1,0:T(8,128)(2,1)S(1)}, bf16[1,2,32,256]{3,2,1,0:T(8,128)(2,1)S(1)}, u32[]{:S(2)}, u32[]{:S(2)}) collective-permute-start(bf16[1,2,32,256]{3,2,1,0:T(8,128)(2,1)S(1)} %fusion.1), channel_id=1, source_target_pairs={{0,1},{1,0},{2,3},{3,2},{4,5},{5,4},{6,7},{7,6},{8,9},{9,8},{10,11... | collective-permute-start | bytes 98312 | tf_op jit(solution)/shard_map/ppermute | solution.py:410
  15.5 4.0 %collective-permute-start.2 = (bf16[1,64,256]{2,1,0:T(8,128)(2,1)S(1)}, bf16[1,64,256]{2,1,0:T(8,128)(2,1)S(1)}, u32[]{:S(2)}, u32[]{:S(2)}) collective-permute-start(bf16[1,64,256]{2,1,0:T(8,128)(2,1)S(1)} %bitcast.19), channel_id=1, source_target_pairs={{0,4},{4,0},{8,12},{12,8},{16,20},{20,16},{24,28},{28,24},{1,5},{5... | collective-permute-start | bytes 98312 | tf_op jit(solution)/shard_map/ppermute | solution.py:410
  19.5 7.4 %collective-permute-start.8 = (bf16[2,64,256]{2,1,0:T(8,128)(2,1)S(1)}, bf16[2,64,256]{2,1,0:T(8,128)(2,1)S(1)}, u32[]{:S(2)}, u32[]{:S(2)}) collective-permute-start(bf16[2,64,256]{2,1,0:T(8,128)(2,1)S(1)} %pad_maximum_fusion.refs_0_), channel_id=1, source_target_pairs={{0,8},{4,12},{8,0},{12,4},{16,24},{20,28},{24,16},{28,20},{1,9},{5... | collective-permute-start | bytes 196616 | tf_op jit(solution)/shard_map/ppermute | solution.py:410
  20.6 6.7 %collective-permute-start.7 = (bf16[2,64,256]{2,1,0:T(8,128)(2,1)S(1)}, bf16[2,64,256]{2,1,0:T(8,128)(2,1)S(1)}, u32[]{:S(2)}, u32[]{:S(2)}) collective-permute-start(bf16[2,64,256]{2,1,0:T(8,128)(2,1)S(1)} %pad_maximum_fusion.refs_0_), channel_id=1, source_target_pairs={{0,16},{4,20},{8,24},{12,28},{16,0},{20,4},{24,8},{28,12},{1,17},{... | collective-permute-start | bytes 196616 | tf_op jit(solution)/shard_map/ppermute | solution.py:410
  22.5 6.2 %collective-permute-start.6 = (bf16[2,64,256]{2,1,0:T(8,128)(2,1)S(1)}, bf16[2,64,256]{2,1,0:T(8,128)(2,1)S(1)}, u32[]{:S(2)}, u32[]{:S(2)}) collective-permute-start(bf16[2,64,256]{2,1,0:T(8,128)(2,1)S(1)} %pad_maximum_fusion.refs_0_), channel_id=1, source_target_pairs={{0,24},{4,28},{8,16},{12,20},{16,8},{20,12},{24,0},{28,4},{1,25},{... | collective-permute-start | bytes 196616 | tf_op jit(solution)/shard_map/ppermute | solution.py:410
  25.3 5.1 %copy-start.2 = (f32[64,256]{1,0:T(8,128)S(1)}, f32[64,256]{1,0:T(8,128)}, u32[]{:S(2)}) copy-start(f32[64,256]{1,0:T(8,128)} %constant.14.clone.sin_ref) | copy-start | bytes 196612
  25.3 5.1 %copy-start.3 = (f32[64,256]{1,0:T(8,128)S(1)}, f32[64,256]{1,0:T(8,128)}, u32[]{:S(2)}) copy-start(f32[64,256]{1,0:T(8,128)} %constant.13.clone.cos_ref) | copy-start | bytes 196612
  25.3 5.0 %collective-permute-start.3 = (bf16[2,64,512]{2,1,0:T(8,128)(2,1)S(1)}, bf16[2,64,512]{2,1,0:T(8,128)(2,1)S(1)}, u32[]{:S(2)}, u32[]{:S(2)}) collective-permute-start(bf16[2,64,512]{2,1,0:T(8,128)(2,1)S(1)} %channel_spectra.1.refs_0_), channel_id=1, source_target_pairs={{0,2},{1,3},{2,0},{3,1},{4,6},{5,7},{6,4},{7,5},{8,10},{9,11},{10,... | collective-permute-start | bytes 393224 | tf_op jit(solution)/shard_map/ppermute | solution.py:410
  29.7 1.6 %collective-permute-start.4 = (bf16[2,64,512]{2,1,0:T(8,128)(2,1)S(1)}, bf16[2,64,512]{2,1,0:T(8,128)(2,1)S(1)}, u32[]{:S(2)}, u32[]{:S(2)}) collective-permute-start(bf16[2,64,512]{2,1,0:T(8,128)(2,1)S(1)} %channel_spectra.1.refs_0_), channel_id=1, source_target_pairs={{0,1},{1,0},{2,3},{3,2},{4,5},{5,4},{6,7},{7,6},{8,9},{9,8},{10,11... | collective-permute-start | bytes 393224 | tf_op jit(solution)/shard_map/ppermute | solution.py:410
  30.4 1.3 %collective-permute-start.5 = (bf16[2,64,512]{2,1,0:T(8,128)(2,1)S(1)}, bf16[2,64,512]{2,1,0:T(8,128)(2,1)S(1)}, u32[]{:S(2)}, u32[]{:S(2)}) collective-permute-start(bf16[2,64,512]{2,1,0:T(8,128)(2,1)S(1)} %collective-permute-done.3.refs_1_), channel_id=1, source_target_pairs={{0,1},{1,0},{2,3},{3,2},{4,5},{5,4},{6,7},{7,6},{8,9},{9,8},{10,11... | collective-permute-start | bytes 393224 | tf_op jit(solution)/shard_map/ppermute | solution.py:410

commit v7 on v6

--- a/solution.py
+++ b/solution.py
@@ -78,8 +78,8 @@
     return jnp.max(hit, axis=1, keepdims=True)
 
 
-def pack_kernel(cw, rec_hbm, src_hbm, out_ref, *refs):
-    *low_refs, high_ref, src_ref, pick_ref, sem = refs
+def pack_kernel(cw, rec_hbm, src_hbm, out_hbm, *refs):
+    *low_refs, high_ref, out_ref, src_ref, pick_ref, sem = refs
     windows, groups, width, span = rec_hbm.shape
     per = groups // out_ref.shape[0]
     order = order_of(out_ref.shape[0])
@@ -107,9 +107,15 @@
     brought.wait()
     wide = jnp.concatenate([columns_of(src_ref[...])] * (local // 128), axis=1)
     onehot = jnp.where(wide == ids, 1.0, 0.0).astype(jnp.bfloat16)
+    sent = []
     for w in range(windows):
-        for copy in copies[w]:
-            copy.wait()
+        for n in range(len(order)):
+            copies[w][n].wait()
+            sent.append(
+                pltpu.make_async_copy(out_ref.at[n, w], out_hbm.at[n, w], sem.at[windows + 1 + w, n])
+            )
+            sent[-1].start()
+    for w in range(windows):
         rows = jnp.concatenate(
             [out_ref[order.index(g // per), w, g % per] for g in range(groups)], axis=0
         )
@@ -121,6 +127,8 @@
                 low_refs[flip][w] = picked
             else:
                 high_ref[flip - reps // 2, w] = picked
+    for copy in sent:
+        copy.wait()
 
 
 def in_hbm(*arrays):
@@ -140,11 +148,12 @@
             jax.ShapeDtypeStruct((reps // 2,) + part, jnp.bfloat16),
         ),
         in_specs=[HBM] * 2,
-        out_specs=(VMEM,) * (reps // 2 + 2),
+        out_specs=(HBM,) + (VMEM,) * (reps // 2 + 1),
         scratch_shapes=[
+            pltpu.VMEM((chans, windows, per, width, span), jnp.bfloat16),
             pltpu.VMEM((1, count), jnp.int32),
             pltpu.VMEM((count, span), jnp.float32),
-            pltpu.SemaphoreType.DMA((1 + windows, chans)),
+            pltpu.SemaphoreType.DMA((1 + 2 * windows, chans)),
         ],
         compiler_params=pltpu.CompilerParams(vmem_limit_bytes=LIMIT),
         name="pack",
@@ -236,15 +245,16 @@
             jnp.abs(x[i + 1][:, :EDGE]) if i < pieces - 1 else blank
         )
     totals = jnp.dot(ext_ref[...], band_ref[...], preferred_element_type=jnp.float32)
-    spectrum = jnp.zeros((rows, 2 * K), jnp.float32)
+    chunks = []
     for i in range(pieces):
         sample = iota((1, CHUNK), 1) + i * CHUNK
         counts = jnp.minimum(sample, HALF) + jnp.minimum(length - 1 - sample, HALF) + 1
         mean = totals[i * rows : (i + 1) * rows] * (1.0 / counts.astype(jnp.float32))
         normed = (x[i][...].astype(jnp.float32) / (mean + EPS)).astype(jnp.bfloat16)
-        spectrum += jnp.dot(
-            normed, table_ref[i * CHUNK : (i + 1) * CHUNK, :], preferred_element_type=jnp.float32
-        )
+        chunks.append(normed)
+    spectrum = jnp.dot(
+        jnp.concatenate(chunks, axis=1), table_ref[...], preferred_element_type=jnp.float32
+    )
     real_part, imag_part = spectrum[:, :K], spectrum[:, K:]
     amplitude = jnp.sqrt(real_part * real_part + imag_part * imag_part)
     high = amplitude.astype(jnp.bfloat16)
@@ -421,15 +431,10 @@
 def gather_sources(low, high, prepare):
     chans, chan = lax.axis_size("chan"), lax.axis_index("chan")
     windows, quarter, span = low[0].shape
-    flip = len(low)
-    while flip:
-        came = swap(high, "rep", flip)
-        low = [part + came[n] for n, part in enumerate(low)]
-        flip //= 2
-        if flip:
-            high = jnp.stack(low[flip:])
-            low = low[:flip]
-    mine = low[0]
+    given = list(low) + [high[n] for n in range(len(low))]
+    mine = given[0]
+    for flip in range(1, len(given)):
+        mine = mine + swap(given[flip], "rep", flip)
     prepared = prepare(mine)
     held = mine.reshape(1, windows * quarter, span)
     if chans == 8 and span == CHUNK:

time: 34.2 us -> 33.5 us (0.980)
  Pallas kernels: 9.43 us -> 8.99 us
  waiting for transfers between devices: 8.35 us -> 8 us
    ppermute x9 -> x10, waiting for transfers between devices: 8.35 us -> 7.99 us  [swap(): return lax.ppermute(x, axis, [(i, i ^ flip) for i in range(size)])]
    ppermute x9 -> x10, starting transfers between devices: 8.2 us -> 8.26 us  [swap(): return lax.ppermute(x, axis, [(i, i ^ flip) for i in range(size)])]
  transfers between devices with their start and end apart: 10 -> 11, of which waited for: 7 -> 7; matrix products, arithmetic and copies ran while one was open for 0% -> 0% of each run, Pallas kernels for 15% -> 14%
where the time goes in v7:
time: 33.5 us; the launch traced here: 33.2 us
  starting transfers between devices  16.1 us (48%)
  Pallas kernels  8.99 us (27%)
  waiting for transfers between devices  8 us (24%)
    ppermute x10, starting transfers between devices, swap(): return lax.ppermute(x, axis, [(i, i ^ flip) for i in range(size)])  8.26 us
    ppermute x10, waiting for transfers between devices, swap(): return lax.ppermute(x, axis, [(i, i ^ flip) for i in range(size)])  7.99 us
    all_to_all x1, starting transfers between devices, shards(): lax.all_to_all(blocks, 'chan', 0, 0, axis_index_groups=[list(order)], til...  7.85 us
    pallas_call x1, Pallas kernels, correlate(): pl.pallas_call(functools.partial(correlate_kernel, flips, cw), out_shape=...  2.25 us
    pallas_call x1, Pallas kernels, pack(): pl.pallas_call(functools.partial(pack_kernel, width * reps), out_shape=(j...  2.04 us
    pallas_call x1, Pallas kernels, stage(): pl.pallas_call(functools.partial(stage_kernel, cw, width), out_shape=(jax...  1.65 us
    pallas_call x1, Pallas kernels, channel_spectra(): pl.pallas_call(functools.partial(channel_kernel, order), out_shape=jax.Sh...  1.28 us
    pallas_call x1, Pallas kernels, lag_kernels(): pl.pallas_call(functools.partial(lag_kernel, windows), out_shape=jax.Shap...  0.99 us
  transfers between devices with their start and end apart: 11, of which 7 were waited for; matrix products, arithmetic and copies ran while one was open for 0% of the time, Pallas kernels for 14%

profile of v7, /device:TPU:0, one launch (start us, length us, event | category | flops | bytes accessed | tf_op | source)
XLA Modules:
  0.0 33.2 jit_solution(11222445495573971198)
XLA Ops:
  0.0 0.0 copy-start.1
  0.0 0.0 copy-start
  0.0 2.0 %pack.1 = (bf16[8,2,1,64,256]{4,3,2,1,0:T(8,128)(2,1)}, bf16[2,32,256]{2,1,0:T(8,128)(2,1)S(1)}, bf16[2,32,256]{2,1,0:T(8,128)(2,1)S(1)}, bf16[2,2,32,256]{3,2,1,0:T(8,128)(2,1)S(1)}) custom-call(bf16[2,8,64,256]{3,2,1,0:T(8,128)(2,1)} %rec_hbm.1, s32[1,128]{1,0:T(1,128)} %bitcast.9), custom_call_target="tpu_custom_call" | custom-call | tf_op jit(solution)/shard_map/pack/pallas_call | solution.py:143
  2.1 7.9 %all-to-all-start = ((bf16[8,128,256]{2,1,0:T(8,128)(2,1)}), bf16[8,128,256]{2,1,0:T(8,128)(2,1)S(1)}, u32[]{:S(2)}, u32[]{:S(2)}) async-start(bf16[8,128,256]{2,1,0:T(8,128)(2,1)} %bitcast.1), calls=%async_computation | async-start | bytes 1048576 | tf_op jit(solution)/shard_map/all_to_all | solution.py:464
  9.9 0.0 collective-permute-start
  9.9 1.6 %collective-permute-start.1 = (bf16[2,32,256]{2,1,0:T(8,128)(2,1)S(1)}, bf16[2,32,256]{2,1,0:T(8,128)(2,1)S(1)}, u32[]{:S(2)}, u32[]{:S(2)}) collective-permute-start(bf16[2,32,256]{2,1,0:T(8,128)(2,1)S(1)} %get-tuple-element.31), channel_id=1, source_target_pairs={{0,2},{1,3},{2,0},{3,1},{4,6},{5,7},{6,4},{7,5},{8,10},{9,11},{10,... | collective-permute-start | bytes 98312 | tf_op jit(solution)/shard_map/ppermute | solution.py:420
  11.5 0.3 collective-permute-start.2
  11.8 0.0 collective-permute-done
  11.8 2.1 %collective-permute-done.1 = bf16[2,32,256]{2,1,0:T(8,128)(2,1)S(1)} collective-permute-done((bf16[2,32,256]{2,1,0:T(8,128)(2,1)S(1)}, bf16[2,32,256]{2,1,0:T(8,128)(2,1)S(1)}, u32[]{:S(2)}, u32[]{:S(2)}) %collective-permute-start.1) | collective-permute-done | bytes 32800 | tf_op jit(solution)/shard_map/ppermute | solution.py:420
  13.9 0.9 %collective-permute-done.2 = bf16[2,32,256]{2,1,0:T(8,128)(2,1)S(1)} collective-permute-done((bf16[2,32,256]{2,1,0:T(8,128)(2,1)S(1)}, bf16[2,32,256]{2,1,0:T(8,128)(2,1)S(1)}, u32[]{:S(2)}, u32[]{:S(2)}) %collective-permute-start.2) | collective-permute-done | bytes 32800 | tf_op jit(solution)/shard_map/ppermute | solution.py:420
  14.8 0.6 %collective-permute-start.3 = (bf16[1,64,256]{2,1,0:T(8,128)(2,1)S(1)}, bf16[1,64,256]{2,1,0:T(8,128)(2,1)S(1)}, u32[]{:S(2)}, u32[]{:S(2)}) collective-permute-start(bf16[1,64,256]{2,1,0:T(8,128)(2,1)S(1)} %bitcast.7), channel_id=1, source_target_pairs={{0,4},{4,0},{8,12},{12,8},{16,20},{20,16},{24,28},{28,24},{1,5},{5... | collective-permute-start | bytes 98312 | tf_op jit(solution)/shard_map/ppermute | solution.py:420
  15.5 1.6 %stage.1 = (bf16[2048,512]{1,0:T(8,128)(2,1)S(1)}, f32[128,1]{1,0:T(8,128)S(1)}, f32[64,1]{1,0:T(8,128)S(1)}, f32[32,256]{1,0:T(8,128)S(1)}) custom-call(bf16[2048,512]{1,0:T(8,128)(2,1)} %constant.10.clone.table_hbm, s32[1,128]{1,0:T(1,128)} %bitcast.10, s32[2,128]{1,0:T(2,128)} %dead_hbm.1, bf16[2,32,256]{2,1,0:T(8,128)(2,1)S(1)} %add_add_fusion.after_hbm), custom_call_target="tpu_custom_call" | custom-call | flops 1 | bytes 4194304 | tf_op jit(solution)/shard_map/stage/pallas_call | solution.py:211
  17.1 1.7 %collective-permute-done.3 = bf16[1,64,256]{2,1,0:T(8,128)(2,1)S(1)} collective-permute-done((bf16[1,64,256]{2,1,0:T(8,128)(2,1)S(1)}, bf16[1,64,256]{2,1,0:T(8,128)(2,1)S(1)}, u32[]{:S(2)}, u32[]{:S(2)}) %collective-permute-start.3) | collective-permute-done | bytes 32800 | tf_op jit(solution)/shard_map/ppermute | solution.py:420
  18.8 0.6 %collective-permute-start.9 = (bf16[2,64,256]{2,1,0:T(8,128)(2,1)S(1)}, bf16[2,64,256]{2,1,0:T(8,128)(2,1)S(1)}, u32[]{:S(2)}, u32[]{:S(2)}) collective-permute-start(bf16[2,64,256]{2,1,0:T(8,128)(2,1)S(1)} %pad_maximum_fusion.refs_0_), channel_id=1, source_target_pairs={{0,8},{4,12},{8,0},{12,4},{16,24},{20,28},{24,16},{28,20},{1,9},{5... | collective-permute-start | bytes 196616 | tf_op jit(solution)/shard_map/ppermute | solution.py:420
  19.5 2.3 %collective-permute-start.8 = (bf16[2,64,256]{2,1,0:T(8,128)(2,1)S(1)}, bf16[2,64,256]{2,1,0:T(8,128)(2,1)S(1)}, u32[]{:S(2)}, u32[]{:S(2)}) collective-permute-start(bf16[2,64,256]{2,1,0:T(8,128)(2,1)S(1)} %pad_maximum_fusion.refs_0_), channel_id=1, source_target_pairs={{0,16},{4,20},{8,24},{12,28},{16,0},{20,4},{24,8},{28,12},{1,17},{... | collective-permute-start | bytes 196616 | tf_op jit(solution)/shard_map/ppermute | solution.py:420
  21.8 1.5 %collective-permute-start.7 = (bf16[2,64,256]{2,1,0:T(8,128)(2,1)S(1)}, bf16[2,64,256]{2,1,0:T(8,128)(2,1)S(1)}, u32[]{:S(2)}, u32[]{:S(2)}) collective-permute-start(bf16[2,64,256]{2,1,0:T(8,128)(2,1)S(1)} %pad_maximum_fusion.refs_0_), channel_id=1, source_target_pairs={{0,24},{4,28},{8,16},{12,20},{16,8},{20,12},{24,0},{28,4},{1,25},{... | collective-permute-start | bytes 196616 | tf_op jit(solution)/shard_map/ppermute | solution.py:420
  23.3 0.0 all-to-all-done.x_ref
  23.3 0.0 copy-done.1
  23.3 0.0 copy-done
  23.3 1.3 %channel_spectra.1.refs_0_ = bf16[2,64,512]{2,1,0:T(8,128)(2,1)S(1)} custom-call(bf16[8,128,256]{2,1,0:T(8,128)(2,1)S(1)} %all-to-all-done.x_ref, f32[128,1]{1,0:T(8,128)S(1)} %get-tuple-element.26.live_ref, bf16[2048,512]{1,0:T(8,128)(2,1)S(1)} %get-tuple-element.27.table_ref.refs_5_, bf16[512,256]{1,0:T(8,128)(2,1)S(1)} %copy-done, ...), custom_call_target="tpu_custom_call" | custom-call | flops 1 | bytes 1 | tf_op jit(solution)/shard_map/channel_spectra/pallas_call | solution.py:286
  24.6 0.0 copy-start.2
  24.6 0.0 copy-start.3
  24.6 1.3 %collective-permute-start.4 = (bf16[2,64,512]{2,1,0:T(8,128)(2,1)S(1)}, bf16[2,64,512]{2,1,0:T(8,128)(2,1)S(1)}, u32[]{:S(2)}, u32[]{:S(2)}) collective-permute-start(bf16[2,64,512]{2,1,0:T(8,128)(2,1)S(1)} %channel_spectra.1.refs_0_), channel_id=1, source_target_pairs={{0,2},{1,3},{2,0},{3,1},{4,6},{5,7},{6,4},{7,5},{8,10},{9,11},{10,... | collective-permute-start | bytes 393224 | tf_op jit(solution)/shard_map/ppermute | solution.py:420
  25.9 0.0 collective-permute-done.9.refs_3_
  25.9 1.2 %collective-permute-done.8.refs_2_ = bf16[2,64,256]{2,1,0:T(8,128)(2,1)S(1)} collective-permute-done((bf16[2,64,256]{2,1,0:T(8,128)(2,1)S(1)}, bf16[2,64,256]{2,1,0:T(8,128)(2,1)S(1)}, u32[]{:S(2)}, u32[]{:S(2)}) %collective-permute-start.8) | collective-permute-done | bytes 65568 | tf_op jit(solution)/shard_map/ppermute | solution.py:420
  27.0 0.9 %collective-permute-done.7.refs_1_ = bf16[2,64,256]{2,1,0:T(8,128)(2,1)S(1)} collective-permute-done((bf16[2,64,256]{2,1,0:T(8,128)(2,1)S(1)}, bf16[2,64,256]{2,1,0:T(8,128)(2,1)S(1)}, u32[]{:S(2)}, u32[]{:S(2)}) %collective-permute-start.7) | collective-permute-done | bytes 65568 | tf_op jit(solution)/shard_map/ppermute | solution.py:420
  28.0 0.8 %source_spectra.1.spec_ref = bf16[64,512]{1,0:T(8,128)(2,1)S(1)} custom-call(bf16[2,64,256]{2,1,0:T(8,128)(2,1)S(1)} %pad_maximum_fusion.refs_0_, bf16[2,64,256]{2,1,0:T(8,128)(2,1)S(1)} %collective-permute-done.7.refs_1_, bf16[2,64,256]{2,1,0:T(8,128)(2,1)S(1)} %collective-permute-done.8.refs_2_, bf16[2,64,256]{2,1,0:T(8,128)(2,1)S(1)} %collective-permute-done.9.refs_3_, ...), custom_call_target="tpu_custom_call" | custom-call | flops 17179869184 | bytes 8388608 | tf_op jit(solution)/shard_map/source_spectra/pallas_call | solution.py:317
  28.8 0.1 collective-permute-start.5
  28.9 0.8 %collective-permute-done.4.refs_1_ = bf16[2,64,512]{2,1,0:T(8,128)(2,1)S(1)} collective-permute-done((bf16[2,64,512]{2,1,0:T(8,128)(2,1)S(1)}, bf16[2,64,512]{2,1,0:T(8,128)(2,1)S(1)}, u32[]{:S(2)}, u32[]{:S(2)}) %collective-permute-start.4) | collective-permute-done | bytes 131104 | tf_op jit(solution)/shard_map/ppermute | solution.py:420
  29.6 0.0 collective-permute-start.6
  29.6 0.0 copy-done.2
  29.6 0.0 copy-done.3
  29.7 1.0 %lag_kernels.1.refs_4_ = bf16[2048,1024]{1,0:T(8,128)(2,1)S(1)} custom-call(bf16[64,512]{1,0:T(8,128)(2,1)S(1)} %source_spectra.1.spec_ref, f32[64,256]{1,0:T(8,128)S(1)} %copy-done.3, f32[64,256]{1,0:T(8,128)S(1)} %copy-done.2), custom_call_target="tpu_custom_call" | custom-call | flops 17179869184 | bytes 8388608 | tf_op jit(solution)/shard_map/lag_kernels/pallas_call | solution.py:353
  30.7 0.0 collective-permute-done.5.refs_2_
  30.7 0.3 collective-permute-done.6.refs_3_
  31.0 2.2 %correlate.1 = f32[32,64,256]{2,1,0:T(8,128)} custom-call(bf16[2,64,512]{2,1,0:T(8,128)(2,1)S(1)} %channel_spectra.1.refs_0_, bf16[2,64,512]{2,1,0:T(8,128)(2,1)S(1)} %collective-permute-done.4.refs_1_, bf16[2,64,512]{2,1,0:T(8,128)(2,1)S(1)} %collective-permute-done.5.refs_2_, bf16[2,64,512]{2,1,0:T(8,128)(2,1)S(1)} %collective-permute-done.6.refs_3_, ...), custom_call_target="tpu_custom_call" | custom-call | tf_op jit(solution)/shard_map/correlate/pallas_call | solution.py:403
  (3 shorter events, 0.0 us)
Async XLA Ops:
  0.0 23.3 %copy-start.1 = (bf16[256,256]{1,0:T(8,128)(2,1)S(1)}, bf16[256,256]{1,0:T(8,128)(2,1)}, u32[]{:S(2)}) copy-start(bf16[256,256]{1,0:T(8,128)(2,1)} %constant.12.clone.bins_ref.refs_7_) | copy-start | bytes 393220
  0.0 23.3 %copy-start = (bf16[512,256]{1,0:T(8,128)(2,1)S(1)}, bf16[512,256]{1,0:T(8,128)(2,1)}, u32[]{:S(2)}) copy-start(bf16[512,256]{1,0:T(8,128)(2,1)} %constant.11.clone.band_ref.refs_6_) | copy-start | bytes 786436
  2.1 21.2 %all-to-all-start = ((bf16[8,128,256]{2,1,0:T(8,128)(2,1)}), bf16[8,128,256]{2,1,0:T(8,128)(2,1)S(1)}, u32[]{:S(2)}, u32[]{:S(2)}) async-start(bf16[8,128,256]{2,1,0:T(8,128)(2,1)} %bitcast.1), calls=%async_computation | async-start | bytes 1048576 | tf_op jit(solution)/shard_map/all_to_all | solution.py:464
  9.9 1.9 %collective-permute-start = (bf16[2,32,256]{2,1,0:T(8,128)(2,1)S(1)}, bf16[2,32,256]{2,1,0:T(8,128)(2,1)S(1)}, u32[]{:S(2)}, u32[]{:S(2)}) collective-permute-start(bf16[2,32,256]{2,1,0:T(8,128)(2,1)S(1)} %get-tuple-element.20), channel_id=1, source_target_pairs={{0,1},{1,0},{2,3},{3,2},{4,5},{5,4},{6,7},{7,6},{8,9},{9,8},{10,11... | collective-permute-start | bytes 98312 | tf_op jit(solution)/shard_map/ppermute | solution.py:420
  9.9 4.0 %collective-permute-start.1 = (bf16[2,32,256]{2,1,0:T(8,128)(2,1)S(1)}, bf16[2,32,256]{2,1,0:T(8,128)(2,1)S(1)}, u32[]{:S(2)}, u32[]{:S(2)}) collective-permute-start(bf16[2,32,256]{2,1,0:T(8,128)(2,1)S(1)} %get-tuple-element.31), channel_id=1, source_target_pairs={{0,2},{1,3},{2,0},{3,1},{4,6},{5,7},{6,4},{7,5},{8,10},{9,11},{10,... | collective-permute-start | bytes 98312 | tf_op jit(solution)/shard_map/ppermute | solution.py:420
  11.5 3.4 %collective-permute-start.2 = (bf16[2,32,256]{2,1,0:T(8,128)(2,1)S(1)}, bf16[2,32,256]{2,1,0:T(8,128)(2,1)S(1)}, u32[]{:S(2)}, u32[]{:S(2)}) collective-permute-start(bf16[2,32,256]{2,1,0:T(8,128)(2,1)S(1)} %get-tuple-element.32), channel_id=1, source_target_pairs={{0,3},{1,2},{2,1},{3,0},{4,7},{5,6},{6,5},{7,4},{8,11},{9,10},{10,... | collective-permute-start | bytes 98312 | tf_op jit(solution)/shard_map/ppermute | solution.py:420
  14.8 4.0 %collective-permute-start.3 = (bf16[1,64,256]{2,1,0:T(8,128)(2,1)S(1)}, bf16[1,64,256]{2,1,0:T(8,128)(2,1)S(1)}, u32[]{:S(2)}, u32[]{:S(2)}) collective-permute-start(bf16[1,64,256]{2,1,0:T(8,128)(2,1)S(1)} %bitcast.7), channel_id=1, source_target_pairs={{0,4},{4,0},{8,12},{12,8},{16,20},{20,16},{24,28},{28,24},{1,5},{5... | collective-permute-start | bytes 98312 | tf_op jit(solution)/shard_map/ppermute | solution.py:420
  18.8 7.0 %collective-permute-start.9 = (bf16[2,64,256]{2,1,0:T(8,128)(2,1)S(1)}, bf16[2,64,256]{2,1,0:T(8,128)(2,1)S(1)}, u32[]{:S(2)}, u32[]{:S(2)}) collective-permute-start(bf16[2,64,256]{2,1,0:T(8,128)(2,1)S(1)} %pad_maximum_fusion.refs_0_), channel_id=1, source_target_pairs={{0,8},{4,12},{8,0},{12,4},{16,24},{20,28},{24,16},{28,20},{1,9},{5... | collective-permute-start | bytes 196616 | tf_op jit(solution)/shard_map/ppermute | solution.py:420
  19.5 7.6 %collective-permute-start.8 = (bf16[2,64,256]{2,1,0:T(8,128)(2,1)S(1)}, bf16[2,64,256]{2,1,0:T(8,128)(2,1)S(1)}, u32[]{:S(2)}, u32[]{:S(2)}) collective-permute-start(bf16[2,64,256]{2,1,0:T(8,128)(2,1)S(1)} %pad_maximum_fusion.refs_0_), channel_id=1, source_target_pairs={{0,16},{4,20},{8,24},{12,28},{16,0},{20,4},{24,8},{28,12},{1,17},{... | collective-permute-start | bytes 196616 | tf_op jit(solution)/shard_map/ppermute | solution.py:420
  21.8 6.2 %collective-permute-start.7 = (bf16[2,64,256]{2,1,0:T(8,128)(2,1)S(1)}, bf16[2,64,256]{2,1,0:T(8,128)(2,1)S(1)}, u32[]{:S(2)}, u32[]{:S(2)}) collective-permute-start(bf16[2,64,256]{2,1,0:T(8,128)(2,1)S(1)} %pad_maximum_fusion.refs_0_), channel_id=1, source_target_pairs={{0,24},{4,28},{8,16},{12,20},{16,8},{20,12},{24,0},{28,4},{1,25},{... | collective-permute-start | bytes 196616 | tf_op jit(solution)/shard_map/ppermute | solution.py:420
  24.6 5.1 %copy-start.2 = (f32[64,256]{1,0:T(8,128)S(1)}, f32[64,256]{1,0:T(8,128)}, u32[]{:S(2)}) copy-start(f32[64,256]{1,0:T(8,128)} %constant.14.clone.sin_ref) | copy-start | bytes 196612
  24.6 5.1 %copy-start.3 = (f32[64,256]{1,0:T(8,128)S(1)}, f32[64,256]{1,0:T(8,128)}, u32[]{:S(2)}) copy-start(f32[64,256]{1,0:T(8,128)} %constant.13.clone.cos_ref) | copy-start | bytes 196612
  24.6 5.0 %collective-permute-start.4 = (bf16[2,64,512]{2,1,0:T(8,128)(2,1)S(1)}, bf16[2,64,512]{2,1,0:T(8,128)(2,1)S(1)}, u32[]{:S(2)}, u32[]{:S(2)}) collective-permute-start(bf16[2,64,512]{2,1,0:T(8,128)(2,1)S(1)} %channel_spectra.1.refs_0_), channel_id=1, source_target_pairs={{0,2},{1,3},{2,0},{3,1},{4,6},{5,7},{6,4},{7,5},{8,10},{9,11},{10,... | collective-permute-start | bytes 393224 | tf_op jit(solution)/shard_map/ppermute | solution.py:420
  28.8 1.9 %collective-permute-start.5 = (bf16[2,64,512]{2,1,0:T(8,128)(2,1)S(1)}, bf16[2,64,512]{2,1,0:T(8,128)(2,1)S(1)}, u32[]{:S(2)}, u32[]{:S(2)}) collective-permute-start(bf16[2,64,512]{2,1,0:T(8,128)(2,1)S(1)} %channel_spectra.1.refs_0_), channel_id=1, source_target_pairs={{0,1},{1,0},{2,3},{3,2},{4,5},{5,4},{6,7},{7,6},{8,9},{9,8},{10,11... | collective-permute-start | bytes 393224 | tf_op jit(solution)/shard_map/ppermute | solution.py:420
  29.6 1.3 %collective-permute-start.6 = (bf16[2,64,512]{2,1,0:T(8,128)(2,1)S(1)}, bf16[2,64,512]{2,1,0:T(8,128)(2,1)S(1)}, u32[]{:S(2)}, u32[]{:S(2)}) collective-permute-start(bf16[2,64,512]{2,1,0:T(8,128)(2,1)S(1)} %collective-permute-done.4.refs_1_), channel_id=1, source_target_pairs={{0,1},{1,0},{2,3},{3,2},{4,5},{5,4},{6,7},{7,6},{8,9},{9,8},{10,11... | collective-permute-start | bytes 393224 | tf_op jit(solution)/shard_map/ppermute | solution.py:420

commit v8 on v7

--- a/solution.py
+++ b/solution.py
@@ -232,26 +232,25 @@
     )(*in_hbm(table, sources.reshape(1, count), dead_list), after)
 
 
-def whiten_rows(x_ref, order, ext_ref, table_ref, band_ref, bins_ref):
+def whiten_rows(x_ref, order, group, table_ref, band_ref, bins_ref):
     pieces, rows, _ = x_ref.shape
     x = [x_ref.at[order.index(i)] for i in range(pieces)]
     length = pieces * CHUNK
+    views, chunks = [], []
+    blank = jnp.zeros((rows, EDGE), jnp.bfloat16)
     for i in range(pieces):
-        here = pl.ds(i * rows, rows)
-        ext_ref[here, EDGE : EDGE + CHUNK] = jnp.abs(x[i][...])
-        blank = jnp.zeros((rows, EDGE), jnp.bfloat16)
-        ext_ref[here, :EDGE] = jnp.abs(x[i - 1][:, CHUNK - EDGE :]) if i else blank
-        ext_ref[here, EDGE + CHUNK :] = (
-            jnp.abs(x[i + 1][:, :EDGE]) if i < pieces - 1 else blank
-        )
-    totals = jnp.dot(ext_ref[...], band_ref[...], preferred_element_type=jnp.float32)
-    chunks = []
+        before = jnp.abs(x[i - 1][:, CHUNK - EDGE :]) if i else blank
+        after = jnp.abs(x[i + 1][:, :EDGE]) if i < pieces - 1 else blank
+        views.append(jnp.concatenate([before, jnp.abs(x[i][...]), after], axis=1))
     for i in range(pieces):
+        n = i % group
+        if n == 0:
+            view = jnp.concatenate(views[i : i + group], axis=0)
+            totals = jnp.dot(view, band_ref[...], preferred_element_type=jnp.float32)
         sample = iota((1, CHUNK), 1) + i * CHUNK
         counts = jnp.minimum(sample, HALF) + jnp.minimum(length - 1 - sample, HALF) + 1
-        mean = totals[i * rows : (i + 1) * rows] * (1.0 / counts.astype(jnp.float32))
-        normed = (x[i][...].astype(jnp.float32) / (mean + EPS)).astype(jnp.bfloat16)
-        chunks.append(normed)
+        mean = totals[n * rows : (n + 1) * rows] * (1.0 / counts.astype(jnp.float32))
+        chunks.append((x[i][...].astype(jnp.float32) / (mean + EPS)).astype(jnp.bfloat16))
     spectrum = jnp.dot(
         jnp.concatenate(chunks, axis=1), table_ref[...], preferred_element_type=jnp.float32
     )
@@ -272,9 +271,9 @@
     return real_part * scale, imag_part * scale
 
 
-def channel_kernel(order, x_ref, live_ref, table_ref, band_ref, bins_ref, out_ref, ext_ref):
+def channel_kernel(order, x_ref, live_ref, table_ref, band_ref, bins_ref, out_ref):
     windows, count, _ = out_ref.shape
-    real_part, imag_part = whiten_rows(x_ref, order, ext_ref, table_ref, band_ref, bins_ref)
+    real_part, imag_part = whiten_rows(x_ref, order, 1, table_ref, band_ref, bins_ref)
     for w in range(windows):
         here = slice(w * count, (w + 1) * count)
         out_ref[w, :, :K] = (real_part[here] * live_ref[here, :]).astype(jnp.bfloat16)
@@ -288,7 +287,6 @@
         out_shape=jax.ShapeDtypeStruct((windows, rows // windows, 2 * K), jnp.bfloat16),
         in_specs=[VMEM] * 5,
         out_specs=VMEM,
-        scratch_shapes=[pltpu.VMEM((pieces * rows, CHUNK + 2 * EDGE), jnp.bfloat16)],
         compiler_params=pltpu.CompilerParams(vmem_limit_bytes=LIMIT),
         cost_estimate=pl.CostEstimate(
             flops=1, bytes_accessed=1, transcendentals=0
@@ -299,14 +297,14 @@
 
 def source_kernel(keys, *refs):
     parts = refs[: len(keys)]
-    live_ref, table_ref, band_ref, bins_ref = refs[len(keys) : -3]
-    out_ref, x_ref, ext_ref = refs[-3:]
+    live_ref, table_ref, band_ref, bins_ref = refs[len(keys) : -2]
+    out_ref, x_ref = refs[-2:]
     chan = lax.axis_index("chan")
     for part, slots in zip(parts, keys):
         for n, key in enumerate(slots):
             x_ref[chan ^ key if key is not None else n] = part[n]
     order = tuple(range(x_ref.shape[0]))
-    real_part, imag_part = whiten_rows(x_ref, order, ext_ref, table_ref, band_ref, bins_ref)
+    real_part, imag_part = whiten_rows(x_ref, order, len(order), table_ref, band_ref, bins_ref)
     out_ref[:, :K] = (real_part * live_ref[...]).astype(jnp.bfloat16)
     out_ref[:, K:] = (imag_part * live_ref[...]).astype(jnp.bfloat16)
 
@@ -321,7 +319,6 @@
         out_specs=VMEM,
         scratch_shapes=[
             pltpu.VMEM((pieces, rows, CHUNK), jnp.bfloat16),
-            pltpu.VMEM((pieces * rows, CHUNK + 2 * EDGE), jnp.bfloat16),
         ],
         compiler_params=pltpu.CompilerParams(vmem_limit_bytes=LIMIT),
         cost_estimate=pl.CostEstimate(flops=1 << 34, bytes_accessed=8 << 20, transcendentals=0),

time: 33.5 us -> 33.2 us (level)
  transfers between devices with their start and end apart: 11 -> 11, of which waited for: 7 -> 7; matrix products, arithmetic and copies ran while one was open for 0% -> 0% of each run, Pallas kernels for 14% -> 13%
where the time goes in v8:
time: 33.2 us; the launch traced here: 33 us
  starting transfers between devices  16.1 us (48%)
  Pallas kernels  8.71 us (26%)
  waiting for transfers between devices  7.99 us (24%)
    ppermute x10, starting transfers between devices, swap(): return lax.ppermute(x, axis, [(i, i ^ flip) for i in range(size)])  8.27 us
    ppermute x10, waiting for transfers between devices, swap(): return lax.ppermute(x, axis, [(i, i ^ flip) for i in range(size)])  7.98 us
    all_to_all x1, starting transfers between devices, shards(): lax.all_to_all(blocks, 'chan', 0, 0, axis_index_groups=[list(order)], til...  7.85 us
    pallas_call x1, Pallas kernels, correlate(): pl.pallas_call(functools.partial(correlate_kernel, flips, cw), out_shape=...  2.24 us
    pallas_call x1, Pallas kernels, pack(): pl.pallas_call(functools.partial(pack_kernel, width * reps), out_shape=(j...  2.04 us
    pallas_call x1, Pallas kernels, stage(): pl.pallas_call(functools.partial(stage_kernel, cw, width), out_shape=(jax...  1.65 us
    pallas_call x1, Pallas kernels, channel_spectra(): pl.pallas_call(functools.partial(channel_kernel, order), out_shape=jax.Sh...  1 us
    pallas_call x1, Pallas kernels, lag_kernels(): pl.pallas_call(functools.partial(lag_kernel, windows), out_shape=jax.Shap...  0.99 us
  transfers between devices with their start and end apart: 11, of which 7 were waited for; matrix products, arithmetic and copies ran while one was open for 0% of the time, Pallas kernels for 13%

profile of v8, /device:TPU:0, one launch (start us, length us, event | category | flops | bytes accessed | tf_op | source)
XLA Modules:
  0.0 33.0 jit_solution(1118911573586818035)
XLA Ops:
  0.0 0.0 copy-start.1
  0.0 0.0 copy-start
  0.0 2.0 %pack.1 = (bf16[8,2,1,64,256]{4,3,2,1,0:T(8,128)(2,1)}, bf16[2,32,256]{2,1,0:T(8,128)(2,1)S(1)}, bf16[2,32,256]{2,1,0:T(8,128)(2,1)S(1)}, bf16[2,2,32,256]{3,2,1,0:T(8,128)(2,1)S(1)}) custom-call(bf16[2,8,64,256]{3,2,1,0:T(8,128)(2,1)} %rec_hbm.1, s32[1,128]{1,0:T(1,128)} %bitcast.9), custom_call_target="tpu_custom_call" | custom-call | tf_op jit(solution)/shard_map/pack/pallas_call | solution.py:143
  2.1 7.9 %all-to-all-start = ((bf16[8,128,256]{2,1,0:T(8,128)(2,1)}), bf16[8,128,256]{2,1,0:T(8,128)(2,1)S(1)}, u32[]{:S(2)}, u32[]{:S(2)}) async-start(bf16[8,128,256]{2,1,0:T(8,128)(2,1)} %bitcast.1), calls=%async_computation | async-start | bytes 1048576 | tf_op jit(solution)/shard_map/all_to_all | solution.py:461
  9.9 0.0 collective-permute-start
  9.9 1.6 %collective-permute-start.1 = (bf16[2,32,256]{2,1,0:T(8,128)(2,1)S(1)}, bf16[2,32,256]{2,1,0:T(8,128)(2,1)S(1)}, u32[]{:S(2)}, u32[]{:S(2)}) collective-permute-start(bf16[2,32,256]{2,1,0:T(8,128)(2,1)S(1)} %get-tuple-element.31), channel_id=1, source_target_pairs={{0,2},{1,3},{2,0},{3,1},{4,6},{5,7},{6,4},{7,5},{8,10},{9,11},{10,... | collective-permute-start | bytes 98312 | tf_op jit(solution)/shard_map/ppermute | solution.py:417
  11.5 0.3 collective-permute-start.2
  11.8 0.0 collective-permute-done
  11.8 2.1 %collective-permute-done.1 = bf16[2,32,256]{2,1,0:T(8,128)(2,1)S(1)} collective-permute-done((bf16[2,32,256]{2,1,0:T(8,128)(2,1)S(1)}, bf16[2,32,256]{2,1,0:T(8,128)(2,1)S(1)}, u32[]{:S(2)}, u32[]{:S(2)}) %collective-permute-start.1) | collective-permute-done | bytes 32800 | tf_op jit(solution)/shard_map/ppermute | solution.py:417
  13.9 0.9 %collective-permute-done.2 = bf16[2,32,256]{2,1,0:T(8,128)(2,1)S(1)} collective-permute-done((bf16[2,32,256]{2,1,0:T(8,128)(2,1)S(1)}, bf16[2,32,256]{2,1,0:T(8,128)(2,1)S(1)}, u32[]{:S(2)}, u32[]{:S(2)}) %collective-permute-start.2) | collective-permute-done | bytes 32800 | tf_op jit(solution)/shard_map/ppermute | solution.py:417
  14.8 0.6 %collective-permute-start.3 = (bf16[1,64,256]{2,1,0:T(8,128)(2,1)S(1)}, bf16[1,64,256]{2,1,0:T(8,128)(2,1)S(1)}, u32[]{:S(2)}, u32[]{:S(2)}) collective-permute-start(bf16[1,64,256]{2,1,0:T(8,128)(2,1)S(1)} %bitcast.7), channel_id=1, source_target_pairs={{0,4},{4,0},{8,12},{12,8},{16,20},{20,16},{24,28},{28,24},{1,5},{5... | collective-permute-start | bytes 98312 | tf_op jit(solution)/shard_map/ppermute | solution.py:417
  15.5 1.6 %stage.1 = (bf16[2048,512]{1,0:T(8,128)(2,1)S(1)}, f32[128,1]{1,0:T(8,128)S(1)}, f32[64,1]{1,0:T(8,128)S(1)}, f32[32,256]{1,0:T(8,128)S(1)}) custom-call(bf16[2048,512]{1,0:T(8,128)(2,1)} %constant.10.clone.table_hbm, s32[1,128]{1,0:T(1,128)} %bitcast.10, s32[2,128]{1,0:T(2,128)} %dead_hbm.1, bf16[2,32,256]{2,1,0:T(8,128)(2,1)S(1)} %add_add_fusion.after_hbm), custom_call_target="tpu_custom_call" | custom-call | flops 1 | bytes 4194304 | tf_op jit(solution)/shard_map/stage/pallas_call | solution.py:211
  17.1 1.7 %collective-permute-done.3 = bf16[1,64,256]{2,1,0:T(8,128)(2,1)S(1)} collective-permute-done((bf16[1,64,256]{2,1,0:T(8,128)(2,1)S(1)}, bf16[1,64,256]{2,1,0:T(8,128)(2,1)S(1)}, u32[]{:S(2)}, u32[]{:S(2)}) %collective-permute-start.3) | collective-permute-done | bytes 32800 | tf_op jit(solution)/shard_map/ppermute | solution.py:417
  18.8 0.6 %collective-permute-start.9 = (bf16[2,64,256]{2,1,0:T(8,128)(2,1)S(1)}, bf16[2,64,256]{2,1,0:T(8,128)(2,1)S(1)}, u32[]{:S(2)}, u32[]{:S(2)}) collective-permute-start(bf16[2,64,256]{2,1,0:T(8,128)(2,1)S(1)} %pad_maximum_fusion.refs_0_), channel_id=1, source_target_pairs={{0,8},{4,12},{8,0},{12,4},{16,24},{20,28},{24,16},{28,20},{1,9},{5... | collective-permute-start | bytes 196616 | tf_op jit(solution)/shard_map/ppermute | solution.py:417
  19.5 2.3 %collective-permute-start.8 = (bf16[2,64,256]{2,1,0:T(8,128)(2,1)S(1)}, bf16[2,64,256]{2,1,0:T(8,128)(2,1)S(1)}, u32[]{:S(2)}, u32[]{:S(2)}) collective-permute-start(bf16[2,64,256]{2,1,0:T(8,128)(2,1)S(1)} %pad_maximum_fusion.refs_0_), channel_id=1, source_target_pairs={{0,16},{4,20},{8,24},{12,28},{16,0},{20,4},{24,8},{28,12},{1,17},{... | collective-permute-start | bytes 196616 | tf_op jit(solution)/shard_map/ppermute | solution.py:417
  21.8 1.5 %collective-permute-start.7 = (bf16[2,64,256]{2,1,0:T(8,128)(2,1)S(1)}, bf16[2,64,256]{2,1,0:T(8,128)(2,1)S(1)}, u32[]{:S(2)}, u32[]{:S(2)}) collective-permute-start(bf16[2,64,256]{2,1,0:T(8,128)(2,1)S(1)} %pad_maximum_fusion.refs_0_), channel_id=1, source_target_pairs={{0,24},{4,28},{8,16},{12,20},{16,8},{20,12},{24,0},{28,4},{1,25},{... | collective-permute-start | bytes 196616 | tf_op jit(solution)/shard_map/ppermute | solution.py:417
  23.3 0.0 all-to-all-done.x_ref
  23.3 0.0 copy-done.1
  23.3 0.0 copy-done
  23.3 1.0 %channel_spectra.1.refs_0_ = bf16[2,64,512]{2,1,0:T(8,128)(2,1)S(1)} custom-call(bf16[8,128,256]{2,1,0:T(8,128)(2,1)S(1)} %all-to-all-done.x_ref, f32[128,1]{1,0:T(8,128)S(1)} %get-tuple-element.26.live_ref, bf16[2048,512]{1,0:T(8,128)(2,1)S(1)} %get-tuple-element.27.table_ref.refs_5_, bf16[512,256]{1,0:T(8,128)(2,1)S(1)} %copy-done, ...), custom_call_target="tpu_custom_call" | custom-call | flops 1 | bytes 1 | tf_op jit(solution)/shard_map/channel_spectra/pallas_call | solution.py:285
  24.3 0.0 copy-start.2
  24.3 0.0 copy-start.3
  24.3 1.3 %collective-permute-start.4 = (bf16[2,64,512]{2,1,0:T(8,128)(2,1)S(1)}, bf16[2,64,512]{2,1,0:T(8,128)(2,1)S(1)}, u32[]{:S(2)}, u32[]{:S(2)}) collective-permute-start(bf16[2,64,512]{2,1,0:T(8,128)(2,1)S(1)} %channel_spectra.1.refs_0_), channel_id=1, source_target_pairs={{0,2},{1,3},{2,0},{3,1},{4,6},{5,7},{6,4},{7,5},{8,10},{9,11},{10,... | collective-permute-start | bytes 393224 | tf_op jit(solution)/shard_map/ppermute | solution.py:417
  25.6 0.0 collective-permute-done.9.refs_3_
  25.6 1.4 %collective-permute-done.8.refs_2_ = bf16[2,64,256]{2,1,0:T(8,128)(2,1)S(1)} collective-permute-done((bf16[2,64,256]{2,1,0:T(8,128)(2,1)S(1)}, bf16[2,64,256]{2,1,0:T(8,128)(2,1)S(1)}, u32[]{:S(2)}, u32[]{:S(2)}) %collective-permute-start.8) | collective-permute-done | bytes 65568 | tf_op jit(solution)/shard_map/ppermute | solution.py:417
  27.0 0.9 %collective-permute-done.7.refs_1_ = bf16[2,64,256]{2,1,0:T(8,128)(2,1)S(1)} collective-permute-done((bf16[2,64,256]{2,1,0:T(8,128)(2,1)S(1)}, bf16[2,64,256]{2,1,0:T(8,128)(2,1)S(1)}, u32[]{:S(2)}, u32[]{:S(2)}) %collective-permute-start.7) | collective-permute-done | bytes 65568 | tf_op jit(solution)/shard_map/ppermute | solution.py:417
  28.0 0.8 %source_spectra.1.spec_ref = bf16[64,512]{1,0:T(8,128)(2,1)S(1)} custom-call(bf16[2,64,256]{2,1,0:T(8,128)(2,1)S(1)} %pad_maximum_fusion.refs_0_, bf16[2,64,256]{2,1,0:T(8,128)(2,1)S(1)} %collective-permute-done.7.refs_1_, bf16[2,64,256]{2,1,0:T(8,128)(2,1)S(1)} %collective-permute-done.8.refs_2_, bf16[2,64,256]{2,1,0:T(8,128)(2,1)S(1)} %collective-permute-done.9.refs_3_, ...), custom_call_target="tpu_custom_call" | custom-call | flops 17179869184 | bytes 8388608 | tf_op jit(solution)/shard_map/source_spectra/pallas_call | solution.py:315
  28.8 0.1 collective-permute-start.5
  28.9 0.5 %collective-permute-done.4.refs_1_ = bf16[2,64,512]{2,1,0:T(8,128)(2,1)S(1)} collective-permute-done((bf16[2,64,512]{2,1,0:T(8,128)(2,1)S(1)}, bf16[2,64,512]{2,1,0:T(8,128)(2,1)S(1)}, u32[]{:S(2)}, u32[]{:S(2)}) %collective-permute-start.4) | collective-permute-done | bytes 131104 | tf_op jit(solution)/shard_map/ppermute | solution.py:417
  29.4 0.0 collective-permute-start.6
  29.4 0.0 copy-done.2
  29.4 0.0 copy-done.3
  29.4 1.0 %lag_kernels.1.refs_4_ = bf16[2048,1024]{1,0:T(8,128)(2,1)S(1)} custom-call(bf16[64,512]{1,0:T(8,128)(2,1)S(1)} %source_spectra.1.spec_ref, f32[64,256]{1,0:T(8,128)S(1)} %copy-done.3, f32[64,256]{1,0:T(8,128)S(1)} %copy-done.2), custom_call_target="tpu_custom_call" | custom-call | flops 17179869184 | bytes 8388608 | tf_op jit(solution)/shard_map/lag_kernels/pallas_call | solution.py:350
  30.4 0.0 collective-permute-done.5.refs_2_
  30.4 0.3 %collective-permute-done.6.refs_3_ = bf16[2,64,512]{2,1,0:T(8,128)(2,1)S(1)} collective-permute-done((bf16[2,64,512]{2,1,0:T(8,128)(2,1)S(1)}, bf16[2,64,512]{2,1,0:T(8,128)(2,1)S(1)}, u32[]{:S(2)}, u32[]{:S(2)}) %collective-permute-start.6) | collective-permute-done | bytes 131104 | tf_op jit(solution)/shard_map/ppermute | solution.py:417
  30.7 2.2 %correlate.1 = f32[32,64,256]{2,1,0:T(8,128)} custom-call(bf16[2,64,512]{2,1,0:T(8,128)(2,1)S(1)} %channel_spectra.1.refs_0_, bf16[2,64,512]{2,1,0:T(8,128)(2,1)S(1)} %collective-permute-done.4.refs_1_, bf16[2,64,512]{2,1,0:T(8,128)(2,1)S(1)} %collective-permute-done.5.refs_2_, bf16[2,64,512]{2,1,0:T(8,128)(2,1)S(1)} %collective-permute-done.6.refs_3_, ...), custom_call_target="tpu_custom_call" | custom-call | tf_op jit(solution)/shard_map/correlate/pallas_call | solution.py:400
  (3 shorter events, 0.0 us)
Async XLA Ops:
  0.0 23.3 %copy-start.1 = (bf16[256,256]{1,0:T(8,128)(2,1)S(1)}, bf16[256,256]{1,0:T(8,128)(2,1)}, u32[]{:S(2)}) copy-start(bf16[256,256]{1,0:T(8,128)(2,1)} %constant.12.clone.bins_ref.refs_7_) | copy-start | bytes 393220
  0.0 23.3 %copy-start = (bf16[512,256]{1,0:T(8,128)(2,1)S(1)}, bf16[512,256]{1,0:T(8,128)(2,1)}, u32[]{:S(2)}) copy-start(bf16[512,256]{1,0:T(8,128)(2,1)} %constant.11.clone.band_ref.refs_6_) | copy-start | bytes 786436
  2.1 21.2 %all-to-all-start = ((bf16[8,128,256]{2,1,0:T(8,128)(2,1)}), bf16[8,128,256]{2,1,0:T(8,128)(2,1)S(1)}, u32[]{:S(2)}, u32[]{:S(2)}) async-start(bf16[8,128,256]{2,1,0:T(8,128)(2,1)} %bitcast.1), calls=%async_computation | async-start | bytes 1048576 | tf_op jit(solution)/shard_map/all_to_all | solution.py:461
  9.9 1.9 %collective-permute-start = (bf16[2,32,256]{2,1,0:T(8,128)(2,1)S(1)}, bf16[2,32,256]{2,1,0:T(8,128)(2,1)S(1)}, u32[]{:S(2)}, u32[]{:S(2)}) collective-permute-start(bf16[2,32,256]{2,1,0:T(8,128)(2,1)S(1)} %get-tuple-element.20), channel_id=1, source_target_pairs={{0,1},{1,0},{2,3},{3,2},{4,5},{5,4},{6,7},{7,6},{8,9},{9,8},{10,11... | collective-permute-start | bytes 98312 | tf_op jit(solution)/shard_map/ppermute | solution.py:417
  9.9 4.0 %collective-permute-start.1 = (bf16[2,32,256]{2,1,0:T(8,128)(2,1)S(1)}, bf16[2,32,256]{2,1,0:T(8,128)(2,1)S(1)}, u32[]{:S(2)}, u32[]{:S(2)}) collective-permute-start(bf16[2,32,256]{2,1,0:T(8,128)(2,1)S(1)} %get-tuple-element.31), channel_id=1, source_target_pairs={{0,2},{1,3},{2,0},{3,1},{4,6},{5,7},{6,4},{7,5},{8,10},{9,11},{10,... | collective-permute-start | bytes 98312 | tf_op jit(solution)/shard_map/ppermute | solution.py:417
  11.5 3.4 %collective-permute-start.2 = (bf16[2,32,256]{2,1,0:T(8,128)(2,1)S(1)}, bf16[2,32,256]{2,1,0:T(8,128)(2,1)S(1)}, u32[]{:S(2)}, u32[]{:S(2)}) collective-permute-start(bf16[2,32,256]{2,1,0:T(8,128)(2,1)S(1)} %get-tuple-element.32), channel_id=1, source_target_pairs={{0,3},{1,2},{2,1},{3,0},{4,7},{5,6},{6,5},{7,4},{8,11},{9,10},{10,... | collective-permute-start | bytes 98312 | tf_op jit(solution)/shard_map/ppermute | solution.py:417
  14.8 4.0 %collective-permute-start.3 = (bf16[1,64,256]{2,1,0:T(8,128)(2,1)S(1)}, bf16[1,64,256]{2,1,0:T(8,128)(2,1)S(1)}, u32[]{:S(2)}, u32[]{:S(2)}) collective-permute-start(bf16[1,64,256]{2,1,0:T(8,128)(2,1)S(1)} %bitcast.7), channel_id=1, source_target_pairs={{0,4},{4,0},{8,12},{12,8},{16,20},{20,16},{24,28},{28,24},{1,5},{5... | collective-permute-start | bytes 98312 | tf_op jit(solution)/shard_map/ppermute | solution.py:417
  18.8 6.8 %collective-permute-start.9 = (bf16[2,64,256]{2,1,0:T(8,128)(2,1)S(1)}, bf16[2,64,256]{2,1,0:T(8,128)(2,1)S(1)}, u32[]{:S(2)}, u32[]{:S(2)}) collective-permute-start(bf16[2,64,256]{2,1,0:T(8,128)(2,1)S(1)} %pad_maximum_fusion.refs_0_), channel_id=1, source_target_pairs={{0,8},{4,12},{8,0},{12,4},{16,24},{20,28},{24,16},{28,20},{1,9},{5... | collective-permute-start | bytes 196616 | tf_op jit(solution)/shard_map/ppermute | solution.py:417
  19.5 7.6 %collective-permute-start.8 = (bf16[2,64,256]{2,1,0:T(8,128)(2,1)S(1)}, bf16[2,64,256]{2,1,0:T(8,128)(2,1)S(1)}, u32[]{:S(2)}, u32[]{:S(2)}) collective-permute-start(bf16[2,64,256]{2,1,0:T(8,128)(2,1)S(1)} %pad_maximum_fusion.refs_0_), channel_id=1, source_target_pairs={{0,16},{4,20},{8,24},{12,28},{16,0},{20,4},{24,8},{28,12},{1,17},{... | collective-permute-start | bytes 196616 | tf_op jit(solution)/shard_map/ppermute | solution.py:417
  21.8 6.2 %collective-permute-start.7 = (bf16[2,64,256]{2,1,0:T(8,128)(2,1)S(1)}, bf16[2,64,256]{2,1,0:T(8,128)(2,1)S(1)}, u32[]{:S(2)}, u32[]{:S(2)}) collective-permute-start(bf16[2,64,256]{2,1,0:T(8,128)(2,1)S(1)} %pad_maximum_fusion.refs_0_), channel_id=1, source_target_pairs={{0,24},{4,28},{8,16},{12,20},{16,8},{20,12},{24,0},{28,4},{1,25},{... | collective-permute-start | bytes 196616 | tf_op jit(solution)/shard_map/ppermute | solution.py:417
  24.3 5.1 %copy-start.2 = (f32[64,256]{1,0:T(8,128)S(1)}, f32[64,256]{1,0:T(8,128)}, u32[]{:S(2)}) copy-start(f32[64,256]{1,0:T(8,128)} %constant.14.clone.sin_ref) | copy-start | bytes 196612
  24.3 5.1 %copy-start.3 = (f32[64,256]{1,0:T(8,128)S(1)}, f32[64,256]{1,0:T(8,128)}, u32[]{:S(2)}) copy-start(f32[64,256]{1,0:T(8,128)} %constant.13.clone.cos_ref) | copy-start | bytes 196612
  24.3 5.0 %collective-permute-start.4 = (bf16[2,64,512]{2,1,0:T(8,128)(2,1)S(1)}, bf16[2,64,512]{2,1,0:T(8,128)(2,1)S(1)}, u32[]{:S(2)}, u32[]{:S(2)}) collective-permute-start(bf16[2,64,512]{2,1,0:T(8,128)(2,1)S(1)} %channel_spectra.1.refs_0_), channel_id=1, source_target_pairs={{0,2},{1,3},{2,0},{3,1},{4,6},{5,7},{6,4},{7,5},{8,10},{9,11},{10,... | collective-permute-start | bytes 393224 | tf_op jit(solution)/shard_map/ppermute | solution.py:417
  28.8 1.6 %collective-permute-start.5 = (bf16[2,64,512]{2,1,0:T(8,128)(2,1)S(1)}, bf16[2,64,512]{2,1,0:T(8,128)(2,1)S(1)}, u32[]{:S(2)}, u32[]{:S(2)}) collective-permute-start(bf16[2,64,512]{2,1,0:T(8,128)(2,1)S(1)} %channel_spectra.1.refs_0_), channel_id=1, source_target_pairs={{0,1},{1,0},{2,3},{3,2},{4,5},{5,4},{6,7},{7,6},{8,9},{9,8},{10,11... | collective-permute-start | bytes 393224 | tf_op jit(solution)/shard_map/ppermute | solution.py:417
  29.4 1.3 %collective-permute-start.6 = (bf16[2,64,512]{2,1,0:T(8,128)(2,1)S(1)}, bf16[2,64,512]{2,1,0:T(8,128)(2,1)S(1)}, u32[]{:S(2)}, u32[]{:S(2)}) collective-permute-start(bf16[2,64,512]{2,1,0:T(8,128)(2,1)S(1)} %collective-permute-done.4.refs_1_), channel_id=1, source_target_pairs={{0,1},{1,0},{2,3},{3,2},{4,5},{5,4},{6,7},{7,6},{8,9},{9,8},{10,11... | collective-permute-start | bytes 393224 | tf_op jit(solution)/shard_map/ppermute | solution.py:417

commit v9 on v8

--- a/solution.py
+++ b/solution.py
@@ -273,7 +273,7 @@
 
 def channel_kernel(order, x_ref, live_ref, table_ref, band_ref, bins_ref, out_ref):
     windows, count, _ = out_ref.shape
-    real_part, imag_part = whiten_rows(x_ref, order, 1, table_ref, band_ref, bins_ref)
+    real_part, imag_part = whiten_rows(x_ref, order, 2, table_ref, band_ref, bins_ref)
     for w in range(windows):
         here = slice(w * count, (w + 1) * count)
         out_ref[w, :, :K] = (real_part[here] * live_ref[here, :]).astype(jnp.bfloat16)

time: 33.2 us -> 33.2 us (level)
  no operation moved by 1% of the time
where the time goes in v9:
time: 33.2 us; the launch traced here: 33 us
  starting transfers between devices  16.1 us (48%)
  Pallas kernels  8.7 us (26%)
  waiting for transfers between devices  7.98 us (24%)
    ppermute x10, starting transfers between devices, swap(): return lax.ppermute(x, axis, [(i, i ^ flip) for i in range(size)])  8.28 us
    ppermute x10, waiting for transfers between devices, swap(): return lax.ppermute(x, axis, [(i, i ^ flip) for i in range(size)])  7.98 us
    all_to_all x1, starting transfers between devices, shards(): lax.all_to_all(blocks, 'chan', 0, 0, axis_index_groups=[list(order)], til...  7.85 us
    pallas_call x1, Pallas kernels, correlate(): pl.pallas_call(functools.partial(correlate_kernel, flips, cw), out_shape=...  2.25 us
    pallas_call x1, Pallas kernels, pack(): pl.pallas_call(functools.partial(pack_kernel, width * reps), out_shape=(j...  2.04 us
    pallas_call x1, Pallas kernels, stage(): pl.pallas_call(functools.partial(stage_kernel, cw, width), out_shape=(jax...  1.65 us
    pallas_call x1, Pallas kernels, lag_kernels(): pl.pallas_call(functools.partial(lag_kernel, windows), out_shape=jax.Shap...  0.99 us
    pallas_call x1, Pallas kernels, channel_spectra(): pl.pallas_call(functools.partial(channel_kernel, order), out_shape=jax.Sh...  0.99 us
  transfers between devices with their start and end apart: 11, of which 7 were waited for; matrix products, arithmetic and copies ran while one was open for 0% of the time, Pallas kernels for 13%

profile of v9, /device:TPU:0, one launch (start us, length us, event | category | flops | bytes accessed | tf_op | source)
XLA Modules:
  0.0 33.0 jit_solution(4923192812286027857)
XLA Ops:
  0.0 0.0 copy-start.1
  0.0 0.0 copy-start
  0.0 2.0 %pack.1 = (bf16[8,2,1,64,256]{4,3,2,1,0:T(8,128)(2,1)}, bf16[2,32,256]{2,1,0:T(8,128)(2,1)S(1)}, bf16[2,32,256]{2,1,0:T(8,128)(2,1)S(1)}, bf16[2,2,32,256]{3,2,1,0:T(8,128)(2,1)S(1)}) custom-call(bf16[2,8,64,256]{3,2,1,0:T(8,128)(2,1)} %rec_hbm.1, s32[1,128]{1,0:T(1,128)} %bitcast.9), custom_call_target="tpu_custom_call" | custom-call | tf_op jit(solution)/shard_map/pack/pallas_call | solution.py:143
  2.1 7.9 %all-to-all-start = ((bf16[8,128,256]{2,1,0:T(8,128)(2,1)}), bf16[8,128,256]{2,1,0:T(8,128)(2,1)S(1)}, u32[]{:S(2)}, u32[]{:S(2)}) async-start(bf16[8,128,256]{2,1,0:T(8,128)(2,1)} %bitcast.1), calls=%async_computation | async-start | bytes 1048576 | tf_op jit(solution)/shard_map/all_to_all | solution.py:461
  9.9 0.0 collective-permute-start
  9.9 1.6 %collective-permute-start.1 = (bf16[2,32,256]{2,1,0:T(8,128)(2,1)S(1)}, bf16[2,32,256]{2,1,0:T(8,128)(2,1)S(1)}, u32[]{:S(2)}, u32[]{:S(2)}) collective-permute-start(bf16[2,32,256]{2,1,0:T(8,128)(2,1)S(1)} %get-tuple-element.31), channel_id=1, source_target_pairs={{0,2},{1,3},{2,0},{3,1},{4,6},{5,7},{6,4},{7,5},{8,10},{9,11},{10,... | collective-permute-start | bytes 98312 | tf_op jit(solution)/shard_map/ppermute | solution.py:417
  11.5 0.3 collective-permute-start.2
  11.8 0.0 collective-permute-done
  11.8 2.1 %collective-permute-done.1 = bf16[2,32,256]{2,1,0:T(8,128)(2,1)S(1)} collective-permute-done((bf16[2,32,256]{2,1,0:T(8,128)(2,1)S(1)}, bf16[2,32,256]{2,1,0:T(8,128)(2,1)S(1)}, u32[]{:S(2)}, u32[]{:S(2)}) %collective-permute-start.1) | collective-permute-done | bytes 32800 | tf_op jit(solution)/shard_map/ppermute | solution.py:417
  13.9 0.9 %collective-permute-done.2 = bf16[2,32,256]{2,1,0:T(8,128)(2,1)S(1)} collective-permute-done((bf16[2,32,256]{2,1,0:T(8,128)(2,1)S(1)}, bf16[2,32,256]{2,1,0:T(8,128)(2,1)S(1)}, u32[]{:S(2)}, u32[]{:S(2)}) %collective-permute-start.2) | collective-permute-done | bytes 32800 | tf_op jit(solution)/shard_map/ppermute | solution.py:417
  14.8 0.6 %collective-permute-start.3 = (bf16[1,64,256]{2,1,0:T(8,128)(2,1)S(1)}, bf16[1,64,256]{2,1,0:T(8,128)(2,1)S(1)}, u32[]{:S(2)}, u32[]{:S(2)}) collective-permute-start(bf16[1,64,256]{2,1,0:T(8,128)(2,1)S(1)} %bitcast.7), channel_id=1, source_target_pairs={{0,4},{4,0},{8,12},{12,8},{16,20},{20,16},{24,28},{28,24},{1,5},{5... | collective-permute-start | bytes 98312 | tf_op jit(solution)/shard_map/ppermute | solution.py:417
  15.5 1.6 %stage.1 = (bf16[2048,512]{1,0:T(8,128)(2,1)S(1)}, f32[128,1]{1,0:T(8,128)S(1)}, f32[64,1]{1,0:T(8,128)S(1)}, f32[32,256]{1,0:T(8,128)S(1)}) custom-call(bf16[2048,512]{1,0:T(8,128)(2,1)} %constant.10.clone.table_hbm, s32[1,128]{1,0:T(1,128)} %bitcast.10, s32[2,128]{1,0:T(2,128)} %dead_hbm.1, bf16[2,32,256]{2,1,0:T(8,128)(2,1)S(1)} %add_add_fusion.after_hbm), custom_call_target="tpu_custom_call" | custom-call | flops 1 | bytes 4194304 | tf_op jit(solution)/shard_map/stage/pallas_call | solution.py:211
  17.1 1.7 %collective-permute-done.3 = bf16[1,64,256]{2,1,0:T(8,128)(2,1)S(1)} collective-permute-done((bf16[1,64,256]{2,1,0:T(8,128)(2,1)S(1)}, bf16[1,64,256]{2,1,0:T(8,128)(2,1)S(1)}, u32[]{:S(2)}, u32[]{:S(2)}) %collective-permute-start.3) | collective-permute-done | bytes 32800 | tf_op jit(solution)/shard_map/ppermute | solution.py:417
  18.8 0.6 %collective-permute-start.9 = (bf16[2,64,256]{2,1,0:T(8,128)(2,1)S(1)}, bf16[2,64,256]{2,1,0:T(8,128)(2,1)S(1)}, u32[]{:S(2)}, u32[]{:S(2)}) collective-permute-start(bf16[2,64,256]{2,1,0:T(8,128)(2,1)S(1)} %pad_maximum_fusion.refs_0_), channel_id=1, source_target_pairs={{0,8},{4,12},{8,0},{12,4},{16,24},{20,28},{24,16},{28,20},{1,9},{5... | collective-permute-start | bytes 196616 | tf_op jit(solution)/shard_map/ppermute | solution.py:417
  19.5 2.3 %collective-permute-start.8 = (bf16[2,64,256]{2,1,0:T(8,128)(2,1)S(1)}, bf16[2,64,256]{2,1,0:T(8,128)(2,1)S(1)}, u32[]{:S(2)}, u32[]{:S(2)}) collective-permute-start(bf16[2,64,256]{2,1,0:T(8,128)(2,1)S(1)} %pad_maximum_fusion.refs_0_), channel_id=1, source_target_pairs={{0,16},{4,20},{8,24},{12,28},{16,0},{20,4},{24,8},{28,12},{1,17},{... | collective-permute-start | bytes 196616 | tf_op jit(solution)/shard_map/ppermute | solution.py:417
  21.8 1.5 %collective-permute-start.7 = (bf16[2,64,256]{2,1,0:T(8,128)(2,1)S(1)}, bf16[2,64,256]{2,1,0:T(8,128)(2,1)S(1)}, u32[]{:S(2)}, u32[]{:S(2)}) collective-permute-start(bf16[2,64,256]{2,1,0:T(8,128)(2,1)S(1)} %pad_maximum_fusion.refs_0_), channel_id=1, source_target_pairs={{0,24},{4,28},{8,16},{12,20},{16,8},{20,12},{24,0},{28,4},{1,25},{... | collective-permute-start | bytes 196616 | tf_op jit(solution)/shard_map/ppermute | solution.py:417
  23.3 0.0 all-to-all-done.x_ref
  23.3 0.0 copy-done.1
  23.3 0.0 copy-done
  23.3 1.0 %channel_spectra.1.refs_0_ = bf16[2,64,512]{2,1,0:T(8,128)(2,1)S(1)} custom-call(bf16[8,128,256]{2,1,0:T(8,128)(2,1)S(1)} %all-to-all-done.x_ref, f32[128,1]{1,0:T(8,128)S(1)} %get-tuple-element.26.live_ref, bf16[2048,512]{1,0:T(8,128)(2,1)S(1)} %get-tuple-element.27.table_ref.refs_5_, bf16[512,256]{1,0:T(8,128)(2,1)S(1)} %copy-done, ...), custom_call_target="tpu_custom_call" | custom-call | flops 1 | bytes 1 | tf_op jit(solution)/shard_map/channel_spectra/pallas_call | solution.py:285
  24.3 0.0 copy-start.2
  24.3 0.0 copy-start.3
  24.3 1.3 %collective-permute-start.4 = (bf16[2,64,512]{2,1,0:T(8,128)(2,1)S(1)}, bf16[2,64,512]{2,1,0:T(8,128)(2,1)S(1)}, u32[]{:S(2)}, u32[]{:S(2)}) collective-permute-start(bf16[2,64,512]{2,1,0:T(8,128)(2,1)S(1)} %channel_spectra.1.refs_0_), channel_id=1, source_target_pairs={{0,2},{1,3},{2,0},{3,1},{4,6},{5,7},{6,4},{7,5},{8,10},{9,11},{10,... | collective-permute-start | bytes 393224 | tf_op jit(solution)/shard_map/ppermute | solution.py:417
  25.6 0.0 collective-permute-done.9.refs_3_
  25.6 1.4 %collective-permute-done.8.refs_2_ = bf16[2,64,256]{2,1,0:T(8,128)(2,1)S(1)} collective-permute-done((bf16[2,64,256]{2,1,0:T(8,128)(2,1)S(1)}, bf16[2,64,256]{2,1,0:T(8,128)(2,1)S(1)}, u32[]{:S(2)}, u32[]{:S(2)}) %collective-permute-start.8) | collective-permute-done | bytes 65568 | tf_op jit(solution)/shard_map/ppermute | solution.py:417
  27.0 0.9 %collective-permute-done.7.refs_1_ = bf16[2,64,256]{2,1,0:T(8,128)(2,1)S(1)} collective-permute-done((bf16[2,64,256]{2,1,0:T(8,128)(2,1)S(1)}, bf16[2,64,256]{2,1,0:T(8,128)(2,1)S(1)}, u32[]{:S(2)}, u32[]{:S(2)}) %collective-permute-start.7) | collective-permute-done | bytes 65568 | tf_op jit(solution)/shard_map/ppermute | solution.py:417
  28.0 0.8 %source_spectra.1.spec_ref = bf16[64,512]{1,0:T(8,128)(2,1)S(1)} custom-call(bf16[2,64,256]{2,1,0:T(8,128)(2,1)S(1)} %pad_maximum_fusion.refs_0_, bf16[2,64,256]{2,1,0:T(8,128)(2,1)S(1)} %collective-permute-done.7.refs_1_, bf16[2,64,256]{2,1,0:T(8,128)(2,1)S(1)} %collective-permute-done.8.refs_2_, bf16[2,64,256]{2,1,0:T(8,128)(2,1)S(1)} %collective-permute-done.9.refs_3_, ...), custom_call_target="tpu_custom_call" | custom-call | flops 17179869184 | bytes 8388608 | tf_op jit(solution)/shard_map/source_spectra/pallas_call | solution.py:315
  28.8 0.1 collective-permute-start.5
  28.9 0.5 %collective-permute-done.4.refs_1_ = bf16[2,64,512]{2,1,0:T(8,128)(2,1)S(1)} collective-permute-done((bf16[2,64,512]{2,1,0:T(8,128)(2,1)S(1)}, bf16[2,64,512]{2,1,0:T(8,128)(2,1)S(1)}, u32[]{:S(2)}, u32[]{:S(2)}) %collective-permute-start.4) | collective-permute-done | bytes 131104 | tf_op jit(solution)/shard_map/ppermute | solution.py:417
  29.4 0.0 collective-permute-start.6
  29.4 0.0 copy-done.2
  29.4 0.0 copy-done.3
  29.4 1.0 %lag_kernels.1.refs_4_ = bf16[2048,1024]{1,0:T(8,128)(2,1)S(1)} custom-call(bf16[64,512]{1,0:T(8,128)(2,1)S(1)} %source_spectra.1.spec_ref, f32[64,256]{1,0:T(8,128)S(1)} %copy-done.3, f32[64,256]{1,0:T(8,128)S(1)} %copy-done.2), custom_call_target="tpu_custom_call" | custom-call | flops 17179869184 | bytes 8388608 | tf_op jit(solution)/shard_map/lag_kernels/pallas_call | solution.py:350
  30.4 0.0 collective-permute-done.5.refs_2_
  30.4 0.3 %collective-permute-done.6.refs_3_ = bf16[2,64,512]{2,1,0:T(8,128)(2,1)S(1)} collective-permute-done((bf16[2,64,512]{2,1,0:T(8,128)(2,1)S(1)}, bf16[2,64,512]{2,1,0:T(8,128)(2,1)S(1)}, u32[]{:S(2)}, u32[]{:S(2)}) %collective-permute-start.6) | collective-permute-done | bytes 131104 | tf_op jit(solution)/shard_map/ppermute | solution.py:417
  30.7 2.2 %correlate.1 = f32[32,64,256]{2,1,0:T(8,128)} custom-call(bf16[2,64,512]{2,1,0:T(8,128)(2,1)S(1)} %channel_spectra.1.refs_0_, bf16[2,64,512]{2,1,0:T(8,128)(2,1)S(1)} %collective-permute-done.4.refs_1_, bf16[2,64,512]{2,1,0:T(8,128)(2,1)S(1)} %collective-permute-done.5.refs_2_, bf16[2,64,512]{2,1,0:T(8,128)(2,1)S(1)} %collective-permute-done.6.refs_3_, ...), custom_call_target="tpu_custom_call" | custom-call | tf_op jit(solution)/shard_map/correlate/pallas_call | solution.py:400
  (3 shorter events, 0.0 us)
Async XLA Ops:
  0.0 23.3 %copy-start.1 = (bf16[256,256]{1,0:T(8,128)(2,1)S(1)}, bf16[256,256]{1,0:T(8,128)(2,1)}, u32[]{:S(2)}) copy-start(bf16[256,256]{1,0:T(8,128)(2,1)} %constant.12.clone.bins_ref.refs_7_) | copy-start | bytes 393220
  0.0 23.3 %copy-start = (bf16[512,256]{1,0:T(8,128)(2,1)S(1)}, bf16[512,256]{1,0:T(8,128)(2,1)}, u32[]{:S(2)}) copy-start(bf16[512,256]{1,0:T(8,128)(2,1)} %constant.11.clone.band_ref.refs_6_) | copy-start | bytes 786436
  2.1 21.2 %all-to-all-start = ((bf16[8,128,256]{2,1,0:T(8,128)(2,1)}), bf16[8,128,256]{2,1,0:T(8,128)(2,1)S(1)}, u32[]{:S(2)}, u32[]{:S(2)}) async-start(bf16[8,128,256]{2,1,0:T(8,128)(2,1)} %bitcast.1), calls=%async_computation | async-start | bytes 1048576 | tf_op jit(solution)/shard_map/all_to_all | solution.py:461
  9.9 1.9 %collective-permute-start = (bf16[2,32,256]{2,1,0:T(8,128)(2,1)S(1)}, bf16[2,32,256]{2,1,0:T(8,128)(2,1)S(1)}, u32[]{:S(2)}, u32[]{:S(2)}) collective-permute-start(bf16[2,32,256]{2,1,0:T(8,128)(2,1)S(1)} %get-tuple-element.20), channel_id=1, source_target_pairs={{0,1},{1,0},{2,3},{3,2},{4,5},{5,4},{6,7},{7,6},{8,9},{9,8},{10,11... | collective-permute-start | bytes 98312 | tf_op jit(solution)/shard_map/ppermute | solution.py:417
  9.9 4.0 %collective-permute-start.1 = (bf16[2,32,256]{2,1,0:T(8,128)(2,1)S(1)}, bf16[2,32,256]{2,1,0:T(8,128)(2,1)S(1)}, u32[]{:S(2)}, u32[]{:S(2)}) collective-permute-start(bf16[2,32,256]{2,1,0:T(8,128)(2,1)S(1)} %get-tuple-element.31), channel_id=1, source_target_pairs={{0,2},{1,3},{2,0},{3,1},{4,6},{5,7},{6,4},{7,5},{8,10},{9,11},{10,... | collective-permute-start | bytes 98312 | tf_op jit(solution)/shard_map/ppermute | solution.py:417
  11.5 3.4 %collective-permute-start.2 = (bf16[2,32,256]{2,1,0:T(8,128)(2,1)S(1)}, bf16[2,32,256]{2,1,0:T(8,128)(2,1)S(1)}, u32[]{:S(2)}, u32[]{:S(2)}) collective-permute-start(bf16[2,32,256]{2,1,0:T(8,128)(2,1)S(1)} %get-tuple-element.32), channel_id=1, source_target_pairs={{0,3},{1,2},{2,1},{3,0},{4,7},{5,6},{6,5},{7,4},{8,11},{9,10},{10,... | collective-permute-start | bytes 98312 | tf_op jit(solution)/shard_map/ppermute | solution.py:417
  14.8 4.0 %collective-permute-start.3 = (bf16[1,64,256]{2,1,0:T(8,128)(2,1)S(1)}, bf16[1,64,256]{2,1,0:T(8,128)(2,1)S(1)}, u32[]{:S(2)}, u32[]{:S(2)}) collective-permute-start(bf16[1,64,256]{2,1,0:T(8,128)(2,1)S(1)} %bitcast.7), channel_id=1, source_target_pairs={{0,4},{4,0},{8,12},{12,8},{16,20},{20,16},{24,28},{28,24},{1,5},{5... | collective-permute-start | bytes 98312 | tf_op jit(solution)/shard_map/ppermute | solution.py:417
  18.8 6.8 %collective-permute-start.9 = (bf16[2,64,256]{2,1,0:T(8,128)(2,1)S(1)}, bf16[2,64,256]{2,1,0:T(8,128)(2,1)S(1)}, u32[]{:S(2)}, u32[]{:S(2)}) collective-permute-start(bf16[2,64,256]{2,1,0:T(8,128)(2,1)S(1)} %pad_maximum_fusion.refs_0_), channel_id=1, source_target_pairs={{0,8},{4,12},{8,0},{12,4},{16,24},{20,28},{24,16},{28,20},{1,9},{5... | collective-permute-start | bytes 196616 | tf_op jit(solution)/shard_map/ppermute | solution.py:417
  19.5 7.6 %collective-permute-start.8 = (bf16[2,64,256]{2,1,0:T(8,128)(2,1)S(1)}, bf16[2,64,256]{2,1,0:T(8,128)(2,1)S(1)}, u32[]{:S(2)}, u32[]{:S(2)}) collective-permute-start(bf16[2,64,256]{2,1,0:T(8,128)(2,1)S(1)} %pad_maximum_fusion.refs_0_), channel_id=1, source_target_pairs={{0,16},{4,20},{8,24},{12,28},{16,0},{20,4},{24,8},{28,12},{1,17},{... | collective-permute-start | bytes 196616 | tf_op jit(solution)/shard_map/ppermute | solution.py:417
  21.8 6.2 %collective-permute-start.7 = (bf16[2,64,256]{2,1,0:T(8,128)(2,1)S(1)}, bf16[2,64,256]{2,1,0:T(8,128)(2,1)S(1)}, u32[]{:S(2)}, u32[]{:S(2)}) collective-permute-start(bf16[2,64,256]{2,1,0:T(8,128)(2,1)S(1)} %pad_maximum_fusion.refs_0_), channel_id=1, source_target_pairs={{0,24},{4,28},{8,16},{12,20},{16,8},{20,12},{24,0},{28,4},{1,25},{... | collective-permute-start | bytes 196616 | tf_op jit(solution)/shard_map/ppermute | solution.py:417
  24.3 5.1 %copy-start.2 = (f32[64,256]{1,0:T(8,128)S(1)}, f32[64,256]{1,0:T(8,128)}, u32[]{:S(2)}) copy-start(f32[64,256]{1,0:T(8,128)} %constant.14.clone.sin_ref) | copy-start | bytes 196612
  24.3 5.1 %copy-start.3 = (f32[64,256]{1,0:T(8,128)S(1)}, f32[64,256]{1,0:T(8,128)}, u32[]{:S(2)}) copy-start(f32[64,256]{1,0:T(8,128)} %constant.13.clone.cos_ref) | copy-start | bytes 196612
  24.3 5.0 %collective-permute-start.4 = (bf16[2,64,512]{2,1,0:T(8,128)(2,1)S(1)}, bf16[2,64,512]{2,1,0:T(8,128)(2,1)S(1)}, u32[]{:S(2)}, u32[]{:S(2)}) collective-permute-start(bf16[2,64,512]{2,1,0:T(8,128)(2,1)S(1)} %channel_spectra.1.refs_0_), channel_id=1, source_target_pairs={{0,2},{1,3},{2,0},{3,1},{4,6},{5,7},{6,4},{7,5},{8,10},{9,11},{10,... | collective-permute-start | bytes 393224 | tf_op jit(solution)/shard_map/ppermute | solution.py:417
  28.8 1.6 %collective-permute-start.5 = (bf16[2,64,512]{2,1,0:T(8,128)(2,1)S(1)}, bf16[2,64,512]{2,1,0:T(8,128)(2,1)S(1)}, u32[]{:S(2)}, u32[]{:S(2)}) collective-permute-start(bf16[2,64,512]{2,1,0:T(8,128)(2,1)S(1)} %channel_spectra.1.refs_0_), channel_id=1, source_target_pairs={{0,1},{1,0},{2,3},{3,2},{4,5},{5,4},{6,7},{7,6},{8,9},{9,8},{10,11... | collective-permute-start | bytes 393224 | tf_op jit(solution)/shard_map/ppermute | solution.py:417
  29.4 1.3 %collective-permute-start.6 = (bf16[2,64,512]{2,1,0:T(8,128)(2,1)S(1)}, bf16[2,64,512]{2,1,0:T(8,128)(2,1)S(1)}, u32[]{:S(2)}, u32[]{:S(2)}) collective-permute-start(bf16[2,64,512]{2,1,0:T(8,128)(2,1)S(1)} %collective-permute-done.4.refs_1_), channel_id=1, source_target_pairs={{0,1},{1,0},{2,3},{3,2},{4,5},{5,4},{6,7},{7,6},{8,9},{9,8},{10,11... | collective-permute-start | bytes 393224 | tf_op jit(solution)/shard_map/ppermute | solution.py:417
